TPU v7x, 32 devices: a whole 2x2x4 slice. The times are simulated.
32 devices in a mesh: section: 2 (over y), ctx: 4 (over z), dp: 4 (over x, core).
Axes of the slice: x: 2, y: 2, z: 4, core: 2. Of those that a mesh axis runs over, the one named last changes fastest.
Arguments:
- activations: bfloat16 [2, 4, 512, 1280], P('section', 'dp', 'ctx'), may hold values from -6 to 6
- out_grads: bfloat16 [2, 4, 512, 1280], P('section', 'dp', 'ctx'), may hold values from -6 to 6
- doc_ids: int32 [4, 4], replicated, may hold values from 0 to 1, never falling along the last dimension, each value on 1 to 3 neighbouring positions
- query_weight: bfloat16 [2, 1280, 640], P('section', None, 'dp'), may hold values from -0.195655948 to 0.195655948
- key_weight: bfloat16 [2, 1280, 640], P('section', None, 'dp'), may hold values from -3.0745935 to 3.0745935
- value_weight: bfloat16 [2, 1280, 640], P('section', None, 'dp'), may hold values from -0.15625 to 0.15625
- out_weight: bfloat16 [2, 640, 1280], P('section', 'dp'), may hold values from -0.25 to 0.25
Outputs:
- received_grad: bfloat16 [2, 4, 512, 1280], P('section', 'dp', 'ctx')
Inputs may be any that keep to these rules, and one draw needn't show every extreme that they name: `doc_ids`: each page stack's documents are runs of whole blocks, numbered from 0 in order; a document covers at most 3 blocks.
All inputs are finite; a program needn't handle non-finite values.
Results may differ from a plain program's by a relative error of at most 0.0085.
The roundings to bfloat16 on the way count: a program that leaves them out, or rounds other values in their place, can miss the bound.
Values may be sent and summed in bfloat16 or wider, within the bound.
No kernel may reach another device: no remote copies, remote signals or barrier semaphores. Data moves between devices by JAX's collectives and lax.ppermute only.
A program may use at most 128 MiB of HBM per device.

v0:
```python
import math

import jax
import jax.numpy as jnp
from jax import lax
from jax.sharding import PartitionSpec as P

HEAD_DIM = 80
BLOCK = 128


NEG = -1e30
HIGHEST = lax.Precision.HIGHEST


def from_behind(array, axis, by):
    length = lax.axis_size(axis)
    return lax.ppermute(array, axis, [(i, (i + by) % length) for i in range(length)])


def expand(allowed_blocks, query_len, key_len):
    page_count = allowed_blocks.shape[0]
    query_blocks = query_len // BLOCK
    key_blocks = key_len // BLOCK
    widened = jnp.broadcast_to(
        allowed_blocks[:, :, None, :, None], (page_count, query_blocks, BLOCK, key_blocks, BLOCK)
    )
    return widened.reshape(page_count, query_len, key_len)


def row_statistics(
    queries, out_grad, all_keys, all_values, block_table, my_offset, head_count, score_scale
):
    page_count, row_count, _ = queries.shape
    length = all_keys.shape[1]
    block_len = math.gcd(length, 512)
    query_four = queries.reshape(page_count, row_count, head_count, HEAD_DIM)
    grad_four = out_grad.reshape(page_count, row_count, head_count, HEAD_DIM)
    my_blocks = lax.dynamic_slice_in_dim(block_table, my_offset // BLOCK, row_count // BLOCK, 1)

    def row_visit(index, totals):
        key_offset = index * block_len
        key_block = lax.dynamic_slice_in_dim(all_keys, key_offset, block_len, 1).reshape(
            page_count, block_len, head_count, HEAD_DIM
        )
        value_block = lax.dynamic_slice_in_dim(all_values, key_offset, block_len, 1).reshape(
            page_count, block_len, head_count, HEAD_DIM
        )
        allowed = expand(
            lax.dynamic_slice_in_dim(my_blocks, key_offset // BLOCK, block_len // BLOCK, 2),
            row_count,
            block_len,
        )[:, None]
        old_max, old_sum, old_dot = totals
        scores = (
            jnp.einsum(
                "brhd,bkhd->bhrk",
                query_four,
                key_block,
                precision=HIGHEST,
                preferred_element_type=jnp.float32,
            )
            * score_scale
        )
        scores = jnp.where(allowed, scores, NEG)
        new_max = jnp.maximum(old_max, jnp.max(scores, axis=-1))
        weights = jnp.where(allowed, jnp.exp(scores - new_max[..., None]), 0.0)
        dprob = jnp.einsum(
            "brhd,bkhd->bhrk", grad_four, value_block, preferred_element_type=jnp.float32
        )
        factor = jnp.exp(old_max - new_max)
        return (
            new_max,
            old_sum * factor + jnp.sum(weights, axis=-1),
            old_dot * factor + jnp.sum(weights * dprob, axis=-1),
        )

    stat_shape = (page_count, head_count, row_count)
    zeros = jnp.zeros(stat_shape, jnp.float32)
    start_state = (jnp.full(stat_shape, NEG, jnp.float32), zeros, zeros)
    final_max, final_sum, final_dot = lax.fori_loop(0, length // block_len, row_visit, start_state)
    log_total = final_max + jnp.log(final_sum)
    row_delta = final_dot / final_sum
    return (jnp.transpose(log_total, (0, 2, 1)), jnp.transpose(row_delta, (0, 2, 1)))


def query_side(
    queries,
    out_grad,
    all_keys,
    all_values,
    block_table,
    my_offset,
    log_total,
    row_delta,
    head_count,
    score_scale,
):
    page_count, row_count, width = queries.shape
    length = all_keys.shape[1]
    block_len = math.gcd(length, 512)
    query_four = queries.reshape(page_count, row_count, head_count, HEAD_DIM)
    grad_four = out_grad.reshape(page_count, row_count, head_count, HEAD_DIM)
    log_heads = jnp.transpose(log_total, (0, 2, 1))
    delta_heads = jnp.transpose(row_delta, (0, 2, 1))
    my_blocks = lax.dynamic_slice_in_dim(block_table, my_offset // BLOCK, row_count // BLOCK, 1)

    def query_visit(index, totals):
        key_offset = index * block_len
        key_block = lax.dynamic_slice_in_dim(all_keys, key_offset, block_len, 1).reshape(
            page_count, block_len, head_count, HEAD_DIM
        )
        value_block = lax.dynamic_slice_in_dim(all_values, key_offset, block_len, 1).reshape(
            page_count, block_len, head_count, HEAD_DIM
        )
        allowed = expand(
            lax.dynamic_slice_in_dim(my_blocks, key_offset // BLOCK, block_len // BLOCK, 2),
            row_count,
            block_len,
        )[:, None]
        scores = (
            jnp.einsum(
                "brhd,bkhd->bhrk",
                query_four,
                key_block,
                precision=HIGHEST,
                preferred_element_type=jnp.float32,
            )
            * score_scale
        )
        scores = jnp.where(allowed, scores, NEG)
        prob = jnp.where(allowed, jnp.exp(scores - log_heads[..., None]), 0.0)
        dprob = jnp.einsum(
            "brhd,bkhd->bhrk", grad_four, value_block, preferred_element_type=jnp.float32
        )
        dscore = prob * (dprob - delta_heads[..., None])
        dscore_low = dscore.astype(jnp.bfloat16).astype(jnp.float32)
        return totals + jnp.einsum(
            "bhrk,bkhd->brhd",
            dscore_low,
            key_block,
            precision=HIGHEST,
            preferred_element_type=jnp.float32,
        )

    start_state = jnp.zeros((page_count, row_count, head_count, HEAD_DIM), jnp.float32)
    summed = lax.fori_loop(0, length // block_len, query_visit, start_state)
    return (summed * score_scale).astype(jnp.bfloat16).reshape(page_count, row_count, width)


def key_side(
    totals,
    portion,
    key_rows,
    value_rows,
    all_log_total,
    all_delta,
    block_table,
    my_offset,
    head_count,
    score_scale,
):
    part_queries, part_grads = portion
    page_count, part_len, _ = part_queries.shape
    row_count = key_rows.shape[1]
    block_len = math.gcd(part_len, 512)
    key_four = key_rows.reshape(page_count, row_count, head_count, HEAD_DIM)
    value_four = value_rows.reshape(page_count, row_count, head_count, HEAD_DIM)
    key_columns = lax.dynamic_slice_in_dim(block_table, my_offset // BLOCK, row_count // BLOCK, 2)

    def key_visit(index, state):
        query_offset = index * block_len
        query_part = lax.dynamic_slice_in_dim(part_queries, query_offset, block_len, 1).reshape(
            page_count, block_len, head_count, HEAD_DIM
        )
        grad_part = (
            lax.dynamic_slice_in_dim(part_grads, query_offset, block_len, 1)
            .astype(jnp.bfloat16)
            .reshape(page_count, block_len, head_count, HEAD_DIM)
        )
        log_part = jnp.transpose(
            lax.dynamic_slice_in_dim(all_log_total, query_offset, block_len, 1), (0, 2, 1)
        )
        delta_part = jnp.transpose(
            lax.dynamic_slice_in_dim(all_delta, query_offset, block_len, 1), (0, 2, 1)
        )
        allowed = expand(
            lax.dynamic_slice_in_dim(key_columns, query_offset // BLOCK, block_len // BLOCK, 1),
            block_len,
            row_count,
        )[:, None]
        key_total, value_total = state
        scores = (
            jnp.einsum(
                "bphd,brhd->bhpr",
                query_part,
                key_four,
                precision=HIGHEST,
                preferred_element_type=jnp.float32,
            )
            * score_scale
        )
        scores = jnp.where(allowed, scores, NEG)
        prob = jnp.where(allowed, jnp.exp(scores - log_part[..., None]), 0.0)
        value_total = value_total + jnp.einsum(
            "bhpr,bphd->brhd",
            prob.astype(jnp.bfloat16),
            grad_part,
            preferred_element_type=jnp.float32,
        )
        dprob = jnp.einsum(
            "bphd,brhd->bhpr", grad_part, value_four, preferred_element_type=jnp.float32
        )
        dscore = prob * (dprob - delta_part[..., None])
        dscore_low = dscore.astype(jnp.bfloat16).astype(jnp.float32)
        key_total = key_total + jnp.einsum(
            "bhpr,bphd->brhd",
            dscore_low,
            query_part,
            precision=HIGHEST,
            preferred_element_type=jnp.float32,
        )
        return (key_total, value_total)

    return lax.fori_loop(0, part_len // block_len, key_visit, totals)


def body(activations, out_grads, doc_ids, query_weight, key_weight, value_weight, out_weight):
    score_scale = HEAD_DIM ** (-0.5)
    row_count = activations.shape[2]
    my_offset = lax.axis_index("ctx") * row_count
    full_query, full_key, full_value, full_out = (
        lax.all_gather(query_weight, "dp", axis=2, tiled=True),
        lax.all_gather(key_weight, "dp", axis=2, tiled=True),
        lax.all_gather(value_weight, "dp", axis=2, tiled=True),
        lax.all_gather(out_weight, "dp", axis=1, tiled=True),
    )
    page_inputs = activations[0]
    page_upstream = out_grads[0]
    page_ids = lax.dynamic_slice_in_dim(doc_ids, lax.axis_index("dp"), 1, 0)
    proj_query = full_query[0]
    proj_key = full_key[0]
    proj_value = full_value[0]
    proj_out = full_out[0]
    head_count = proj_query.shape[1] // HEAD_DIM
    inputs = page_inputs.astype(jnp.float32)
    inv_rms = lax.rsqrt(jnp.mean(inputs * inputs, axis=-1, keepdims=True) + 1e-05)
    normed = (inputs * inv_rms).astype(jnp.bfloat16)
    queries = jnp.einsum("brd,dh->brh", normed, proj_query, preferred_element_type=jnp.float32)
    key_rows = jnp.einsum("brd,dh->brh", normed, proj_key, preferred_element_type=jnp.float32)
    value_rows = jnp.einsum(
        "brd,dh->brh", normed, proj_value, preferred_element_type=jnp.float32
    ).astype(jnp.bfloat16)
    out_grad = jnp.einsum(
        "brd,hd->brh", page_upstream, proj_out, preferred_element_type=jnp.float32
    ).astype(jnp.bfloat16)
    block_table = page_ids[:, :, None] == page_ids[:, None, :]
    all_keys, wide_values = (
        lax.all_gather(key_rows, "ctx", axis=1, tiled=True),
        lax.all_gather(value_rows.astype(jnp.float32), "ctx", axis=1, tiled=True),
    )
    all_values = wide_values.astype(jnp.bfloat16)
    log_total, row_delta = row_statistics(
        queries, out_grad, all_keys, all_values, block_table, my_offset, head_count, score_scale
    )
    all_log_total, all_delta = (
        lax.all_gather(log_total, "ctx", axis=1, tiled=True),
        lax.all_gather(row_delta, "ctx", axis=1, tiled=True),
    )
    q_grad = query_side(
        queries,
        out_grad,
        all_keys,
        all_values,
        block_table,
        my_offset,
        log_total,
        row_delta,
        head_count,
        score_scale,
    )
    empty = jnp.zeros((key_rows.shape[0], row_count, head_count, HEAD_DIM), jnp.float32)
    key_total, value_total = key_side(
        (empty, empty),
        (
            lax.all_gather(queries, "ctx", axis=1, tiled=True),
            lax.all_gather(out_grad.astype(jnp.float32), "ctx", axis=1, tiled=True),
        ),
        key_rows,
        value_rows,
        all_log_total,
        all_delta,
        block_table,
        my_offset,
        head_count,
        score_scale,
    )
    k_grad = (key_total * score_scale).astype(jnp.bfloat16).reshape(key_rows.shape)
    v_grad = value_total.astype(jnp.bfloat16).reshape(value_rows.shape)
    summed = jnp.einsum("brh,dh->brd", q_grad, proj_query, preferred_element_type=jnp.float32)
    summed = summed + jnp.einsum(
        "brh,dh->brd", k_grad, proj_key, preferred_element_type=jnp.float32
    )
    normed_grad = summed + jnp.einsum(
        "brh,dh->brd", v_grad, proj_value, preferred_element_type=jnp.float32
    )
    branch = inv_rms * normed_grad - inputs * inv_rms**3 * jnp.mean(
        normed_grad * inputs, axis=-1, keepdims=True
    )
    branch_grad = branch.astype(jnp.bfloat16)[None]
    return from_behind(branch_grad, "section", -1)


def solution(mesh):
    return jax.shard_map(
        body,
        mesh=mesh,
        in_specs=(
            P("section", "dp", "ctx", None),
            P("section", "dp", "ctx", None),
            P(),
            P("section", None, "dp"),
            P("section", None, "dp"),
            P("section", None, "dp"),
            P("section", "dp", None),
        ),
        out_specs=P("section", "dp", "ctx", None),
        check_vma=False,
    )
```

profile of v0, /device:TPU:0, one launch (start us, length us, event | category | flops | bytes accessed | tf_op | source)
XLA Modules:
  0.0 217.6 jit_solution(16143003009868170029)
XLA Ops:
  6.5 0.0 copy-start
  6.5 0.0 all-gather.11.cloned.1.call-start
  6.5 0.7 all-gather.11.cloned.1.call-update
  7.3 0.0 all-gather.13.cloned.1.call-start
  7.3 0.7 all-gather.13.cloned.1.call-update
  8.0 0.0 all-gather.17.cloned.1.call-start
  8.1 0.7 all-gather.17.cloned.1.call-update
  8.7 0.0 all-gather.15.cloned.1.call-start
  8.8 0.5 all-gather.15.cloned.1.call-update
  9.3 0.0 all-gather.19.cloned.1.call-start
  9.4 1.1 fusion.32
  10.5 21.2 %all-gather.11.cloned.1.call-done = bf16[1,1280,640]{1,2,0:T(8,128)(2,1)} async-done(((bf16[1,1280,160]{1,2,0:T(8,128)(2,1)}), bf16[1,1280,640]{1,2,0:T(8,128)(2,1)}) %all-gather.11.cloned.1.call-update) | async-done | bytes 1638416 | tf_op jit(solution)/shard_map/all_gather | solution.py:234
  31.7 2.8 %fusion.11 = f32[128,640]{1,0:T(8,128)} fusion(bf16[1,1280,640]{1,2,0:T(8,128)(2,1)} %all-gather.11.cloned.1.call-done, bf16[1,1,128,1280]{3,2,1,0:T(8,128)(2,1)S(1)} %copy-done.2, f32[128]{0:T(128)S(1)} %get-tuple-element.81), kind=kOutput, calls=%fused_computation.19 | convolution fusion | flops 210206720 | bytes 2294272 | tf_op jit(solution)/shard_map/brd,dh->brh/dot_general | solution.py:250
  34.5 0.0 all-gather.19.cloned.1.call-update
  34.5 0.0 all-gather.21.cloned.1.call-start
  34.6 0.7 fusion.44
  35.3 0.1 broadcast_compare_fusion
  35.3 0.2 dynamic-slice_reduce_fusion
  35.5 0.1 broadcast_bitcast_fusion.1
  35.6 0.1 broadcast_bitcast_fusion
  35.7 17.6 %all-gather.13.cloned.1.call-done = bf16[1,1280,640]{1,2,0:T(8,128)(2,1)} async-done(((bf16[1,1280,160]{1,2,0:T(8,128)(2,1)}), bf16[1,1280,640]{1,2,0:T(8,128)(2,1)}) %all-gather.13.cloned.1.call-update) | async-done | bytes 1638416 | tf_op jit(solution)/shard_map/all_gather | solution.py:233
  53.3 2.8 %fusion.8 = f32[128,640]{1,0:T(8,128)} fusion(bf16[1,1280,640]{1,2,0:T(8,128)(2,1)} %all-gather.13.cloned.1.call-done, bf16[1,1,128,1280]{3,2,1,0:T(8,128)(2,1)S(1)} %copy-done.2, f32[128]{0:T(128)S(1)} %get-tuple-element.81), kind=kOutput, calls=%fused_computation.16 | convolution fusion | flops 210206720 | bytes 2294272 | tf_op jit(solution)/shard_map/brd,dh->brh/dot_general | solution.py:249
  56.1 0.0 all-gather.21.cloned.1.call-update
  56.1 0.0 copy-start.8
  56.1 18.8 %all-gather.17.cloned.1.call-done = bf16[1,1280,640]{1,2,0:T(8,128)(2,1)} async-done(((bf16[1,1280,160]{1,2,0:T(8,128)(2,1)}), bf16[1,1280,640]{1,2,0:T(8,128)(2,1)}) %all-gather.17.cloned.1.call-update) | async-done | bytes 1638416 | tf_op jit(solution)/shard_map/all_gather | solution.py:235
  74.9 2.1 fusion.18
  77.0 19.4 %all-gather.15.cloned.1.call-done = bf16[1,640,1280]{2,1,0:T(8,128)(2,1)} async-done(((bf16[1,160,1280]{2,1,0:T(8,128)(2,1)}), bf16[1,640,1280]{2,1,0:T(8,128)(2,1)}) %all-gather.15.cloned.1.call-update) | async-done | bytes 1638416 | tf_op jit(solution)/shard_map/all_gather | solution.py:236
  96.4 2.1 fusion.15
  98.5 0.9 copy.18
  99.4 0.9 copy.22
  100.3 0.8 copy.19
  101.1 0.8 copy.24
  101.9 25.5 %all-gather.1 = bf16[512,640]{1,0:T(8,128)(2,1)S(1)} all-gather(bf16[128,640]{1,0:T(8,128)(2,1)S(1)} %fusion.18), channel_id=3, replica_groups=mesh['section'=2,'ctx'=4,'dp'=4] {'ctx'}, dimensions={0}, use_global_device_ids=true | all-gather | bytes 819200 | tf_op jit(solution)/shard_map/all_gather | solution.py:260
  127.4 1.1 copy.20
  128.5 22.5 %all-gather.3 = bf16[512,640]{1,0:T(8,128)(2,1)S(1)} all-gather(bf16[128,640]{1,0:T(8,128)(2,1)S(1)} %fusion.15), channel_id=5, replica_groups=mesh['section'=2,'ctx'=4,'dp'=4] {'ctx'}, dimensions={0}, use_global_device_ids=true | all-gather | bytes 819200 | tf_op jit(solution)/shard_map/all_gather | solution.py:287
  151.0 0.3 copy.23
  151.3 0.0 all-gather.19.cloned.1.call-done
  151.3 2.9 %copy.17 = f32[512,640]{0,1:T(8,128)} copy(f32[512,640]{1,0:T(8,128)} %all-gather.19.cloned.1.call-done) | data formatting | bytes 2621440 | tf_op jit(solution)/shard_map/all_gather | solution.py:259
  154.2 3.5 %fusion.49 = (f32[8,128]{1,0:T(8,128)S(1)}, f32[8,128,512]{2,1,0:T(8,128)S(1)}) fusion(f32[128,8,80]{0,2,1:T(8,128)} %bitcast.149, f32[512,8,80]{0,2,1:T(8,128)} %bitcast.142, pred[512]{0:T(512)(128)(4,1)S(1)} %broadcast_bitcast_fusion.1), kind=kOutput, calls=%fused_computation.73 | convolution fusion | flops 504888320 | bytes 3740160 | tf_op jit(solution)/shard_map/while/body/eval_jaxpr/brhd,bkhd->bhrk/dot_general | solution.py:122
  157.8 0.0 copy-done.10
  157.8 0.0 copy-done.12
  157.8 2.1 fusion
  159.9 13.4 %all_gather.37 = f32[1,512,8]{1,2,0:T(8,128)S(1)} all-gather(f32[1,128,8]{1,2,0:T(8,128)S(1)} %get-tuple-element.67), channel_id=1, replica_groups=mesh['section'=2,'ctx'=4,'dp'=4] {'ctx'}, dimensions={1}, use_global_device_ids=true | all-gather | bytes 20480 | tf_op jit(solution)/shard_map/all_gather | solution.py:267
  173.3 13.3 %all_gather.39 = f32[1,512,8]{1,2,0:T(8,128)S(1)} all-gather(f32[1,128,8]{1,2,0:T(8,128)S(1)} %get-tuple-element.66), channel_id=1, replica_groups=mesh['section'=2,'ctx'=4,'dp'=4] {'ctx'}, dimensions={1}, use_global_device_ids=true | all-gather | bytes 20480 | tf_op jit(solution)/shard_map/all_gather | solution.py:268
  186.6 0.0 all-gather.21.cloned.1.call-done
  186.7 2.8 %copy.21 = f32[512,640]{0,1:T(8,128)} copy(f32[512,640]{1,0:T(8,128)} %all-gather.21.cloned.1.call-done) | data formatting | bytes 2621440 | tf_op jit(solution)/shard_map/all_gather | solution.py:286
  189.4 5.5 %exponential_select_fusion = f32[8,512,128]{2,1,0:T(8,128)S(1)} fusion(f32[512,8,80]{0,2,1:T(8,128)} %bitcast.146, f32[128,8,80]{0,2,1:T(8,128)} %bitcast.155, f32[8,512]{1,0:T(8,128)S(1)} %bitcast.157, pred[512]{0:T(512)(128)(4,1)S(1)} %broadcast_bitcast_fusion), kind=kOutput, calls=%fused_computation.3 | convolution fusion | flops 505413632 | bytes 3752448 | tf_op jit(solution)/shard_map/while/body/eval_jaxpr/bphd,brhd->bhpr/dot_general | solution.py:194
  194.9 0.3 convolution_convert_fusion
  195.3 0.6 copy-done.11
  195.8 1.0 multiply_convert_fusion
  196.9 0.0 copy-done.7
  196.9 0.0 copy-start.1
  196.9 0.8 fusion.14
  197.7 0.6 copy-done.1
  198.4 1.6 fusion.13
  200.0 0.5 fusion.6
  200.5 0.9 copy-done.4
  201.4 0.5 convolution_add_fusion.1
  201.9 0.1 copy-done.5
  202.1 0.5 fusion.31
  202.6 0.2 fusion.36
  202.8 1.7 collective-permute-start
  204.5 5.5 %collective-permute-done = bf16[1,1,128,1280]{3,2,1,0:T(8,128)(2,1)S(1)} collective-permute-done((bf16[1,1,128,1280]{3,2,1,0:T(8,128)(2,1)S(1)}, bf16[1,1,128,1280]{3,2,1,0:T(8,128)(2,1)S(1)}, u32[]{:S(2)}, u32[]{:S(2)}) %collective-permute-start) | collective-permute-done | bytes 327712 | tf_op jit(solution)/shard_map/ppermute | solution.py:18
  210.0 0.7 copy.26
  (22 shorter events, 0.1 us)
Async XLA Ops:
  6.5 89.9 %copy-start = (bf16[1,1,128,1280]{3,2,1,0:T(8,128)(2,1)S(1)}, bf16[1,1,128,1280]{3,2,1,0:T(8,128)(2,1)}, u32[]{:S(2)}) copy-start(bf16[1,1,128,1280]{3,2,1,0:T(8,128)(2,1)} %param.8) | copy-start | bytes 983044
  6.5 25.1 %copy-start.2 = (bf16[1,1,128,1280]{3,2,1,0:T(8,128)(2,1)S(1)}, bf16[1,1,128,1280]{3,2,1,0:T(8,128)(2,1)}, u32[]{:S(2)}) copy-start(bf16[1,1,128,1280]{3,2,1,0:T(8,128)(2,1)} %param.7) | copy-start | bytes 983044
  6.5 25.1 %all-gather.11.cloned.1.call-start = ((), (), s32[]{:S(2)}) async-start(), calls=%async_computation | async-start | bytes 2048000 | tf_op jit(solution)/shard_map/all_gather | solution.py:234
  7.3 46.0 %all-gather.13.cloned.1.call-start = ((), (), s32[]{:S(2)}) async-start(), calls=%async_computation.1 | async-start | bytes 2048000 | tf_op jit(solution)/shard_map/all_gather | solution.py:233
  8.0 66.9 %all-gather.17.cloned.1.call-start = ((), (), s32[]{:S(2)}) async-start(), calls=%async_computation.3 | async-start | bytes 2048000 | tf_op jit(solution)/shard_map/all_gather | solution.py:235
  8.7 87.6 %all-gather.15.cloned.1.call-start = ((), (), s32[]{:S(2)}) async-start(), calls=%async_computation.2 | async-start | bytes 2048000 | tf_op jit(solution)/shard_map/all_gather | solution.py:236
  9.3 142.0 %all-gather.19.cloned.1.call-start = ((), (), s32[]{:S(2)}) async-start(), calls=%async_computation.4 | async-start | bytes 1638400 | tf_op jit(solution)/shard_map/all_gather | solution.py:259
  34.5 152.2 %all-gather.21.cloned.1.call-start = ((), (), s32[]{:S(2)}) async-start(), calls=%async_computation.5 | async-start | bytes 1638400 | tf_op jit(solution)/shard_map/all_gather | solution.py:286
  56.1 42.3 %copy-start.9 = (f32[128,640]{1,0:T(8,128)S(1)}, f32[128,640]{1,0:T(8,128)}, u32[]{:S(2)}) copy-start(f32[128,640]{1,0:T(8,128)} %fusion.8) | copy-start | bytes 983044
  56.1 43.2 %copy-start.8 = (f32[128,640]{1,0:T(8,128)S(1)}, f32[128,640]{1,0:T(8,128)}, u32[]{:S(2)}) copy-start(f32[128,640]{1,0:T(8,128)} %fusion.11) | copy-start | bytes 983044
  154.2 3.5 %copy-start.10 = (bf16[512,640]{0,1:T(8,128)(2,1)S(1)}, bf16[512,640]{0,1:T(8,128)(2,1)}, u32[]{:S(2)}) copy-start(bf16[512,640]{0,1:T(8,128)(2,1)} %copy.20) | copy-start | bytes 1966084
  154.2 3.5 %copy-start.12 = (bf16[128,640]{0,1:T(8,128)(2,1)S(1)}, bf16[128,640]{0,1:T(8,128)(2,1)}, u32[]{:S(2)}) copy-start(bf16[128,640]{0,1:T(8,128)(2,1)} %copy.19) | copy-start | bytes 491524
  194.9 0.9 copy-start.11
  195.3 1.6 copy-start.7
  195.8 1.9 copy-start.3
  196.9 1.5 copy-start.1
  198.4 1.6 copy-start.6
  200.0 1.4 copy-start.4
  200.5 1.6 copy-start.5
  202.8 7.1 %collective-permute-start = (bf16[1,1,128,1280]{3,2,1,0:T(8,128)(2,1)S(1)}, bf16[1,1,128,1280]{3,2,1,0:T(8,128)(2,1)S(1)}, u32[]{:S(2)}, u32[]{:S(2)}) collective-permute-start(bf16[1,1,128,1280]{3,2,1,0:T(8,128)(2,1)S(1)} %fusion.36), channel_id=1, source_target_pairs={{0,16},{16,0},{1,17},{17,1},{2,18},{18,2},{3,19},{19,3},{4,20},{20... | collective-permute-start | bytes 983048 | tf_op jit(solution)/shard_map/ppermute | solution.py:18
Sparse Core Ops, SparseCore 0:
  8.9 22.7 all-gather.10
  33.2 20.0 all-gather.12
  54.9 20.0 all-gather.16
  76.3 20.0 all-gather.14
  97.8 46.0 all-gather.18
  145.4 33.0 all-gather.20
where the time goes:
time: 218 us
  waiting for transfers between devices  85.1 us (39%)
  blocking collectives  74.8 us (34%)
  matrix products  26.1 us (12%)
  local copies, waits for them, and re-layouts  14.5 us (7%)
  between operations  13.7 us (6%)
    all_gather x1, blocking collectives, body(): lax.all_gather(value_rows.astype(jnp.float32), 'ctx', axis=1, tiled=True)  25.5 us
    all_gather x1, blocking collectives, body(): lax.all_gather(out_grad.astype(jnp.float32), 'ctx', axis=1, tiled=True)  22.5 us
    all_gather x1, waiting for transfers between devices, body(): lax.all_gather(key_weight, 'dp', axis=2, tiled=True)  21.2 us
    all_gather x1, waiting for transfers between devices, body(): lax.all_gather(out_weight, 'dp', axis=1, tiled=True)  19.4 us
    all_gather x1, waiting for transfers between devices, body(): lax.all_gather(value_weight, 'dp', axis=2, tiled=True)  18.8 us
    all_gather x1, waiting for transfers between devices, body(): lax.all_gather(query_weight, 'dp', axis=2, tiled=True)  17.6 us
    all_gather x1, blocking collectives, body(): lax.all_gather(log_total, 'ctx', axis=1, tiled=True)  13.4 us
    all_gather x1, blocking collectives, body(): lax.all_gather(row_delta, 'ctx', axis=1, tiled=True)  13.3 us
  transfers between devices with their start and end apart: 7, of which 5 were waited for; matrix products, arithmetic and copies ran while one was open for 12% of the time, Pallas kernels for 0%

commit v1 on v0

v1 whole, which is shorter than its diff:
```python
import functools
import math

import jax
import jax.numpy as jnp
from jax import lax
from jax.experimental import pallas as pl
from jax.experimental.pallas import tpu as pltpu
from jax.sharding import PartitionSpec as P

HEAD_DIM = 80
BLOCK = 128
QKV = 3 * HEAD_DIM
NEG = -1e30
SCALE = HEAD_DIM**-0.5
LOG2E = math.log2(math.e)
F32 = jnp.float32
BF16 = jnp.bfloat16


def dot_nn(a, b):
    return lax.dot_general(a, b, (((1,), (0,)), ((), ())), preferred_element_type=F32)


def dot_nt(a, b):
    return lax.dot_general(a, b, (((1,), (1,)), ((), ())), preferred_element_type=F32)


def split(x):
    high = x.astype(BF16)
    return high, (x - high.astype(F32)).astype(BF16)


def inverse_rms(x):
    return lax.rsqrt(jnp.mean(x * x, axis=-1, keepdims=True) + 1e-05)


def window_flags(ids_ref, count):
    page, me, blocks = lax.axis_index("dp"), lax.axis_index("ctx"), lax.axis_size("ctx")
    mine = ids_ref[page, me]

    def same(at):
        inside = jnp.clip(at, 0, blocks - 1)
        return (inside == at) & (ids_ref[page, inside] == mine)

    flags = []
    for place in range(1, count):
        behind = same(me - place)
        flags.append((behind, behind | same(me + count - place)))
    return flags


def masks(flags):
    ones = jnp.ones((1, BLOCK), F32)
    row_mask = jnp.concatenate([ones] + [ones * valid.astype(F32) for _, valid in flags], axis=1)
    window = row_mask.shape[1]
    first = lax.broadcasted_iota(jnp.int32, (16, window), 0) == 0
    key_bias = jnp.where(first, 1.0 - row_mask, 0.0).astype(BF16)
    query_bias = jnp.where(first, NEG, 0.0).astype(BF16)
    return key_bias, query_bias, row_mask


def heads_backward(packs, grads, normed, key_bias, query_bias, row_mask):
    window = normed.shape[1]
    chunk = min(window, 384)
    qkv = [dot_nn(pack, normed) for pack in packs]
    queries, keys = [], []
    key_rows, value_rows = [], []
    for part in qkv:
        q_high, q_low = split(part[:HEAD_DIM] * (SCALE * LOG2E))
        k_high, k_low = split(part[HEAD_DIM : 2 * HEAD_DIM])
        queries.append(jnp.concatenate([q_high, q_high, q_low, query_bias], axis=0))
        keys.append(jnp.concatenate([k_high, k_low], axis=0))
        key_rows.append(jnp.concatenate([k_high, k_low, k_high, key_bias], axis=0).T)
        value_rows.append(part[2 * HEAD_DIM :].astype(BF16).T)

    heads = range(len(packs))
    own_query, own_key, own_value = [None for _ in heads], [0.0 for _ in heads], [0.0 for _ in heads]
    for start in range(0, window, chunk):
        cols = slice(start, start + chunk)
        scores = [dot_nn(key_rows[h], queries[h][:, cols]) for h in heads]
        dprob = [dot_nn(value_rows[h], grads[h][:, cols]) for h in heads]
        weights, inverse, delta = [], [], []
        for h in heads:
            weights.append(jnp.exp2(scores[h] - jnp.max(scores[h], axis=0, keepdims=True)))
            total = 1.0 / jnp.sum(weights[h], axis=0, keepdims=True)
            delta.append(jnp.sum(weights[h] * dprob[h], axis=0, keepdims=True) * total)
            inverse.append(total * row_mask[:, cols])
        for h in heads:
            prob = weights[h][:BLOCK] * inverse[h]
            dscore = (prob * (dprob[h][:BLOCK] - delta[h])).astype(BF16)
            own_value[h] = own_value[h] + dot_nt(grads[h][:, cols], prob.astype(BF16))
            own_key[h] = own_key[h] + dot_nt(queries[h][HEAD_DIM:QKV, cols], dscore)
            if start == 0:
                dscore_rows = (
                    weights[h][:, :BLOCK]
                    * inverse[h][:, :BLOCK]
                    * (dprob[h][:, :BLOCK] - delta[h][:, :BLOCK])
                ).astype(BF16)
                own_query[h] = dot_nn(keys[h], dscore_rows)
    result = None
    for h in heads:
        q_grad = ((own_query[h][:HEAD_DIM] + own_query[h][HEAD_DIM:]) * SCALE).astype(BF16)
        k_grad = ((own_key[h][:HEAD_DIM] + own_key[h][HEAD_DIM:]) * (1.0 / LOG2E)).astype(BF16)
        rows = jnp.concatenate([q_grad, k_grad, own_value[h].astype(BF16)], axis=0).T
        part = dot_nn(rows, packs[h])
        result = part if result is None else result + part
    return result


def for_place(index, count, flags, fill):
    if index == 0:
        fill(0)
        return
    behind = flags[index - 1][0]
    even = lax.rem(lax.axis_index("ctx"), 2) == 0
    for is_behind, is_even in ((a, b) for a in (True, False) for b in (True, False)):
        distance = index if is_behind else count - index
        slot = 2 * distance - 1 if is_behind != is_even else 2 * distance

        @pl.when((behind == is_behind) & (even == is_even))
        def _():
            fill(slot)


def transposed_normed(input_ref):
    x = input_ref[...].astype(F32)
    return (x * inverse_rms(x)).astype(BF16).T


def pack_kernel(*refs):
    weights, (local_ref, shared_ref, sems) = refs[:3], refs[3:]
    even = lax.rem(lax.axis_index("ctx"), 2) == 0

    def to(ref, at):
        return ref.at[pl.ds(at * HEAD_DIM, HEAD_DIM), :]

    heads = local_ref.shape[0] // QKV
    copies = [
        pltpu.make_async_copy(
            to(weights[at], h), to(local_ref, 3 * h + at), sems.at[3 * h + at]
        )
        for h in range(heads)
        for at in range(3)
    ]
    for copy in copies:
        copy.start()
    for copy in copies:
        copy.wait()
    shared_ref[:HEAD_DIM, :] = local_ref[QKV + HEAD_DIM : QKV + 2 * HEAD_DIM, :]
    for is_even, at in ((True, 0), (False, 2)):

        @pl.when(even == is_even)
        def _():
            first = QKV + at * HEAD_DIM
            shared_ref[HEAD_DIM:, :] = local_ref[first : first + HEAD_DIM, :]


def start_kernel(input_ref, grad_ref, even_ref, odd_ref, *refs):
    *weight_refs, normed_ref, to_even_ref, to_odd_ref = refs
    width = normed_ref.shape[0]
    normed_ref[...] = transposed_normed(input_ref)
    to_even_ref[:width, :] = transposed_normed(odd_ref)
    to_odd_ref[:width, :] = transposed_normed(even_ref)
    grad_rows(grad_ref, weight_refs, (to_even_ref, to_odd_ref), width)


def grad_rows(grad_ref, weight_refs, rows_refs, start):
    for weight_ref in weight_refs:
        size = weight_ref.shape[0]
        part = dot_nt(weight_ref[...], grad_ref[...]).astype(BF16)
        for rows_ref in rows_refs:
            rows_ref[start : start + size, :] = part
        start += size


def relay_kernel(skip, grad_ref, even_ref, odd_ref, *refs):
    *weight_refs, to_even_ref, to_odd_ref = refs
    rows = even_ref.shape[0] - skip
    to_even_ref[:rows, :] = odd_ref[skip:, :]
    to_odd_ref[:rows, :] = even_ref[skip:, :]
    grad_rows(grad_ref, weight_refs, (to_even_ref, to_odd_ref), rows)


def first_kernel(count, grad_at, ids_ref, *refs):
    slots = 2 * count - 1
    blocks, grad_slots = refs[:slots], refs[slots : 2 * slots]
    *pack_refs, normed_ref, total_ref, window_ref = refs[2 * slots :]
    width, rows = normed_ref.shape[0], window_ref.shape[0]
    flags = window_flags(ids_ref, count)
    for index in range(count):

        def fill(slot):
            cols = pl.ds(index * BLOCK, BLOCK)
            normed_ref[:, cols] = blocks[slot][:width, :]
            window_ref[:, cols] = grad_slots[slot][grad_at[slot] : grad_at[slot] + rows, :]

        for_place(index, count, flags, fill)
    packs = [ref[at : at + QKV, :] for ref in pack_refs for at in range(0, ref.shape[0], QKV)]
    grads = [window_ref[h * HEAD_DIM : (h + 1) * HEAD_DIM, :] for h in range(len(packs))]
    total_ref[...] = heads_backward(packs, grads, normed_ref[...], *masks(flags))


def next_kernel(count, grad_at, places, shared, last, ids_ref, *refs):
    slots = 2 * count - 1
    grad_slots = refs[:slots]
    per_head = 2 if shared else 1
    normed_ref, so_far_ref, *pieces = refs[slots : slots + 2 + per_head * len(places)]
    *rest, total_ref, window_ref, pack_ref = refs[slots + 2 + per_head * len(places) :]
    flags = window_flags(ids_ref, count)
    for index in range(count):

        def fill(slot):
            cols = pl.ds(index * BLOCK, BLOCK)
            for at, h in enumerate(places):
                to = slice(at * HEAD_DIM, (at + 1) * HEAD_DIM)
                start = grad_at[slot] + h * HEAD_DIM
                window_ref[to, cols] = grad_slots[slot][start : start + HEAD_DIM, :]

        for_place(index, count, flags, fill)
    packs, grads = [], []
    even = lax.rem(lax.axis_index("ctx"), 2) == 0
    for at in range(len(places)):
        if shared:
            mine, other = pieces[2 * at : 2 * at + 2]
            pack_ref[at, HEAD_DIM : 2 * HEAD_DIM, :] = mine[:HEAD_DIM, :]
            for is_even in (True, False):

                @pl.when(even == is_even)
                def _():
                    low, high = mine[HEAD_DIM:, :], other[...]
                    pack_ref[at, :HEAD_DIM, :] = low if is_even else high
                    pack_ref[at, 2 * HEAD_DIM :, :] = high if is_even else low

            packs.append(pack_ref[at])
        else:
            packs.append(pieces[at][...])
        grads.append(window_ref[at * HEAD_DIM : (at + 1) * HEAD_DIM, :])
    total = so_far_ref[...] + heads_backward(packs, grads, normed_ref[...], *masks(flags))
    if last:
        x = rest[0][...].astype(F32)
        inv_rms = inverse_rms(x)
        branch = inv_rms * total - x * inv_rms**3 * jnp.mean(total * x, axis=-1, keepdims=True)
        total_ref[...] = branch.astype(BF16)
    else:
        total_ref[...] = total


def call(kernel, operands, out_shape, window, scratch=(), scalars=True, space=pltpu.VMEM):
    vmem = pl.BlockSpec(memory_space=pltpu.VMEM)
    specs = [pl.BlockSpec(memory_space=pltpu.SMEM)] if scalars else []
    if space != pltpu.VMEM:
        operands = [pltpu.with_memory_space_constraint(ref, space) for ref in operands]
    return pl.pallas_call(
        kernel,
        out_shape=out_shape,
        in_specs=specs + [pl.BlockSpec(memory_space=space)] * (len(operands) - len(specs)),
        out_specs=jax.tree.map(lambda _: vmem, out_shape),
        scratch_shapes=list(scratch),
        compiler_params=pltpu.CompilerParams(vmem_limit_bytes=(8 << 20) + window * (32 << 10)),
        cost_estimate=pl.CostEstimate(flops=1000, bytes_accessed=1000, transcendentals=0),
    )(*operands)


def pair_swap(array, first):
    length, width = lax.axis_size("ctx"), lax.axis_size("dp")
    pairs = []
    for i in range(length):
        low = i - (i - first) % 2
        for d in range(width):
            if low >= 0 and low + 1 < length:
                pairs.append((i * width + d, (2 * low + 1 - i) * width + d))
            else:
                pairs.append((i * width + d, i * width + (d ^ 1)))
    return lax.ppermute(array, ("ctx", "dp"), pairs)


def pair_steps(even, odd):
    return pair_swap(odd, 0), pair_swap(even, 1)


def after(values, *others):
    return lax.optimization_barrier((values, others))[0]


def dp_swap(array, by):
    return lax.ppermute(array, "dp", [(i, i ^ by) for i in range(lax.axis_size("dp"))])


def body(activations, out_grads, doc_ids, query_weight, key_weight, value_weight, out_weight):
    own_input, own_grad = activations[0, 0], out_grads[0, 0]
    width = own_input.shape[-1]
    count = 3 * lax.axis_size("ctx") // 4
    window = count * BLOCK
    heads = query_weight.shape[2] // HEAD_DIM

    sized = lambda rows, columns, dtype: jax.ShapeDtypeStruct((rows, columns), dtype)
    some = 2 * heads * HEAD_DIM

    own_out = out_weight[0]
    far_out = dp_swap(own_out, 2)
    near_out = dp_swap(own_out, 1)
    steps = [pair_steps(own_input, own_input)]
    local, shared = call(
        pack_kernel,
        [query_weight[0].T, key_weight[0].T, value_weight[0].T],
        (sized(heads * QKV, width, BF16), sized(2 * HEAD_DIM, width, BF16)),
        window,
        scratch=[pltpu.SemaphoreType.DMA((3 * heads,))],
        scalars=False,
        space=pltpu.HBM,
    )
    far_shared = dp_swap(shared, 2)
    near = dp_swap(after(local, steps[0], far_out, near_out), 1)

    normed, near_grad, to_odd_first = call(
        start_kernel,
        [own_input, own_grad, *steps[0], own_out, near_out],
        (sized(width, BLOCK, BF16),) + (sized(width + some, BLOCK, BF16),) * 2,
        window,
        scalars=False,
    )
    steps.append(pair_steps(to_odd_first, near_grad))
    far_near_out = dp_swap(far_out, 1)
    skip = width if count == 3 else 0
    far_grad, to_odd = call(
        functools.partial(relay_kernel, skip),
        [after(own_grad, near), *steps[1], far_out, far_near_out],
        (sized(steps[1][0].shape[0] - skip + some, BLOCK, BF16),) * 2,
        window,
        scalars=False,
    )
    steps.append(pair_steps(to_odd, far_grad))
    far_whole = dp_swap(after(local[:QKV], far_out, far_grad), 2)
    while len(steps) < count + 1:
        drop = {count - 1: width, count: some}.get(len(steps), 0)
        steps.append(pair_steps(*(ref[drop:] for ref in steps[-1])))

    def slots(own, first, until_end):
        pairs = [pair for pair in steps[first : first + count - 1]]
        refs = [own] + [ref for pair in pairs for ref in pair]
        return refs, [ref.shape[0] - until_end for ref in refs]

    first_pair = (to_odd_first, near_grad)
    normed_slots = [normed] + [ref for pair in [first_pair] + steps[1 : count - 1] for ref in pair]
    grad_slots, _ = slots(near_grad, 1, 0)
    grad_at = [ref.shape[0] - some for ref in grad_slots[:3]]
    grad_at += [ref.shape[0] - 2 * some for ref in grad_slots[3:]]
    window_normed, total = call(
        functools.partial(first_kernel, count, grad_at),
        [doc_ids, *normed_slots, *grad_slots, local, near],
        (sized(width, window, BF16), sized(BLOCK, width, F32)),
        window,
        scratch=[pltpu.VMEM((some, window), BF16)],
    )

    far_near_shared = dp_swap(after(far_shared, steps[2]), 1)
    ctx_edge = pair_swap(after(far_shared, steps[2])[HEAD_DIM:], 0)
    far_near_edge = dp_swap(after(ctx_edge, total), 1)
    grad_slots, grad_at = slots(far_grad, 2, some)

    def add(total, places, shared, pieces, extra=()):
        return call(
            functools.partial(next_kernel, count, grad_at, places, shared, bool(extra)),
            [doc_ids, *grad_slots, window_normed, total, *pieces, *extra],
            sized(BLOCK, width, BF16 if extra else F32),
            window,
            scratch=[
                pltpu.VMEM((len(places) * HEAD_DIM, window), BF16),
                pltpu.VMEM((len(places), QKV, width), BF16),
            ],
        )

    pieces = (far_shared, ctx_edge, far_near_shared, far_near_edge)
    total = add(total, (1, heads + 1), True, pieces)
    far_near_whole = dp_swap(after(far_whole, total), 1)
    total = add(total, (0,), False, [far_whole])
    result = add(total, (heads,), False, [far_near_whole], [own_input])
    sections = lax.axis_size("section")
    result = lax.ppermute(result, "section", [(i, (i - 1) % sections) for i in range(sections)])
    return result[None, None]


def solution(mesh):
    return jax.shard_map(
        body,
        mesh=mesh,
        in_specs=(
            P("section", "dp", "ctx", None),
            P("section", "dp", "ctx", None),
            P(),
            P("section", None, "dp"),
            P("section", None, "dp"),
            P("section", None, "dp"),
            P("section", "dp", None),
        ),
        out_specs=P("section", "dp", "ctx", None),
        check_vma=False,
    )
```

time: 218 us -> 63 us (0.29)
  blocking collectives: 74.8 us -> 0 us
  waiting for transfers between devices: 85.1 us -> 31.6 us
  matrix products: 26.1 us -> 0 us
  starting transfers between devices: 1.87 us -> 16.9 us
  local copies, waits for them, and re-layouts: 14.5 us -> 0.81 us
  between operations: 13.7 us -> 0.16 us
  Pallas kernels: 0 us -> 13.4 us
    all_gather x6 -> x0, waiting for transfers between devices: 77 us -> none  [the longest x1 21.2 us: body(): lax.all_gather(key_weight, 'dp', axis=2, tiled=True)]
    all_gather x4 -> x0, blocking collectives: 74.8 us -> none  [the longest x1 25.5 us: body(): lax.all_gather(value_rows.astype(jnp.float32), 'ctx', axis=1, tiled=True)]
    ppermute x1 -> x19, waiting for transfers between devices: 5.46 us -> 31.6 us  [the longest x9 23 us: pair_swap(): return lax.ppermute(array, ('ctx', 'dp'), pairs)]
    dot_general x14 -> x0, matrix products: 26.1 us -> none  [the longest x1 5.48 us: key_visit(): jnp.einsum('bphd,brhd->bhpr', query_part, key_four, precision=HIGHEST, pr...]
    ppermute x1 -> x19, starting transfers between devices: 1.68 us -> 16.9 us  [the longest x9 10.2 us: pair_swap(): return lax.ppermute(array, ('ctx', 'dp'), pairs)]
    pallas_call x0 -> x7, Pallas kernels: none -> 13.4 us  [call(): pl.pallas_call(kernel, out_shape=out_shape, in_specs=specs + [pl.BlockSpe...]
    all_gather x2 -> x0, local copies, waits for them, and re-layouts: 5.67 us -> none  [the longest x1 2.9 us: body(): lax.all_gather(key_rows, 'ctx', axis=1, tiled=True)]
    convert_element_type x4 -> x0, local copies, waits for them, and re-layouts: 2.98 us -> none  [the longest x1 1.1 us: body(): all_values = wide_values.astype(jnp.bfloat16)]
  transfers between devices with their start and end apart: 7 -> 19, of which waited for: 5 -> 6; matrix products, arithmetic and copies ran while one was open for 12% -> 0% of each run, Pallas kernels for 0% -> 18%
where the time goes in v1:
time: 63 us; the launch traced here: 62.9 us
  waiting for transfers between devices  31.6 us (50%)
  starting transfers between devices  16.9 us (27%)
  Pallas kernels  13.4 us (21%)
  local copies, waits for them, and re-layouts  0.81 us (1%)
    ppermute x9, waiting for transfers between devices, pair_swap(): return lax.ppermute(array, ('ctx', 'dp'), pairs)  23 us
    pallas_call x7, Pallas kernels, call(): pl.pallas_call(kernel, out_shape=out_shape, in_specs=specs + [pl.BlockSpe...  13.4 us
    ppermute x9, starting transfers between devices, pair_swap(): return lax.ppermute(array, ('ctx', 'dp'), pairs)  10.2 us
    ppermute x1, waiting for transfers between devices, body(): lax.ppermute(result, 'section', [(i, (i - 1) % sections) for i in range(s...  8.59 us
    ppermute x9, starting transfers between devices, dp_swap(): lax.ppermute(array, 'dp', [(i, i ^ by) for i in range(lax.axis_size('dp'))])  5.09 us
    ppermute x1, starting transfers between devices, body(): lax.ppermute(result, 'section', [(i, (i - 1) % sections) for i in range(s...  1.58 us
  transfers between devices with their start and end apart: 19, of which 6 were waited for; matrix products, arithmetic and copies ran while one was open for 0% of the time, Pallas kernels for 18%

profile of v1, /device:TPU:0, one launch (start us, length us, event | category | flops | bytes accessed | tf_op | source)
XLA Modules:
  0.0 62.9 jit_solution(6595586319354664226)
XLA Ops:
  0.0 0.0 copy-start.2
  0.0 0.0 copy-start
  0.0 0.0 copy-start.1
  0.0 3.0 %collective-permute-start.2 = (bf16[160,1280]{1,0:T(8,128)(2,1)}, bf16[160,1280]{1,0:T(8,128)(2,1)S(1)}, u32[]{:S(2)}, u32[]{:S(2)}) collective-permute-start(bf16[160,1280]{1,0:T(8,128)(2,1)} %bitcast.19), channel_id=1, source_target_pairs={{0,2},{1,3},{2,0},{3,1},{4,6},{5,7},{6,4},{7,5},{8,10},{9,11},{10,... | collective-permute-start | bytes 1228808 | tf_op jit(solution)/shard_map/ppermute | solution.py:287
  3.0 0.0 collective-permute-start.3
  3.0 1.6 %collective-permute-start = (bf16[128,1280]{1,0:T(8,128)(2,1)}, bf16[128,1280]{1,0:T(8,128)(2,1)S(1)}, u32[]{:S(2)}, u32[]{:S(2)}) collective-permute-start(bf16[128,1280]{1,0:T(8,128)(2,1)} %bitcast.13), channel_id=1, source_target_pairs={{0,4},{1,5},{2,6},{3,7},{4,0},{5,1},{6,2},{7,3},{8,12},{9,13},{10,... | collective-permute-start | bytes 983048 | tf_op jit(solution)/shard_map/ppermute | solution.py:275
  4.6 0.2 collective-permute-start.1
  4.8 1.4 %shard_map.73 = (bf16[480,1280]{1,0:T(8,128)(2,1)S(1)}, bf16[160,1280]{1,0:T(8,128)(2,1)S(1)}) custom-call(bf16[160,1280]{1,0:T(8,128)(2,1)} %bitcast.22, bf16[160,1280]{1,0:T(8,128)(2,1)} %bitcast.23, bf16[160,1280]{1,0:T(8,128)(2,1)} %bitcast.24), custom_call_target="tpu_custom_call" | custom-call | flops 1000 | bytes 1000 | tf_op jit(solution)/shard_map/pallas_call | solution.py:254
  6.3 7.1 %collective-permute-done.even_ref = bf16[128,1280]{1,0:T(8,128)(2,1)S(1)} collective-permute-done((bf16[128,1280]{1,0:T(8,128)(2,1)}, bf16[128,1280]{1,0:T(8,128)(2,1)S(1)}, u32[]{:S(2)}, u32[]{:S(2)}) %collective-permute-start) | collective-permute-done | bytes 327712 | tf_op jit(solution)/shard_map/ppermute | solution.py:275
  13.4 0.0 collective-permute-done.1.odd_ref
  13.4 0.0 collective-permute-done.2.refs_0_
  13.4 0.0 collective-permute-done.3.refs_1_
  13.4 0.1 collective-permute-start.4
  13.4 0.0 copy-done.2
  13.5 0.0 copy-done
  13.5 0.0 copy-done.1
  13.5 0.6 shard_map.74
  14.1 2.7 %collective-permute-start.5 = (bf16[1600,128]{1,0:T(8,128)(2,1)S(1)}, bf16[1600,128]{1,0:T(8,128)(2,1)S(1)}, u32[]{:S(2)}, u32[]{:S(2)}) collective-permute-start(bf16[1600,128]{1,0:T(8,128)(2,1)S(1)} %get-tuple-element.23.refs_2_.refs_5_), channel_id=1, source_target_pairs={{0,4},{1,5},{2,6},{3,7},{4,0},{5,1},{6,2},{7,3},{8,12},{9,13},{10,... | collective-permute-start | bytes 1228808 | tf_op jit(solution)/shard_map/ppermute | solution.py:275
  16.8 0.2 collective-permute-start.6
  17.0 0.3 collective-permute-start.7
  17.3 0.5 collective-permute-start.12
  17.9 0.0 copy-start.3
  17.9 0.0 collective-permute-done.4.refs_11_
  17.9 9.0 %collective-permute-done.5.even_ref.refs_3_.refs_6_ = bf16[1600,128]{1,0:T(8,128)(2,1)S(1)} collective-permute-done((bf16[1600,128]{1,0:T(8,128)(2,1)S(1)}, bf16[1600,128]{1,0:T(8,128)(2,1)S(1)}, u32[]{:S(2)}, u32[]{:S(2)}) %collective-permute-start.5) | collective-permute-done | bytes 409632 | tf_op jit(solution)/shard_map/ppermute | solution.py:275
  26.9 0.0 collective-permute-done.6.odd_ref.refs_4_.refs_7_
  26.9 0.0 collective-permute-done.7.refs_1_
  26.9 0.4 shard_map.75
  27.3 0.6 collective-permute-start.16
  27.9 2.2 %collective-permute-start.8 = (bf16[640,128]{1,0:T(8,128)(2,1)S(1)}, bf16[640,128]{1,0:T(8,128)(2,1)S(1)}, u32[]{:S(2)}, u32[]{:S(2)}) collective-permute-start(bf16[640,128]{1,0:T(8,128)(2,1)S(1)} %get-tuple-element.25.refs_0_), channel_id=1, source_target_pairs={{0,4},{1,5},{2,6},{3,7},{4,0},{5,1},{6,2},{7,3},{8,12},{9,13},{10,... | collective-permute-start | bytes 491528 | tf_op jit(solution)/shard_map/ppermute | solution.py:275
  30.2 0.0 collective-permute-start.9
  30.2 0.0 collective-permute-done.12.refs_7_
  30.2 3.8 %collective-permute-done.8.refs_8_.refs_1_ = bf16[640,128]{1,0:T(8,128)(2,1)S(1)} collective-permute-done((bf16[640,128]{1,0:T(8,128)(2,1)S(1)}, bf16[640,128]{1,0:T(8,128)(2,1)S(1)}, u32[]{:S(2)}, u32[]{:S(2)}) %collective-permute-start.8) | collective-permute-done | bytes 163872 | tf_op jit(solution)/shard_map/ppermute | solution.py:275
  33.9 0.0 collective-permute-done.9.refs_9_.refs_2_
  34.0 1.8 %collective-permute-start.13 = (bf16[80,1280]{1,0:T(8,128)(2,1)S(1)}, bf16[80,1280]{1,0:T(8,128)(2,1)S(1)}, u32[]{:S(2)}, u32[]{:S(2)}) collective-permute-start(bf16[80,1280]{1,0:T(8,128)(2,1)S(1)} %slice.14), channel_id=1, source_target_pairs={{0,4},{1,5},{2,6},{3,7},{4,0},{5,1},{6,2},{7,3},{8,12},{9,13},{10,... | collective-permute-start | bytes 614408 | tf_op jit(solution)/shard_map/ppermute | solution.py:275
  35.8 0.0 collective-permute-start.14
  35.8 0.0 copy-done.3
  35.8 4.0 %shard_map.76 = (bf16[1280,384]{1,0:T(8,128)(2,1)S(1)}, f32[128,1280]{1,0:T(8,128)S(1)}) custom-call(s32[4,4]{1,0:T(4,128)S(1)} %copy-done.3, bf16[1280,128]{1,0:T(8,128)(2,1)S(1)} %get-tuple-element.27.refs_0_, bf16[1600,128]{1,0:T(8,128)(2,1)S(1)} %get-tuple-element.24.refs_1_, bf16[1600,128]{1,0:T(8,128)(2,1)S(1)} %get-tuple-element.23.refs_2_.refs_5_, ...), custom_call_target="tpu_custom_call" | custom-call | flops 1000 | bytes 1000 | tf_op jit(solution)/shard_map/pallas_call | solution.py:254
  39.7 0.1 collective-permute-done.13.refs_8_
  39.8 0.5 collective-permute-start.15
  40.3 1.3 %collective-permute-start.10 = (bf16[320,128]{1,0:T(8,128)(2,1)S(1)}, bf16[320,128]{1,0:T(8,128)(2,1)S(1)}, u32[]{:S(2)}, u32[]{:S(2)}) collective-permute-start(bf16[320,128]{1,0:T(8,128)(2,1)S(1)} %slice.16), channel_id=1, source_target_pairs={{0,4},{1,5},{2,6},{3,7},{4,0},{5,1},{6,2},{7,3},{8,12},{9,13},{10,... | collective-permute-start | bytes 245768 | tf_op jit(solution)/shard_map/ppermute | solution.py:275
  41.6 0.2 collective-permute-start.11
  41.8 3.0 %collective-permute-done.10.refs_3_ = bf16[320,128]{1,0:T(8,128)(2,1)S(1)} collective-permute-done((bf16[320,128]{1,0:T(8,128)(2,1)S(1)}, bf16[320,128]{1,0:T(8,128)(2,1)S(1)}, u32[]{:S(2)}, u32[]{:S(2)}) %collective-permute-start.10) | collective-permute-done | bytes 81952 | tf_op jit(solution)/shard_map/ppermute | solution.py:275
  44.8 0.0 collective-permute-done.11.refs_4_
  44.8 0.0 collective-permute-done.14.refs_9_
  44.8 0.0 collective-permute-done.15.refs_10_
  44.8 2.7 %shard_map.77.refs_6_ = f32[128,1280]{1,0:T(8,128)S(1)} custom-call(s32[4,4]{1,0:T(4,128)S(1)} %copy-done.3, bf16[640,128]{1,0:T(8,128)(2,1)S(1)} %get-tuple-element.25.refs_0_, bf16[640,128]{1,0:T(8,128)(2,1)S(1)} %collective-permute-done.8.refs_8_.refs_1_, bf16[640,128]{1,0:T(8,128)(2,1)S(1)} %collective-permute-done.9.refs_9_.refs_2_, ...), custom_call_target="tpu_custom_call" | custom-call | flops 1000 | bytes 1000 | tf_op jit(solution)/shard_map/pallas_call | solution.py:254
  47.5 0.0 collective-permute-done.16.refs_7_
  47.5 0.1 collective-permute-start.17
  47.6 2.1 %shard_map.78.refs_6_ = f32[128,1280]{1,0:T(8,128)S(1)} custom-call(s32[4,4]{1,0:T(4,128)S(1)} %copy-done.3, bf16[640,128]{1,0:T(8,128)(2,1)S(1)} %get-tuple-element.25.refs_0_, bf16[640,128]{1,0:T(8,128)(2,1)S(1)} %collective-permute-done.8.refs_8_.refs_1_, bf16[640,128]{1,0:T(8,128)(2,1)S(1)} %collective-permute-done.9.refs_9_.refs_2_, ...), custom_call_target="tpu_custom_call" | custom-call | flops 1000 | bytes 1000 | tf_op jit(solution)/shard_map/pallas_call | solution.py:254
  49.7 0.0 collective-permute-done.17.refs_7_
  49.7 2.2 %shard_map.79 = bf16[128,1280]{1,0:T(8,128)(2,1)S(1)} custom-call(s32[4,4]{1,0:T(4,128)S(1)} %copy-done.3, bf16[640,128]{1,0:T(8,128)(2,1)S(1)} %get-tuple-element.25.refs_0_, bf16[640,128]{1,0:T(8,128)(2,1)S(1)} %collective-permute-done.8.refs_8_.refs_1_, bf16[640,128]{1,0:T(8,128)(2,1)S(1)} %collective-permute-done.9.refs_9_.refs_2_, ...), custom_call_target="tpu_custom_call" | custom-call | flops 1000 | bytes 1000 | tf_op jit(solution)/shard_map/pallas_call | solution.py:254
  52.0 1.6 %collective-permute-start.18 = (bf16[128,1280]{1,0:T(8,128)(2,1)S(1)}, bf16[128,1280]{1,0:T(8,128)(2,1)S(1)}, u32[]{:S(2)}, u32[]{:S(2)}) collective-permute-start(bf16[128,1280]{1,0:T(8,128)(2,1)S(1)} %shard_map.79), channel_id=1, source_target_pairs={{0,16},{16,0},{1,17},{17,1},{2,18},{18,2},{3,19},{19,3},{4,20},{20... | collective-permute-start | bytes 983048 | tf_op jit(solution)/shard_map/ppermute | solution.py:380
  53.5 8.6 %collective-permute-done.18 = bf16[128,1280]{1,0:T(8,128)(2,1)S(1)} collective-permute-done((bf16[128,1280]{1,0:T(8,128)(2,1)S(1)}, bf16[128,1280]{1,0:T(8,128)(2,1)S(1)}, u32[]{:S(2)}, u32[]{:S(2)}) %collective-permute-start.18) | collective-permute-done | bytes 327712 | tf_op jit(solution)/shard_map/ppermute | solution.py:380
  62.1 0.7 %copy.9 = bf16[1,1,128,1280]{3,2,1,0:T(8,128)(2,1)} copy(bf16[1,1,128,1280]{3,2,1,0:T(8,128)(2,1)S(1)} %bitcast.25) | data formatting | bytes 655360
  (4 shorter events, 0.1 us)
Async XLA Ops:
  0.0 13.4 %copy-start.2 = (bf16[1,160,1280]{2,1,0:T(8,128)(2,1)S(1)}, bf16[1,160,1280]{2,1,0:T(8,128)(2,1)}, u32[]{:S(2)}) copy-start(bf16[1,160,1280]{2,1,0:T(8,128)(2,1)} %param.13) | copy-start | bytes 1228804
  0.0 13.5 %copy-start = (bf16[1,1,128,1280]{3,2,1,0:T(8,128)(2,1)S(1)}, bf16[1,1,128,1280]{3,2,1,0:T(8,128)(2,1)}, u32[]{:S(2)}) copy-start(bf16[1,1,128,1280]{3,2,1,0:T(8,128)(2,1)} %param.7) | copy-start | bytes 983044
  0.0 13.5 %copy-start.1 = (bf16[1,1,128,1280]{3,2,1,0:T(8,128)(2,1)S(1)}, bf16[1,1,128,1280]{3,2,1,0:T(8,128)(2,1)}, u32[]{:S(2)}) copy-start(bf16[1,1,128,1280]{3,2,1,0:T(8,128)(2,1)} %param.8) | copy-start | bytes 983044
  0.0 13.3 %collective-permute-start.2 = (bf16[160,1280]{1,0:T(8,128)(2,1)}, bf16[160,1280]{1,0:T(8,128)(2,1)S(1)}, u32[]{:S(2)}, u32[]{:S(2)}) collective-permute-start(bf16[160,1280]{1,0:T(8,128)(2,1)} %bitcast.19), channel_id=1, source_target_pairs={{0,2},{1,3},{2,0},{3,1},{4,6},{5,7},{6,4},{7,5},{8,10},{9,11},{10,... | collective-permute-start | bytes 1228808 | tf_op jit(solution)/shard_map/ppermute | solution.py:287
  3.0 10.3 %collective-permute-start.3 = (bf16[160,1280]{1,0:T(8,128)(2,1)}, bf16[160,1280]{1,0:T(8,128)(2,1)S(1)}, u32[]{:S(2)}, u32[]{:S(2)}) collective-permute-start(bf16[160,1280]{1,0:T(8,128)(2,1)} %bitcast.20), channel_id=1, source_target_pairs={{0,1},{1,0},{2,3},{3,2},{4,5},{5,4},{6,7},{7,6},{8,9},{9,8},{10,11... | collective-permute-start | bytes 1228808 | tf_op jit(solution)/shard_map/ppermute | solution.py:287
  3.0 10.3 %collective-permute-start = (bf16[128,1280]{1,0:T(8,128)(2,1)}, bf16[128,1280]{1,0:T(8,128)(2,1)S(1)}, u32[]{:S(2)}, u32[]{:S(2)}) collective-permute-start(bf16[128,1280]{1,0:T(8,128)(2,1)} %bitcast.13), channel_id=1, source_target_pairs={{0,4},{1,5},{2,6},{3,7},{4,0},{5,1},{6,2},{7,3},{8,12},{9,13},{10,... | collective-permute-start | bytes 983048 | tf_op jit(solution)/shard_map/ppermute | solution.py:275
  4.6 8.8 %collective-permute-start.1 = (bf16[128,1280]{1,0:T(8,128)(2,1)}, bf16[128,1280]{1,0:T(8,128)(2,1)S(1)}, u32[]{:S(2)}, u32[]{:S(2)}) collective-permute-start(bf16[128,1280]{1,0:T(8,128)(2,1)} %bitcast.14), channel_id=1, source_target_pairs={{0,1},{1,0},{2,3},{3,2},{4,8},{5,9},{6,10},{7,11},{8,4},{9,5},{10,... | collective-permute-start | bytes 983048 | tf_op jit(solution)/shard_map/ppermute | solution.py:275
  13.4 4.6 %collective-permute-start.4 = (bf16[480,1280]{1,0:T(8,128)(2,1)S(1)}, bf16[480,1280]{1,0:T(8,128)(2,1)S(1)}, u32[]{:S(2)}, u32[]{:S(2)}) collective-permute-start(bf16[480,1280]{1,0:T(8,128)(2,1)S(1)} %get-tuple-element.21.refs_10_), channel_id=1, source_target_pairs={{0,1},{1,0},{2,3},{3,2},{4,5},{5,4},{6,7},{7,6},{8,9},{9,8},{10,11... | collective-permute-start | bytes 3686408 | tf_op jit(solution)/shard_map/ppermute | solution.py:287
  14.1 12.8 %collective-permute-start.5 = (bf16[1600,128]{1,0:T(8,128)(2,1)S(1)}, bf16[1600,128]{1,0:T(8,128)(2,1)S(1)}, u32[]{:S(2)}, u32[]{:S(2)}) collective-permute-start(bf16[1600,128]{1,0:T(8,128)(2,1)S(1)} %get-tuple-element.23.refs_2_.refs_5_), channel_id=1, source_target_pairs={{0,4},{1,5},{2,6},{3,7},{4,0},{5,1},{6,2},{7,3},{8,12},{9,13},{10,... | collective-permute-start | bytes 1228808 | tf_op jit(solution)/shard_map/ppermute | solution.py:275
  16.8 10.1 %collective-permute-start.6 = (bf16[1600,128]{1,0:T(8,128)(2,1)S(1)}, bf16[1600,128]{1,0:T(8,128)(2,1)S(1)}, u32[]{:S(2)}, u32[]{:S(2)}) collective-permute-start(bf16[1600,128]{1,0:T(8,128)(2,1)S(1)} %get-tuple-element.24.refs_1_), channel_id=1, source_target_pairs={{0,1},{1,0},{2,3},{3,2},{4,8},{5,9},{6,10},{7,11},{8,4},{9,5},{10,... | collective-permute-start | bytes 1228808 | tf_op jit(solution)/shard_map/ppermute | solution.py:275
  17.0 9.9 %collective-permute-start.7 = (bf16[160,1280]{1,0:T(8,128)(2,1)S(1)}, bf16[160,1280]{1,0:T(8,128)(2,1)S(1)}, u32[]{:S(2)}, u32[]{:S(2)}) collective-permute-start(bf16[160,1280]{1,0:T(8,128)(2,1)S(1)} %collective-permute-done.2.refs_0_), channel_id=1, source_target_pairs={{0,1},{1,0},{2,3},{3,2},{4,5},{5,4},{6,7},{7,6},{8,9},{9,8},{10,11... | collective-permute-start | bytes 1228808 | tf_op jit(solution)/shard_map/ppermute | solution.py:287
  17.3 12.8 %collective-permute-start.12 = (bf16[160,1280]{1,0:T(8,128)(2,1)S(1)}, bf16[160,1280]{1,0:T(8,128)(2,1)S(1)}, u32[]{:S(2)}, u32[]{:S(2)}) collective-permute-start(bf16[160,1280]{1,0:T(8,128)(2,1)S(1)} %get-tuple-element.30), channel_id=1, source_target_pairs={{0,2},{1,3},{2,0},{3,1},{4,6},{5,7},{6,4},{7,5},{8,10},{9,11},{10,... | collective-permute-start | bytes 1228808 | tf_op jit(solution)/shard_map/ppermute | solution.py:287
  17.9 17.9 %copy-start.3 = (s32[4,4]{1,0:T(4,128)S(1)}, s32[4,4]{1,0:T(4,128)}, u32[]{:S(2)}) copy-start(s32[4,4]{1,0:T(4,128)} %ids_ref.7) | copy-start | bytes 196
  27.3 20.2 %collective-permute-start.16 = (bf16[240,1280]{1,0:T(8,128)(2,1)S(1)}, bf16[240,1280]{1,0:T(8,128)(2,1)S(1)}, u32[]{:S(2)}, u32[]{:S(2)}) collective-permute-start(bf16[240,1280]{1,0:T(8,128)(2,1)S(1)} %slice.15), channel_id=1, source_target_pairs={{0,2},{1,3},{2,0},{3,1},{4,6},{5,7},{6,4},{7,5},{8,10},{9,11},{10,... | collective-permute-start | bytes 1843208 | tf_op jit(solution)/shard_map/ppermute | solution.py:287
  27.9 6.0 %collective-permute-start.8 = (bf16[640,128]{1,0:T(8,128)(2,1)S(1)}, bf16[640,128]{1,0:T(8,128)(2,1)S(1)}, u32[]{:S(2)}, u32[]{:S(2)}) collective-permute-start(bf16[640,128]{1,0:T(8,128)(2,1)S(1)} %get-tuple-element.25.refs_0_), channel_id=1, source_target_pairs={{0,4},{1,5},{2,6},{3,7},{4,0},{5,1},{6,2},{7,3},{8,12},{9,13},{10,... | collective-permute-start | bytes 491528 | tf_op jit(solution)/shard_map/ppermute | solution.py:275
  30.2 3.8 %collective-permute-start.9 = (bf16[640,128]{1,0:T(8,128)(2,1)S(1)}, bf16[640,128]{1,0:T(8,128)(2,1)S(1)}, u32[]{:S(2)}, u32[]{:S(2)}) collective-permute-start(bf16[640,128]{1,0:T(8,128)(2,1)S(1)} %get-tuple-element.26), channel_id=1, source_target_pairs={{0,1},{1,0},{2,3},{3,2},{4,8},{5,9},{6,10},{7,11},{8,4},{9,5},{10,... | collective-permute-start | bytes 491528 | tf_op jit(solution)/shard_map/ppermute | solution.py:275
  34.0 5.9 %collective-permute-start.13 = (bf16[80,1280]{1,0:T(8,128)(2,1)S(1)}, bf16[80,1280]{1,0:T(8,128)(2,1)S(1)}, u32[]{:S(2)}, u32[]{:S(2)}) collective-permute-start(bf16[80,1280]{1,0:T(8,128)(2,1)S(1)} %slice.14), channel_id=1, source_target_pairs={{0,4},{1,5},{2,6},{3,7},{4,0},{5,1},{6,2},{7,3},{8,12},{9,13},{10,... | collective-permute-start | bytes 614408 | tf_op jit(solution)/shard_map/ppermute | solution.py:275
  35.8 9.0 %collective-permute-start.14 = (bf16[160,1280]{1,0:T(8,128)(2,1)S(1)}, bf16[160,1280]{1,0:T(8,128)(2,1)S(1)}, u32[]{:S(2)}, u32[]{:S(2)}) collective-permute-start(bf16[160,1280]{1,0:T(8,128)(2,1)S(1)} %collective-permute-done.12.refs_7_), channel_id=1, source_target_pairs={{0,1},{1,0},{2,3},{3,2},{4,5},{5,4},{6,7},{7,6},{8,9},{9,8},{10,11... | collective-permute-start | bytes 1228808 | tf_op jit(solution)/shard_map/ppermute | solution.py:287
  39.8 5.0 %collective-permute-start.15 = (bf16[80,1280]{1,0:T(8,128)(2,1)S(1)}, bf16[80,1280]{1,0:T(8,128)(2,1)S(1)}, u32[]{:S(2)}, u32[]{:S(2)}) collective-permute-start(bf16[80,1280]{1,0:T(8,128)(2,1)S(1)} %collective-permute-done.13.refs_8_), channel_id=1, source_target_pairs={{0,1},{1,0},{2,3},{3,2},{4,5},{5,4},{6,7},{7,6},{8,9},{9,8},{10,11... | collective-permute-start | bytes 614408 | tf_op jit(solution)/shard_map/ppermute | solution.py:287
  40.3 4.4 %collective-permute-start.10 = (bf16[320,128]{1,0:T(8,128)(2,1)S(1)}, bf16[320,128]{1,0:T(8,128)(2,1)S(1)}, u32[]{:S(2)}, u32[]{:S(2)}) collective-permute-start(bf16[320,128]{1,0:T(8,128)(2,1)S(1)} %slice.16), channel_id=1, source_target_pairs={{0,4},{1,5},{2,6},{3,7},{4,0},{5,1},{6,2},{7,3},{8,12},{9,13},{10,... | collective-permute-start | bytes 245768 | tf_op jit(solution)/shard_map/ppermute | solution.py:275
  41.6 3.2 %collective-permute-start.11 = (bf16[320,128]{1,0:T(8,128)(2,1)S(1)}, bf16[320,128]{1,0:T(8,128)(2,1)S(1)}, u32[]{:S(2)}, u32[]{:S(2)}) collective-permute-start(bf16[320,128]{1,0:T(8,128)(2,1)S(1)} %slice.17), channel_id=1, source_target_pairs={{0,1},{1,0},{2,3},{3,2},{4,8},{5,9},{6,10},{7,11},{8,4},{9,5},{10,... | collective-permute-start | bytes 245768 | tf_op jit(solution)/shard_map/ppermute | solution.py:275
  47.5 2.2 %collective-permute-start.17 = (bf16[240,1280]{1,0:T(8,128)(2,1)S(1)}, bf16[240,1280]{1,0:T(8,128)(2,1)S(1)}, u32[]{:S(2)}, u32[]{:S(2)}) collective-permute-start(bf16[240,1280]{1,0:T(8,128)(2,1)S(1)} %collective-permute-done.16.refs_7_), channel_id=1, source_target_pairs={{0,1},{1,0},{2,3},{3,2},{4,5},{5,4},{6,7},{7,6},{8,9},{9,8},{10,11... | collective-permute-start | bytes 1843208 | tf_op jit(solution)/shard_map/ppermute | solution.py:287
  52.0 10.2 %collective-permute-start.18 = (bf16[128,1280]{1,0:T(8,128)(2,1)S(1)}, bf16[128,1280]{1,0:T(8,128)(2,1)S(1)}, u32[]{:S(2)}, u32[]{:S(2)}) collective-permute-start(bf16[128,1280]{1,0:T(8,128)(2,1)S(1)} %shard_map.79), channel_id=1, source_target_pairs={{0,16},{16,0},{1,17},{17,1},{2,18},{18,2},{3,19},{19,3},{4,20},{20... | collective-permute-start | bytes 983048 | tf_op jit(solution)/shard_map/ppermute | solution.py:380

commit v2 on v1

--- a/solution.py
+++ b/solution.py
@@ -11,6 +11,7 @@
 HEAD_DIM = 80
 BLOCK = 128
 QKV = 3 * HEAD_DIM
+NEAR_CUT = 320
 NEG = -1e30
 SCALE = HEAD_DIM**-0.5
 LOG2E = math.log2(math.e)
@@ -129,31 +130,18 @@
 
 
 def pack_kernel(*refs):
-    weights, (local_ref, shared_ref, sems) = refs[:3], refs[3:]
-    even = lax.rem(lax.axis_index("ctx"), 2) == 0
-
-    def to(ref, at):
+    *weights, local_ref, sems = refs
+    heads = local_ref.shape[0] // QKV
+
+    def part(ref, at):
         return ref.at[pl.ds(at * HEAD_DIM, HEAD_DIM), :]
 
-    heads = local_ref.shape[0] // QKV
-    copies = [
-        pltpu.make_async_copy(
-            to(weights[at], h), to(local_ref, 3 * h + at), sems.at[3 * h + at]
-        )
-        for h in range(heads)
-        for at in range(3)
-    ]
+    pairs = [(part(weights[at], h), part(local_ref, 3 * h + at)) for h in range(heads) for at in range(3)]
+    copies = [pltpu.make_async_copy(*pair, sems.at[i]) for i, pair in enumerate(pairs)]
     for copy in copies:
         copy.start()
     for copy in copies:
         copy.wait()
-    shared_ref[:HEAD_DIM, :] = local_ref[QKV + HEAD_DIM : QKV + 2 * HEAD_DIM, :]
-    for is_even, at in ((True, 0), (False, 2)):
-
-        @pl.when(even == is_even)
-        def _():
-            first = QKV + at * HEAD_DIM
-            shared_ref[HEAD_DIM:, :] = local_ref[first : first + HEAD_DIM, :]
 
 
 def start_kernel(input_ref, grad_ref, even_ref, odd_ref, *refs):
@@ -196,17 +184,20 @@
             window_ref[:, cols] = grad_slots[slot][grad_at[slot] : grad_at[slot] + rows, :]
 
         for_place(index, count, flags, fill)
-    packs = [ref[at : at + QKV, :] for ref in pack_refs for at in range(0, ref.shape[0], QKV)]
+    local_ref, *near_refs = pack_refs
+    near = jnp.concatenate([ref[...] for ref in near_refs], axis=0)
+    starts = range(0, local_ref.shape[0], QKV)
+    packs = [local_ref[at : at + QKV, :] for at in starts] + [near[at : at + QKV] for at in starts]
     grads = [window_ref[h * HEAD_DIM : (h + 1) * HEAD_DIM, :] for h in range(len(packs))]
     total_ref[...] = heads_backward(packs, grads, normed_ref[...], *masks(flags))
 
 
-def next_kernel(count, grad_at, places, shared, last, ids_ref, *refs):
+def next_kernel(count, grad_at, places, last, ids_ref, *refs):
     slots = 2 * count - 1
     grad_slots = refs[:slots]
-    per_head = 2 if shared else 1
-    normed_ref, so_far_ref, *pieces = refs[slots : slots + 2 + per_head * len(places)]
-    *rest, total_ref, window_ref, pack_ref = refs[slots + 2 + per_head * len(places) :]
+    normed_ref, so_far_ref, *rest, total_ref, window_ref = refs[slots:]
+    if last:
+        *rest, input_ref = rest
     flags = window_flags(ids_ref, count)
     for index in range(count):
 
@@ -218,27 +209,13 @@
                 window_ref[to, cols] = grad_slots[slot][start : start + HEAD_DIM, :]
 
         for_place(index, count, flags, fill)
-    packs, grads = [], []
-    even = lax.rem(lax.axis_index("ctx"), 2) == 0
-    for at in range(len(places)):
-        if shared:
-            mine, other = pieces[2 * at : 2 * at + 2]
-            pack_ref[at, HEAD_DIM : 2 * HEAD_DIM, :] = mine[:HEAD_DIM, :]
-            for is_even in (True, False):
-
-                @pl.when(even == is_even)
-                def _():
-                    low, high = mine[HEAD_DIM:, :], other[...]
-                    pack_ref[at, :HEAD_DIM, :] = low if is_even else high
-                    pack_ref[at, 2 * HEAD_DIM :, :] = high if is_even else low
-
-            packs.append(pack_ref[at])
-        else:
-            packs.append(pieces[at][...])
-        grads.append(window_ref[at * HEAD_DIM : (at + 1) * HEAD_DIM, :])
+    packs = [rest[0][...]]
+    if len(places) > 1:
+        packs.append(jnp.concatenate([ref[...] for ref in rest[1:]], axis=0))
+    grads = [window_ref[at * HEAD_DIM : (at + 1) * HEAD_DIM, :] for at in range(len(places))]
     total = so_far_ref[...] + heads_backward(packs, grads, normed_ref[...], *masks(flags))
     if last:
-        x = rest[0][...].astype(F32)
+        x = input_ref[...].astype(F32)
         inv_rms = inverse_rms(x)
         branch = inv_rms * total - x * inv_rms**3 * jnp.mean(total * x, axis=-1, keepdims=True)
         total_ref[...] = branch.astype(BF16)
@@ -297,85 +274,77 @@
     sized = lambda rows, columns, dtype: jax.ShapeDtypeStruct((rows, columns), dtype)
     some = 2 * heads * HEAD_DIM
 
+    out_rows = heads * HEAD_DIM
     own_out = out_weight[0]
     far_out = dp_swap(own_out, 2)
     near_out = dp_swap(own_out, 1)
     steps = [pair_steps(own_input, own_input)]
-    local, shared = call(
+    local = call(
         pack_kernel,
         [query_weight[0].T, key_weight[0].T, value_weight[0].T],
-        (sized(heads * QKV, width, BF16), sized(2 * HEAD_DIM, width, BF16)),
+        sized(heads * QKV, width, BF16),
         window,
         scratch=[pltpu.SemaphoreType.DMA((3 * heads,))],
         scalars=False,
         space=pltpu.HBM,
     )
-    far_shared = dp_swap(shared, 2)
-    near = dp_swap(after(local, steps[0], far_out, near_out), 1)
-
-    normed, near_grad, to_odd_first = call(
+    near = [dp_swap(part, 1) for part in (local[:NEAR_CUT], local[NEAR_CUT:])]
+    far_last = dp_swap(local[QKV : 2 * QKV], 2)
+
+    normed, near_grad, first_odd = call(
         start_kernel,
-        [own_input, own_grad, *steps[0], own_out, near_out],
+        [own_input, after(own_grad, far_out), *steps[0], own_out, near_out],
         (sized(width, BLOCK, BF16),) + (sized(width + some, BLOCK, BF16),) * 2,
         window,
         scalars=False,
     )
-    steps.append(pair_steps(to_odd_first, near_grad))
-    far_near_out = dp_swap(far_out, 1)
+    steps.append(pair_steps(first_odd, near_grad))
+    far_out = after(far_out, normed)
+    far_near_out = [dp_swap(far_out[at : at + HEAD_DIM], 1) for at in range(0, out_rows, HEAD_DIM)]
     skip = width if count == 3 else 0
     far_grad, to_odd = call(
         functools.partial(relay_kernel, skip),
-        [after(own_grad, near), *steps[1], far_out, far_near_out],
+        [own_grad, *steps[1], far_out, *far_near_out],
         (sized(steps[1][0].shape[0] - skip + some, BLOCK, BF16),) * 2,
         window,
         scalars=False,
     )
     steps.append(pair_steps(to_odd, far_grad))
-    far_whole = dp_swap(after(local[:QKV], far_out, far_grad), 2)
+    far_first = dp_swap(after(local[:QKV], far_last, far_grad), 2)
+    thirds = after(far_last, far_grad)
+    far_near_last = [dp_swap(thirds[at : at + HEAD_DIM], 1) for at in range(0, QKV, HEAD_DIM)]
     while len(steps) < count + 1:
         drop = {count - 1: width, count: some}.get(len(steps), 0)
         steps.append(pair_steps(*(ref[drop:] for ref in steps[-1])))
 
-    def slots(own, first, until_end):
-        pairs = [pair for pair in steps[first : first + count - 1]]
-        refs = [own] + [ref for pair in pairs for ref in pair]
-        return refs, [ref.shape[0] - until_end for ref in refs]
-
-    first_pair = (to_odd_first, near_grad)
-    normed_slots = [normed] + [ref for pair in [first_pair] + steps[1 : count - 1] for ref in pair]
-    grad_slots, _ = slots(near_grad, 1, 0)
-    grad_at = [ref.shape[0] - some for ref in grad_slots[:3]]
-    grad_at += [ref.shape[0] - 2 * some for ref in grad_slots[3:]]
+    flat = lambda own, pairs: [own] + [ref for pair in pairs for ref in pair]
+    normed_slots = flat(normed, [(first_odd, near_grad)] + steps[1 : count - 1])
+    near_slots = flat(near_grad, steps[1:count])
+    near_at = [ref.shape[0] - some for ref in near_slots[:3]]
+    near_at += [ref.shape[0] - 2 * some for ref in near_slots[3:]]
+    far_slots = flat(far_grad, steps[2 : count + 1])
+    far_at = [ref.shape[0] - some for ref in far_slots]
     window_normed, total = call(
-        functools.partial(first_kernel, count, grad_at),
-        [doc_ids, *normed_slots, *grad_slots, local, near],
+        functools.partial(first_kernel, count, near_at),
+        [doc_ids, *normed_slots, *near_slots, local, *near],
         (sized(width, window, BF16), sized(BLOCK, width, F32)),
         window,
         scratch=[pltpu.VMEM((some, window), BF16)],
     )
 
-    far_near_shared = dp_swap(after(far_shared, steps[2]), 1)
-    ctx_edge = pair_swap(after(far_shared, steps[2])[HEAD_DIM:], 0)
-    far_near_edge = dp_swap(after(ctx_edge, total), 1)
-    grad_slots, grad_at = slots(far_grad, 2, some)
-
-    def add(total, places, shared, pieces, extra=()):
+    def add(total, places, packs, extra=()):
         return call(
-            functools.partial(next_kernel, count, grad_at, places, shared, bool(extra)),
-            [doc_ids, *grad_slots, window_normed, total, *pieces, *extra],
+            functools.partial(next_kernel, count, far_at, places, bool(extra)),
+            [doc_ids, *far_slots, window_normed, total, *packs, *extra],
             sized(BLOCK, width, BF16 if extra else F32),
             window,
-            scratch=[
-                pltpu.VMEM((len(places) * HEAD_DIM, window), BF16),
-                pltpu.VMEM((len(places), QKV, width), BF16),
-            ],
+            scratch=[pltpu.VMEM((len(places) * HEAD_DIM, window), BF16)],
         )
 
-    pieces = (far_shared, ctx_edge, far_near_shared, far_near_edge)
-    total = add(total, (1, heads + 1), True, pieces)
-    far_near_whole = dp_swap(after(far_whole, total), 1)
-    total = add(total, (0,), False, [far_whole])
-    result = add(total, (heads,), False, [far_near_whole], [own_input])
+    total = add(total, (1, heads + 1), [far_last, *far_near_last])
+    far_near_first = dp_swap(after(far_first, total), 1)
+    total = add(total, (0,), [far_first])
+    result = add(total, (heads,), [far_near_first], [own_input])
     sections = lax.axis_size("section")
     result = lax.ppermute(result, "section", [(i, (i - 1) % sections) for i in range(sections)])
     return result[None, None]

time: 63 us -> 60.9 us (0.967)
  waiting for transfers between devices: 31.6 us -> 28.9 us
    ppermute x9 -> x8, waiting for transfers between devices: 23 us -> 6.51 us  [pair_swap(): return lax.ppermute(array, ('ctx', 'dp'), pairs)]
    ppermute x9 -> x12, waiting for transfers between devices: 0.02 us -> 13.8 us  [dp_swap(): lax.ppermute(array, 'dp', [(i, i ^ by) for i in range(lax.axis_size('dp'))])]
    ppermute x9 -> x12, starting transfers between devices: 5.09 us -> 5.72 us  [dp_swap(): lax.ppermute(array, 'dp', [(i, i ^ by) for i in range(lax.axis_size('dp'))])]
    ppermute x9 -> x8, starting transfers between devices: 10.2 us -> 10 us  [pair_swap(): return lax.ppermute(array, ('ctx', 'dp'), pairs)]
  transfers between devices with their start and end apart: 19 -> 21, of which waited for: 6 -> 7; matrix products, arithmetic and copies ran while one was open for 0% -> 0% of each run, Pallas kernels for 18% -> 18%
where the time goes in v2:
time: 60.9 us; the launch traced here: 60.7 us
  waiting for transfers between devices  28.9 us (47%)
  starting transfers between devices  17.3 us (28%)
  Pallas kernels  13.3 us (22%)
  local copies, waits for them, and re-layouts  0.99 us (2%)
    ppermute x12, waiting for transfers between devices, dp_swap(): lax.ppermute(array, 'dp', [(i, i ^ by) for i in range(lax.axis_size('dp'))])  13.8 us
    pallas_call x7, Pallas kernels, call(): pl.pallas_call(kernel, out_shape=out_shape, in_specs=specs + [pl.BlockSpe...  13.3 us
    ppermute x8, starting transfers between devices, pair_swap(): return lax.ppermute(array, ('ctx', 'dp'), pairs)  10 us
    ppermute x1, waiting for transfers between devices, body(): lax.ppermute(result, 'section', [(i, (i - 1) % sections) for i in range(s...  8.6 us
    ppermute x8, waiting for transfers between devices, pair_swap(): return lax.ppermute(array, ('ctx', 'dp'), pairs)  6.51 us
    ppermute x12, starting transfers between devices, dp_swap(): lax.ppermute(array, 'dp', [(i, i ^ by) for i in range(lax.axis_size('dp'))])  5.72 us
    ppermute x1, starting transfers between devices, body(): lax.ppermute(result, 'section', [(i, (i - 1) % sections) for i in range(s...  1.58 us
  transfers between devices with their start and end apart: 21, of which 7 were waited for; matrix products, arithmetic and copies ran while one was open for 0% of the time, Pallas kernels for 18%

profile of v2, /device:TPU:0, one launch (start us, length us, event | category | flops | bytes accessed | tf_op | source)
XLA Modules:
  0.0 60.7 jit_solution(17363349626617863753)
XLA Ops:
  0.0 3.0 %collective-permute-start.1 = (bf16[128,1280]{1,0:T(8,128)(2,1)}, bf16[128,1280]{1,0:T(8,128)(2,1)S(1)}, u32[]{:S(2)}, u32[]{:S(2)}) collective-permute-start(bf16[128,1280]{1,0:T(8,128)(2,1)} %bitcast.13), channel_id=1, source_target_pairs={{0,4},{1,5},{2,6},{3,7},{4,0},{5,1},{6,2},{7,3},{8,12},{9,13},{10,... | collective-permute-start | bytes 983048 | tf_op jit(solution)/shard_map/ppermute | solution.py:252
  3.0 0.0 collective-permute-start.2
  3.0 1.5 %collective-permute-start = (bf16[160,1280]{1,0:T(8,128)(2,1)}, bf16[160,1280]{1,0:T(8,128)(2,1)S(1)}, u32[]{:S(2)}, u32[]{:S(2)}) collective-permute-start(bf16[160,1280]{1,0:T(8,128)(2,1)} %bitcast.19), channel_id=1, source_target_pairs={{0,2},{1,3},{2,0},{3,1},{4,6},{5,7},{6,4},{7,5},{8,10},{9,11},{10,... | collective-permute-start | bytes 1228808 | tf_op jit(solution)/shard_map/ppermute | solution.py:264
  4.5 0.2 collective-permute-start.3
  4.7 1.4 %shard_map.75.refs_10_ = bf16[480,1280]{1,0:T(8,128)(2,1)S(1)} custom-call(bf16[160,1280]{1,0:T(8,128)(2,1)} %bitcast.22, bf16[160,1280]{1,0:T(8,128)(2,1)} %bitcast.23, bf16[160,1280]{1,0:T(8,128)(2,1)} %bitcast.24), custom_call_target="tpu_custom_call" | custom-call | flops 1000 | bytes 1000 | tf_op jit(solution)/shard_map/pallas_call | solution.py:231
  6.2 0.0 copy-start
  6.2 0.0 copy-start.1
  6.2 0.0 copy-start.2
  6.2 0.1 fusion
  6.3 0.6 collective-permute-start.14
  6.9 8.6 %collective-permute-done.refs_0_ = bf16[160,1280]{1,0:T(8,128)(2,1)S(1)} collective-permute-done((bf16[160,1280]{1,0:T(8,128)(2,1)}, bf16[160,1280]{1,0:T(8,128)(2,1)S(1)}, u32[]{:S(2)}, u32[]{:S(2)}) %collective-permute-start) | collective-permute-done | bytes 409632 | tf_op jit(solution)/shard_map/ppermute | solution.py:264
  15.5 0.0 collective-permute-done.1.even_ref
  15.5 0.0 collective-permute-done.2.odd_ref
  15.5 0.0 collective-permute-done.3.refs_1_
  15.5 0.0 copy-done
  15.5 0.0 copy-done.1
  15.5 0.0 copy-done.2
  15.5 0.6 shard_map.73
  16.1 3.4 %collective-permute-start.4 = (bf16[1600,128]{1,0:T(8,128)(2,1)S(1)}, bf16[1600,128]{1,0:T(8,128)(2,1)S(1)}, u32[]{:S(2)}, u32[]{:S(2)}) collective-permute-start(bf16[1600,128]{1,0:T(8,128)(2,1)S(1)} %get-tuple-element.18.refs_2_.refs_5_), channel_id=1, source_target_pairs={{0,4},{1,5},{2,6},{3,7},{4,0},{5,1},{6,2},{7,3},{8,12},{9,13},{10,... | collective-permute-start | bytes 1228808 | tf_op jit(solution)/shard_map/ppermute | solution.py:252
  19.5 0.0 collective-permute-start.5
  19.5 0.6 collective-permute-start.6
  20.1 0.1 collective-permute-start.7
  20.2 0.1 slice.46
  20.2 1.3 %collective-permute-done.6.refs_1_ = bf16[80,1280]{1,0:T(8,128)(2,1)S(1)} collective-permute-done((bf16[80,1280]{1,0:T(8,128)(2,1)S(1)}, bf16[80,1280]{1,0:T(8,128)(2,1)S(1)}, u32[]{:S(2)}, u32[]{:S(2)}) %collective-permute-start.6) | collective-permute-done | bytes 204832 | tf_op jit(solution)/shard_map/ppermute | solution.py:264
  21.5 0.1 collective-permute-start.12
  21.7 0.1 collective-permute-done.7.refs_2_
  21.8 0.3 collective-permute-start.13
  22.2 4.8 %collective-permute-done.4.even_ref.refs_3_.refs_6_ = bf16[1600,128]{1,0:T(8,128)(2,1)S(1)} collective-permute-done((bf16[1600,128]{1,0:T(8,128)(2,1)S(1)}, bf16[1600,128]{1,0:T(8,128)(2,1)S(1)}, u32[]{:S(2)}, u32[]{:S(2)}) %collective-permute-start.4) | collective-permute-done | bytes 409632 | tf_op jit(solution)/shard_map/ppermute | solution.py:252
  26.9 0.0 collective-permute-done.5.odd_ref.refs_4_.refs_7_
  26.9 0.4 shard_map.74
  27.4 0.0 copy-start.3
  27.4 1.8 %collective-permute-start.8 = (bf16[640,128]{1,0:T(8,128)(2,1)S(1)}, bf16[640,128]{1,0:T(8,128)(2,1)S(1)}, u32[]{:S(2)}, u32[]{:S(2)}) collective-permute-start(bf16[640,128]{1,0:T(8,128)(2,1)S(1)} %get-tuple-element.22.refs_0_), channel_id=1, source_target_pairs={{0,4},{1,5},{2,6},{3,7},{4,0},{5,1},{6,2},{7,3},{8,12},{9,13},{10,... | collective-permute-start | bytes 491528 | tf_op jit(solution)/shard_map/ppermute | solution.py:252
  29.2 0.0 collective-permute-start.9
  29.2 0.0 collective-permute-done.14.refs_7_
  29.2 1.5 %collective-permute-start.18 = (bf16[240,1280]{1,0:T(8,128)(2,1)S(1)}, bf16[240,1280]{1,0:T(8,128)(2,1)S(1)}, u32[]{:S(2)}, u32[]{:S(2)}) collective-permute-start(bf16[240,1280]{1,0:T(8,128)(2,1)S(1)} %get-tuple-element.27), channel_id=1, source_target_pairs={{0,2},{1,3},{2,0},{3,1},{4,6},{5,7},{6,4},{7,5},{8,10},{9,11},{10,... | collective-permute-start | bytes 1843208 | tf_op jit(solution)/shard_map/ppermute | solution.py:264
  30.7 0.0 collective-permute-done.13.refs_12_
  30.7 0.3 collective-permute-start.15
  31.0 1.7 %collective-permute-done.8.refs_8_.refs_1_ = bf16[640,128]{1,0:T(8,128)(2,1)S(1)} collective-permute-done((bf16[640,128]{1,0:T(8,128)(2,1)S(1)}, bf16[640,128]{1,0:T(8,128)(2,1)S(1)}, u32[]{:S(2)}, u32[]{:S(2)}) %collective-permute-start.8) | collective-permute-done | bytes 163872 | tf_op jit(solution)/shard_map/ppermute | solution.py:252
  32.8 0.0 collective-permute-start.16
  32.8 0.0 collective-permute-done.9.refs_9_.refs_2_
  32.8 0.5 collective-permute-start.17
  33.3 0.0 collective-permute-done.12.refs_11_
  33.3 1.8 %collective-permute-start.10 = (bf16[320,128]{1,0:T(8,128)(2,1)S(1)}, bf16[320,128]{1,0:T(8,128)(2,1)S(1)}, u32[]{:S(2)}, u32[]{:S(2)}) collective-permute-start(bf16[320,128]{1,0:T(8,128)(2,1)S(1)} %slice.44), channel_id=1, source_target_pairs={{0,4},{1,5},{2,6},{3,7},{4,0},{5,1},{6,2},{7,3},{8,12},{9,13},{10,... | collective-permute-start | bytes 245768 | tf_op jit(solution)/shard_map/ppermute | solution.py:252
  35.1 0.0 collective-permute-done.15.refs_8_
  35.1 0.0 collective-permute-start.11
  35.1 0.0 copy-done.3
  35.1 4.0 %shard_map.76 = (bf16[1280,384]{1,0:T(8,128)(2,1)S(1)}, f32[128,1280]{1,0:T(8,128)S(1)}) custom-call(s32[4,4]{1,0:T(4,128)S(1)} %copy-done.3, bf16[1280,128]{1,0:T(8,128)(2,1)S(1)} %get-tuple-element.20.refs_0_, bf16[1600,128]{1,0:T(8,128)(2,1)S(1)} %get-tuple-element.19.refs_1_, bf16[1600,128]{1,0:T(8,128)(2,1)S(1)} %get-tuple-element.18.refs_2_.refs_5_, ...), custom_call_target="tpu_custom_call" | custom-call | flops 1000 | bytes 1000 | tf_op jit(solution)/shard_map/pallas_call | solution.py:231
  39.1 0.0 collective-permute-done.16.refs_9_
  39.1 0.0 collective-permute-done.17.refs_10_
  39.1 0.0 collective-permute-done.10.refs_3_
  39.1 0.0 collective-permute-done.11.refs_4_
  39.1 2.6 %shard_map.77.refs_6_ = f32[128,1280]{1,0:T(8,128)S(1)} custom-call(s32[4,4]{1,0:T(4,128)S(1)} %copy-done.3, bf16[640,128]{1,0:T(8,128)(2,1)S(1)} %get-tuple-element.22.refs_0_, bf16[640,128]{1,0:T(8,128)(2,1)S(1)} %collective-permute-done.8.refs_8_.refs_1_, bf16[640,128]{1,0:T(8,128)(2,1)S(1)} %collective-permute-done.9.refs_9_.refs_2_, ...), custom_call_target="tpu_custom_call" | custom-call | flops 1000 | bytes 1000 | tf_op jit(solution)/shard_map/pallas_call | solution.py:231
  41.7 3.7 %collective-permute-done.18.refs_7_ = bf16[240,1280]{1,0:T(8,128)(2,1)S(1)} collective-permute-done((bf16[240,1280]{1,0:T(8,128)(2,1)S(1)}, bf16[240,1280]{1,0:T(8,128)(2,1)S(1)}, u32[]{:S(2)}, u32[]{:S(2)}) %collective-permute-start.18) | collective-permute-done | bytes 614432 | tf_op jit(solution)/shard_map/ppermute | solution.py:264
  45.5 0.0 collective-permute-start.19
  45.5 2.1 %shard_map.78.refs_6_ = f32[128,1280]{1,0:T(8,128)S(1)} custom-call(s32[4,4]{1,0:T(4,128)S(1)} %copy-done.3, bf16[640,128]{1,0:T(8,128)(2,1)S(1)} %get-tuple-element.22.refs_0_, bf16[640,128]{1,0:T(8,128)(2,1)S(1)} %collective-permute-done.8.refs_8_.refs_1_, bf16[640,128]{1,0:T(8,128)(2,1)S(1)} %collective-permute-done.9.refs_9_.refs_2_, ...), custom_call_target="tpu_custom_call" | custom-call | flops 1000 | bytes 1000 | tf_op jit(solution)/shard_map/pallas_call | solution.py:231
  47.6 0.0 collective-permute-done.19.refs_7_
  47.6 2.2 %shard_map.79 = bf16[128,1280]{1,0:T(8,128)(2,1)S(1)} custom-call(s32[4,4]{1,0:T(4,128)S(1)} %copy-done.3, bf16[640,128]{1,0:T(8,128)(2,1)S(1)} %get-tuple-element.22.refs_0_, bf16[640,128]{1,0:T(8,128)(2,1)S(1)} %collective-permute-done.8.refs_8_.refs_1_, bf16[640,128]{1,0:T(8,128)(2,1)S(1)} %collective-permute-done.9.refs_9_.refs_2_, ...), custom_call_target="tpu_custom_call" | custom-call | flops 1000 | bytes 1000 | tf_op jit(solution)/shard_map/pallas_call | solution.py:231
  49.8 1.6 %collective-permute-start.20 = (bf16[128,1280]{1,0:T(8,128)(2,1)S(1)}, bf16[128,1280]{1,0:T(8,128)(2,1)S(1)}, u32[]{:S(2)}, u32[]{:S(2)}) collective-permute-start(bf16[128,1280]{1,0:T(8,128)(2,1)S(1)} %shard_map.79), channel_id=1, source_target_pairs={{0,16},{16,0},{1,17},{17,1},{2,18},{18,2},{3,19},{19,3},{4,20},{20... | collective-permute-start | bytes 983048 | tf_op jit(solution)/shard_map/ppermute | solution.py:349
  51.4 8.6 %collective-permute-done.20 = bf16[128,1280]{1,0:T(8,128)(2,1)S(1)} collective-permute-done((bf16[128,1280]{1,0:T(8,128)(2,1)S(1)}, bf16[128,1280]{1,0:T(8,128)(2,1)S(1)}, u32[]{:S(2)}, u32[]{:S(2)}) %collective-permute-start.20) | collective-permute-done | bytes 327712 | tf_op jit(solution)/shard_map/ppermute | solution.py:349
  60.0 0.7 %copy.9 = bf16[1,1,128,1280]{3,2,1,0:T(8,128)(2,1)} copy(bf16[1,1,128,1280]{3,2,1,0:T(8,128)(2,1)S(1)} %bitcast.25) | data formatting | bytes 655360
  (5 shorter events, 0.1 us)
Async XLA Ops:
  0.0 15.5 %collective-permute-start.1 = (bf16[128,1280]{1,0:T(8,128)(2,1)}, bf16[128,1280]{1,0:T(8,128)(2,1)S(1)}, u32[]{:S(2)}, u32[]{:S(2)}) collective-permute-start(bf16[128,1280]{1,0:T(8,128)(2,1)} %bitcast.13), channel_id=1, source_target_pairs={{0,4},{1,5},{2,6},{3,7},{4,0},{5,1},{6,2},{7,3},{8,12},{9,13},{10,... | collective-permute-start | bytes 983048 | tf_op jit(solution)/shard_map/ppermute | solution.py:252
  3.0 12.5 %collective-permute-start.2 = (bf16[128,1280]{1,0:T(8,128)(2,1)}, bf16[128,1280]{1,0:T(8,128)(2,1)S(1)}, u32[]{:S(2)}, u32[]{:S(2)}) collective-permute-start(bf16[128,1280]{1,0:T(8,128)(2,1)} %bitcast.14), channel_id=1, source_target_pairs={{0,1},{1,0},{2,3},{3,2},{4,8},{5,9},{6,10},{7,11},{8,4},{9,5},{10,... | collective-permute-start | bytes 983048 | tf_op jit(solution)/shard_map/ppermute | solution.py:252
  3.0 12.5 %collective-permute-start = (bf16[160,1280]{1,0:T(8,128)(2,1)}, bf16[160,1280]{1,0:T(8,128)(2,1)S(1)}, u32[]{:S(2)}, u32[]{:S(2)}) collective-permute-start(bf16[160,1280]{1,0:T(8,128)(2,1)} %bitcast.19), channel_id=1, source_target_pairs={{0,2},{1,3},{2,0},{3,1},{4,6},{5,7},{6,4},{7,5},{8,10},{9,11},{10,... | collective-permute-start | bytes 1228808 | tf_op jit(solution)/shard_map/ppermute | solution.py:264
  4.5 11.0 %collective-permute-start.3 = (bf16[160,1280]{1,0:T(8,128)(2,1)}, bf16[160,1280]{1,0:T(8,128)(2,1)S(1)}, u32[]{:S(2)}, u32[]{:S(2)}) collective-permute-start(bf16[160,1280]{1,0:T(8,128)(2,1)} %bitcast.20), channel_id=1, source_target_pairs={{0,1},{1,0},{2,3},{3,2},{4,5},{5,4},{6,7},{7,6},{8,9},{9,8},{10,11... | collective-permute-start | bytes 1228808 | tf_op jit(solution)/shard_map/ppermute | solution.py:264
  6.2 9.4 %copy-start = (bf16[1,1,128,1280]{3,2,1,0:T(8,128)(2,1)S(1)}, bf16[1,1,128,1280]{3,2,1,0:T(8,128)(2,1)}, u32[]{:S(2)}) copy-start(bf16[1,1,128,1280]{3,2,1,0:T(8,128)(2,1)} %param.7) | copy-start | bytes 983044
  6.2 9.4 %copy-start.1 = (bf16[1,1,128,1280]{3,2,1,0:T(8,128)(2,1)S(1)}, bf16[1,1,128,1280]{3,2,1,0:T(8,128)(2,1)}, u32[]{:S(2)}) copy-start(bf16[1,1,128,1280]{3,2,1,0:T(8,128)(2,1)} %param.8) | copy-start | bytes 983044
  6.2 9.3 %copy-start.2 = (bf16[1,160,1280]{2,1,0:T(8,128)(2,1)S(1)}, bf16[1,160,1280]{2,1,0:T(8,128)(2,1)}, u32[]{:S(2)}) copy-start(bf16[1,160,1280]{2,1,0:T(8,128)(2,1)} %param.13) | copy-start | bytes 1228804
  6.3 22.9 %collective-permute-start.14 = (bf16[240,1280]{1,0:T(8,128)(2,1)S(1)}, bf16[240,1280]{1,0:T(8,128)(2,1)S(1)}, u32[]{:S(2)}, u32[]{:S(2)}) collective-permute-start(bf16[240,1280]{1,0:T(8,128)(2,1)S(1)} %get-tuple-element.30), channel_id=1, source_target_pairs={{0,2},{1,3},{2,0},{3,1},{4,6},{5,7},{6,4},{7,5},{8,10},{9,11},{10,... | collective-permute-start | bytes 1843208 | tf_op jit(solution)/shard_map/ppermute | solution.py:264
  16.1 10.8 %collective-permute-start.4 = (bf16[1600,128]{1,0:T(8,128)(2,1)S(1)}, bf16[1600,128]{1,0:T(8,128)(2,1)S(1)}, u32[]{:S(2)}, u32[]{:S(2)}) collective-permute-start(bf16[1600,128]{1,0:T(8,128)(2,1)S(1)} %get-tuple-element.18.refs_2_.refs_5_), channel_id=1, source_target_pairs={{0,4},{1,5},{2,6},{3,7},{4,0},{5,1},{6,2},{7,3},{8,12},{9,13},{10,... | collective-permute-start | bytes 1228808 | tf_op jit(solution)/shard_map/ppermute | solution.py:252
  19.5 7.4 %collective-permute-start.5 = (bf16[1600,128]{1,0:T(8,128)(2,1)S(1)}, bf16[1600,128]{1,0:T(8,128)(2,1)S(1)}, u32[]{:S(2)}, u32[]{:S(2)}) collective-permute-start(bf16[1600,128]{1,0:T(8,128)(2,1)S(1)} %get-tuple-element.19.refs_1_), channel_id=1, source_target_pairs={{0,1},{1,0},{2,3},{3,2},{4,8},{5,9},{6,10},{7,11},{8,4},{9,5},{10,... | collective-permute-start | bytes 1228808 | tf_op jit(solution)/shard_map/ppermute | solution.py:252
  19.5 2.0 %collective-permute-start.6 = (bf16[80,1280]{1,0:T(8,128)(2,1)S(1)}, bf16[80,1280]{1,0:T(8,128)(2,1)S(1)}, u32[]{:S(2)}, u32[]{:S(2)}) collective-permute-start(bf16[80,1280]{1,0:T(8,128)(2,1)S(1)} %get-tuple-element.35), channel_id=1, source_target_pairs={{0,1},{1,0},{2,3},{3,2},{4,5},{5,4},{6,7},{7,6},{8,9},{9,8},{10,11... | collective-permute-start | bytes 614408 | tf_op jit(solution)/shard_map/ppermute | solution.py:264
  20.1 1.7 %collective-permute-start.7 = (bf16[80,1280]{1,0:T(8,128)(2,1)S(1)}, bf16[80,1280]{1,0:T(8,128)(2,1)S(1)}, u32[]{:S(2)}, u32[]{:S(2)}) collective-permute-start(bf16[80,1280]{1,0:T(8,128)(2,1)S(1)} %get-tuple-element.34), channel_id=1, source_target_pairs={{0,1},{1,0},{2,3},{3,2},{4,5},{5,4},{6,7},{7,6},{8,9},{9,8},{10,11... | collective-permute-start | bytes 614408 | tf_op jit(solution)/shard_map/ppermute | solution.py:264
  21.5 11.7 %collective-permute-start.12 = (bf16[320,1280]{1,0:T(8,128)(2,1)S(1)}, bf16[320,1280]{1,0:T(8,128)(2,1)S(1)}, u32[]{:S(2)}, u32[]{:S(2)}) collective-permute-start(bf16[320,1280]{1,0:T(8,128)(2,1)S(1)} %slice.46), channel_id=1, source_target_pairs={{0,1},{1,0},{2,3},{3,2},{4,5},{5,4},{6,7},{7,6},{8,9},{9,8},{10,11... | collective-permute-start | bytes 2457608 | tf_op jit(solution)/shard_map/ppermute | solution.py:264
  21.8 8.9 %collective-permute-start.13 = (bf16[160,1280]{1,0:T(8,128)(2,1)S(1)}, bf16[160,1280]{1,0:T(8,128)(2,1)S(1)}, u32[]{:S(2)}, u32[]{:S(2)}) collective-permute-start(bf16[160,1280]{1,0:T(8,128)(2,1)S(1)} %slice.47), channel_id=1, source_target_pairs={{0,1},{1,0},{2,3},{3,2},{4,5},{5,4},{6,7},{7,6},{8,9},{9,8},{10,11... | collective-permute-start | bytes 1228808 | tf_op jit(solution)/shard_map/ppermute | solution.py:264
  27.4 7.8 %copy-start.3 = (s32[4,4]{1,0:T(4,128)S(1)}, s32[4,4]{1,0:T(4,128)}, u32[]{:S(2)}) copy-start(s32[4,4]{1,0:T(4,128)} %ids_ref.7) | copy-start | bytes 196
  27.4 5.4 %collective-permute-start.8 = (bf16[640,128]{1,0:T(8,128)(2,1)S(1)}, bf16[640,128]{1,0:T(8,128)(2,1)S(1)}, u32[]{:S(2)}, u32[]{:S(2)}) collective-permute-start(bf16[640,128]{1,0:T(8,128)(2,1)S(1)} %get-tuple-element.22.refs_0_), channel_id=1, source_target_pairs={{0,4},{1,5},{2,6},{3,7},{4,0},{5,1},{6,2},{7,3},{8,12},{9,13},{10,... | collective-permute-start | bytes 491528 | tf_op jit(solution)/shard_map/ppermute | solution.py:252
  29.2 3.6 %collective-permute-start.9 = (bf16[640,128]{1,0:T(8,128)(2,1)S(1)}, bf16[640,128]{1,0:T(8,128)(2,1)S(1)}, u32[]{:S(2)}, u32[]{:S(2)}) collective-permute-start(bf16[640,128]{1,0:T(8,128)(2,1)S(1)} %get-tuple-element.23), channel_id=1, source_target_pairs={{0,1},{1,0},{2,3},{3,2},{4,8},{5,9},{6,10},{7,11},{8,4},{9,5},{10,... | collective-permute-start | bytes 491528 | tf_op jit(solution)/shard_map/ppermute | solution.py:252
  29.2 16.3 %collective-permute-start.18 = (bf16[240,1280]{1,0:T(8,128)(2,1)S(1)}, bf16[240,1280]{1,0:T(8,128)(2,1)S(1)}, u32[]{:S(2)}, u32[]{:S(2)}) collective-permute-start(bf16[240,1280]{1,0:T(8,128)(2,1)S(1)} %get-tuple-element.27), channel_id=1, source_target_pairs={{0,2},{1,3},{2,0},{3,1},{4,6},{5,7},{6,4},{7,5},{8,10},{9,11},{10,... | collective-permute-start | bytes 1843208 | tf_op jit(solution)/shard_map/ppermute | solution.py:264
  30.7 4.4 %collective-permute-start.15 = (bf16[80,1280]{1,0:T(8,128)(2,1)S(1)}, bf16[80,1280]{1,0:T(8,128)(2,1)S(1)}, u32[]{:S(2)}, u32[]{:S(2)}) collective-permute-start(bf16[80,1280]{1,0:T(8,128)(2,1)S(1)} %get-tuple-element.33), channel_id=1, source_target_pairs={{0,1},{1,0},{2,3},{3,2},{4,5},{5,4},{6,7},{7,6},{8,9},{9,8},{10,11... | collective-permute-start | bytes 614408 | tf_op jit(solution)/shard_map/ppermute | solution.py:264
  32.8 6.3 %collective-permute-start.16 = (bf16[80,1280]{1,0:T(8,128)(2,1)S(1)}, bf16[80,1280]{1,0:T(8,128)(2,1)S(1)}, u32[]{:S(2)}, u32[]{:S(2)}) collective-permute-start(bf16[80,1280]{1,0:T(8,128)(2,1)S(1)} %get-tuple-element.32), channel_id=1, source_target_pairs={{0,1},{1,0},{2,3},{3,2},{4,5},{5,4},{6,7},{7,6},{8,9},{9,8},{10,11... | collective-permute-start | bytes 614408 | tf_op jit(solution)/shard_map/ppermute | solution.py:264
  32.8 6.3 %collective-permute-start.17 = (bf16[80,1280]{1,0:T(8,128)(2,1)S(1)}, bf16[80,1280]{1,0:T(8,128)(2,1)S(1)}, u32[]{:S(2)}, u32[]{:S(2)}) collective-permute-start(bf16[80,1280]{1,0:T(8,128)(2,1)S(1)} %get-tuple-element.31), channel_id=1, source_target_pairs={{0,1},{1,0},{2,3},{3,2},{4,5},{5,4},{6,7},{7,6},{8,9},{9,8},{10,11... | collective-permute-start | bytes 614408 | tf_op jit(solution)/shard_map/ppermute | solution.py:264
  33.3 5.8 %collective-permute-start.10 = (bf16[320,128]{1,0:T(8,128)(2,1)S(1)}, bf16[320,128]{1,0:T(8,128)(2,1)S(1)}, u32[]{:S(2)}, u32[]{:S(2)}) collective-permute-start(bf16[320,128]{1,0:T(8,128)(2,1)S(1)} %slice.44), channel_id=1, source_target_pairs={{0,4},{1,5},{2,6},{3,7},{4,0},{5,1},{6,2},{7,3},{8,12},{9,13},{10,... | collective-permute-start | bytes 245768 | tf_op jit(solution)/shard_map/ppermute | solution.py:252
  35.1 4.0 %collective-permute-start.11 = (bf16[320,128]{1,0:T(8,128)(2,1)S(1)}, bf16[320,128]{1,0:T(8,128)(2,1)S(1)}, u32[]{:S(2)}, u32[]{:S(2)}) collective-permute-start(bf16[320,128]{1,0:T(8,128)(2,1)S(1)} %slice.45), channel_id=1, source_target_pairs={{0,1},{1,0},{2,3},{3,2},{4,8},{5,9},{6,10},{7,11},{8,4},{9,5},{10,... | collective-permute-start | bytes 245768 | tf_op jit(solution)/shard_map/ppermute | solution.py:252
  45.5 2.1 %collective-permute-start.19 = (bf16[240,1280]{1,0:T(8,128)(2,1)S(1)}, bf16[240,1280]{1,0:T(8,128)(2,1)S(1)}, u32[]{:S(2)}, u32[]{:S(2)}) collective-permute-start(bf16[240,1280]{1,0:T(8,128)(2,1)S(1)} %collective-permute-done.18.refs_7_), channel_id=1, source_target_pairs={{0,1},{1,0},{2,3},{3,2},{4,5},{5,4},{6,7},{7,6},{8,9},{9,8},{10,11... | collective-permute-start | bytes 1843208 | tf_op jit(solution)/shard_map/ppermute | solution.py:264
  49.8 10.2 %collective-permute-start.20 = (bf16[128,1280]{1,0:T(8,128)(2,1)S(1)}, bf16[128,1280]{1,0:T(8,128)(2,1)S(1)}, u32[]{:S(2)}, u32[]{:S(2)}) collective-permute-start(bf16[128,1280]{1,0:T(8,128)(2,1)S(1)} %shard_map.79), channel_id=1, source_target_pairs={{0,16},{16,0},{1,17},{17,1},{2,18},{18,2},{3,19},{19,3},{4,20},{20... | collective-permute-start | bytes 983048 | tf_op jit(solution)/shard_map/ppermute | solution.py:349

commit v3 on v2

--- a/solution.py
+++ b/solution.py
@@ -278,7 +278,8 @@
     own_out = out_weight[0]
     far_out = dp_swap(own_out, 2)
     near_out = dp_swap(own_out, 1)
-    steps = [pair_steps(own_input, own_input)]
+    first = after(own_input, near_out)
+    steps = [pair_steps(first, first)]
     local = call(
         pack_kernel,
         [query_weight[0].T, key_weight[0].T, value_weight[0].T],
@@ -288,7 +289,8 @@
         scalars=False,
         space=pltpu.HBM,
     )
-    near = [dp_swap(part, 1) for part in (local[:NEAR_CUT], local[NEAR_CUT:])]
+    ready = after(local, far_out)
+    near = [dp_swap(part, 1) for part in (ready[:NEAR_CUT], ready[NEAR_CUT:])]
     far_last = dp_swap(local[QKV : 2 * QKV], 2)
 
     normed, near_grad, first_odd = call(
@@ -310,7 +312,7 @@
         scalars=False,
     )
     steps.append(pair_steps(to_odd, far_grad))
-    far_first = dp_swap(after(local[:QKV], far_last, far_grad), 2)
+    far_first = dp_swap(after(local[:QKV], far_grad), 2)
     thirds = after(far_last, far_grad)
     far_near_last = [dp_swap(thirds[at : at + HEAD_DIM], 1) for at in range(0, QKV, HEAD_DIM)]
     while len(steps) < count + 1:

time: 60.9 us -> 60.8 us (level)
  starting transfers between devices: 17.3 us -> 16.2 us
  waiting for transfers between devices: 28.9 us -> 30 us
    ppermute x8, waiting for transfers between devices: 6.51 us -> 9.49 us  [pair_swap(): return lax.ppermute(array, ('ctx', 'dp'), pairs)]
    ppermute x12, waiting for transfers between devices: 13.8 us -> 11.9 us  [dp_swap(): lax.ppermute(array, 'dp', [(i, i ^ by) for i in range(lax.axis_size('dp'))])]
    ppermute x8, starting transfers between devices: 10 us -> 8.18 us  [pair_swap(): return lax.ppermute(array, ('ctx', 'dp'), pairs)]
    ppermute x12, starting transfers between devices: 5.72 us -> 6.4 us  [dp_swap(): lax.ppermute(array, 'dp', [(i, i ^ by) for i in range(lax.axis_size('dp'))])]
  transfers between devices with their start and end apart: 21 -> 21, of which waited for: 7 -> 8; matrix products, arithmetic and copies ran while one was open for 0% -> 0% of each run, Pallas kernels for 18% -> 18%
where the time goes in v3:
time: 60.8 us; the launch traced here: 60.7 us
  waiting for transfers between devices  30 us (49%)
  starting transfers between devices  16.2 us (27%)
  Pallas kernels  13.4 us (22%)
  local copies, waits for them, and re-layouts  0.99 us (2%)
    pallas_call x7, Pallas kernels, call(): pl.pallas_call(kernel, out_shape=out_shape, in_specs=specs + [pl.BlockSpe...  13.4 us
    ppermute x12, waiting for transfers between devices, dp_swap(): lax.ppermute(array, 'dp', [(i, i ^ by) for i in range(lax.axis_size('dp'))])  11.9 us
    ppermute x8, waiting for transfers between devices, pair_swap(): return lax.ppermute(array, ('ctx', 'dp'), pairs)  9.49 us
    ppermute x1, waiting for transfers between devices, body(): lax.ppermute(result, 'section', [(i, (i - 1) % sections) for i in range(s...  8.6 us
    ppermute x8, starting transfers between devices, pair_swap(): return lax.ppermute(array, ('ctx', 'dp'), pairs)  8.18 us
    ppermute x12, starting transfers between devices, dp_swap(): lax.ppermute(array, 'dp', [(i, i ^ by) for i in range(lax.axis_size('dp'))])  6.4 us
    ppermute x1, starting transfers between devices, body(): lax.ppermute(result, 'section', [(i, (i - 1) % sections) for i in range(s...  1.58 us
  transfers between devices with their start and end apart: 21, of which 8 were waited for; matrix products, arithmetic and copies ran while one was open for 0% of the time, Pallas kernels for 18%

profile of v3, /device:TPU:0, one launch (start us, length us, event | category | flops | bytes accessed | tf_op | source)
XLA Modules:
  0.0 60.7 jit_solution(8442775553494901740)
XLA Ops:
  0.0 0.5 collective-permute-start.1
  0.5 2.5 %collective-permute-start = (bf16[160,1280]{1,0:T(8,128)(2,1)}, bf16[160,1280]{1,0:T(8,128)(2,1)S(1)}, u32[]{:S(2)}, u32[]{:S(2)}) collective-permute-start(bf16[160,1280]{1,0:T(8,128)(2,1)} %bitcast.20), channel_id=1, source_target_pairs={{0,2},{1,3},{2,0},{3,1},{4,6},{5,7},{6,4},{7,5},{8,10},{9,11},{10,... | collective-permute-start | bytes 1228808 | tf_op jit(solution)/shard_map/ppermute | solution.py:264
  2.9 0.0 copy-start
  2.9 1.4 %shard_map.75.refs_10_ = bf16[480,1280]{1,0:T(8,128)(2,1)S(1)} custom-call(bf16[160,1280]{1,0:T(8,128)(2,1)} %bitcast.22, bf16[160,1280]{1,0:T(8,128)(2,1)} %bitcast.23, bf16[160,1280]{1,0:T(8,128)(2,1)} %bitcast.24), custom_call_target="tpu_custom_call" | custom-call | flops 1000 | bytes 1000 | tf_op jit(solution)/shard_map/pallas_call | solution.py:231
  4.4 0.0 collective-permute-done.1.refs_1_
  4.4 0.0 copy-done
  4.4 0.0 copy-start.1
  4.4 0.0 copy-start.2
  4.4 1.6 %collective-permute-start.2 = (bf16[128,1280]{1,0:T(8,128)(2,1)S(1)}, bf16[128,1280]{1,0:T(8,128)(2,1)S(1)}, u32[]{:S(2)}, u32[]{:S(2)}) collective-permute-start(bf16[128,1280]{1,0:T(8,128)(2,1)S(1)} %bitcast.13), channel_id=1, source_target_pairs={{0,4},{1,5},{2,6},{3,7},{4,0},{5,1},{6,2},{7,3},{8,12},{9,13},{10,... | collective-permute-start | bytes 983048 | tf_op jit(solution)/shard_map/ppermute | solution.py:252
  6.1 0.0 collective-permute-start.3
  6.1 0.1 fusion
  6.2 0.6 collective-permute-start.14
  6.8 6.7 %collective-permute-done.refs_0_ = bf16[160,1280]{1,0:T(8,128)(2,1)S(1)} collective-permute-done((bf16[160,1280]{1,0:T(8,128)(2,1)}, bf16[160,1280]{1,0:T(8,128)(2,1)S(1)}, u32[]{:S(2)}, u32[]{:S(2)}) %collective-permute-start) | collective-permute-done | bytes 409632 | tf_op jit(solution)/shard_map/ppermute | solution.py:264
  13.5 0.9 %collective-permute-done.2.even_ref = bf16[128,1280]{1,0:T(8,128)(2,1)S(1)} collective-permute-done((bf16[128,1280]{1,0:T(8,128)(2,1)S(1)}, bf16[128,1280]{1,0:T(8,128)(2,1)S(1)}, u32[]{:S(2)}, u32[]{:S(2)}) %collective-permute-start.2) | collective-permute-done | bytes 327712 | tf_op jit(solution)/shard_map/ppermute | solution.py:252
  14.4 0.0 collective-permute-done.3.odd_ref
  14.4 0.0 copy-done.1
  14.4 0.0 copy-done.2
  14.4 0.6 shard_map.73
  15.0 2.8 %collective-permute-start.4 = (bf16[1600,128]{1,0:T(8,128)(2,1)S(1)}, bf16[1600,128]{1,0:T(8,128)(2,1)S(1)}, u32[]{:S(2)}, u32[]{:S(2)}) collective-permute-start(bf16[1600,128]{1,0:T(8,128)(2,1)S(1)} %get-tuple-element.21.refs_2_.refs_5_), channel_id=1, source_target_pairs={{0,4},{1,5},{2,6},{3,7},{4,0},{5,1},{6,2},{7,3},{8,12},{9,13},{10,... | collective-permute-start | bytes 1228808 | tf_op jit(solution)/shard_map/ppermute | solution.py:252
  17.7 0.0 collective-permute-start.5
  17.8 0.6 collective-permute-start.6
  18.3 0.1 collective-permute-start.7
  18.4 0.1 slice.37
  18.5 1.3 %collective-permute-done.6.refs_1_ = bf16[80,1280]{1,0:T(8,128)(2,1)S(1)} collective-permute-done((bf16[80,1280]{1,0:T(8,128)(2,1)S(1)}, bf16[80,1280]{1,0:T(8,128)(2,1)S(1)}, u32[]{:S(2)}, u32[]{:S(2)}) %collective-permute-start.6) | collective-permute-done | bytes 204832 | tf_op jit(solution)/shard_map/ppermute | solution.py:264
  19.8 0.1 collective-permute-start.12
  19.9 0.1 collective-permute-done.7.refs_2_
  20.1 0.3 collective-permute-start.13
  20.4 6.4 %collective-permute-done.4.even_ref.refs_3_.refs_6_ = bf16[1600,128]{1,0:T(8,128)(2,1)S(1)} collective-permute-done((bf16[1600,128]{1,0:T(8,128)(2,1)S(1)}, bf16[1600,128]{1,0:T(8,128)(2,1)S(1)}, u32[]{:S(2)}, u32[]{:S(2)}) %collective-permute-start.4) | collective-permute-done | bytes 409632 | tf_op jit(solution)/shard_map/ppermute | solution.py:252
  26.8 0.0 collective-permute-done.5.odd_ref.refs_4_.refs_7_
  26.8 0.4 shard_map.74
  27.2 0.0 copy-start.3
  27.2 1.9 %collective-permute-start.8 = (bf16[640,128]{1,0:T(8,128)(2,1)S(1)}, bf16[640,128]{1,0:T(8,128)(2,1)S(1)}, u32[]{:S(2)}, u32[]{:S(2)}) collective-permute-start(bf16[640,128]{1,0:T(8,128)(2,1)S(1)} %get-tuple-element.25.refs_0_), channel_id=1, source_target_pairs={{0,4},{1,5},{2,6},{3,7},{4,0},{5,1},{6,2},{7,3},{8,12},{9,13},{10,... | collective-permute-start | bytes 491528 | tf_op jit(solution)/shard_map/ppermute | solution.py:252
  29.1 0.0 collective-permute-start.9
  29.1 0.0 collective-permute-done.14.refs_7_
  29.1 0.9 %collective-permute-start.18 = (bf16[240,1280]{1,0:T(8,128)(2,1)S(1)}, bf16[240,1280]{1,0:T(8,128)(2,1)S(1)}, u32[]{:S(2)}, u32[]{:S(2)}) collective-permute-start(bf16[240,1280]{1,0:T(8,128)(2,1)S(1)} %get-tuple-element.31), channel_id=1, source_target_pairs={{0,2},{1,3},{2,0},{3,1},{4,6},{5,7},{6,4},{7,5},{8,10},{9,11},{10,... | collective-permute-start | bytes 1843208 | tf_op jit(solution)/shard_map/ppermute | solution.py:264
  30.1 0.0 collective-permute-done.13.refs_12_
  30.1 0.3 collective-permute-start.15
  30.4 2.2 %collective-permute-done.8.refs_8_.refs_1_ = bf16[640,128]{1,0:T(8,128)(2,1)S(1)} collective-permute-done((bf16[640,128]{1,0:T(8,128)(2,1)S(1)}, bf16[640,128]{1,0:T(8,128)(2,1)S(1)}, u32[]{:S(2)}, u32[]{:S(2)}) %collective-permute-start.8) | collective-permute-done | bytes 163872 | tf_op jit(solution)/shard_map/ppermute | solution.py:252
  32.6 0.0 collective-permute-start.16
  32.6 0.0 collective-permute-done.9.refs_9_.refs_2_
  32.6 0.5 collective-permute-start.17
  33.1 0.0 collective-permute-done.12.refs_11_
  33.1 1.9 %collective-permute-start.10 = (bf16[320,128]{1,0:T(8,128)(2,1)S(1)}, bf16[320,128]{1,0:T(8,128)(2,1)S(1)}, u32[]{:S(2)}, u32[]{:S(2)}) collective-permute-start(bf16[320,128]{1,0:T(8,128)(2,1)S(1)} %slice.44), channel_id=1, source_target_pairs={{0,4},{1,5},{2,6},{3,7},{4,0},{5,1},{6,2},{7,3},{8,12},{9,13},{10,... | collective-permute-start | bytes 245768 | tf_op jit(solution)/shard_map/ppermute | solution.py:252
  35.0 0.0 collective-permute-done.15.refs_8_
  35.0 0.0 collective-permute-start.11
  35.0 0.0 copy-done.3
  35.0 4.0 %shard_map.76 = (bf16[1280,384]{1,0:T(8,128)(2,1)S(1)}, f32[128,1280]{1,0:T(8,128)S(1)}) custom-call(s32[4,4]{1,0:T(4,128)S(1)} %copy-done.3, bf16[1280,128]{1,0:T(8,128)(2,1)S(1)} %get-tuple-element.23.refs_0_, bf16[1600,128]{1,0:T(8,128)(2,1)S(1)} %get-tuple-element.22.refs_1_, bf16[1600,128]{1,0:T(8,128)(2,1)S(1)} %get-tuple-element.21.refs_2_.refs_5_, ...), custom_call_target="tpu_custom_call" | custom-call | flops 1000 | bytes 1000 | tf_op jit(solution)/shard_map/pallas_call | solution.py:231
  39.0 0.0 collective-permute-done.16.refs_9_
  39.0 0.0 collective-permute-done.17.refs_10_
  39.0 0.0 collective-permute-done.10.refs_3_
  39.0 0.0 collective-permute-done.11.refs_4_
  39.0 2.6 %shard_map.77.refs_6_ = f32[128,1280]{1,0:T(8,128)S(1)} custom-call(s32[4,4]{1,0:T(4,128)S(1)} %copy-done.3, bf16[640,128]{1,0:T(8,128)(2,1)S(1)} %get-tuple-element.25.refs_0_, bf16[640,128]{1,0:T(8,128)(2,1)S(1)} %collective-permute-done.8.refs_8_.refs_1_, bf16[640,128]{1,0:T(8,128)(2,1)S(1)} %collective-permute-done.9.refs_9_.refs_2_, ...), custom_call_target="tpu_custom_call" | custom-call | flops 1000 | bytes 1000 | tf_op jit(solution)/shard_map/pallas_call | solution.py:231
  41.6 3.7 %collective-permute-done.18.refs_7_ = bf16[240,1280]{1,0:T(8,128)(2,1)S(1)} collective-permute-done((bf16[240,1280]{1,0:T(8,128)(2,1)S(1)}, bf16[240,1280]{1,0:T(8,128)(2,1)S(1)}, u32[]{:S(2)}, u32[]{:S(2)}) %collective-permute-start.18) | collective-permute-done | bytes 614432 | tf_op jit(solution)/shard_map/ppermute | solution.py:264
  45.4 0.0 collective-permute-start.19
  45.4 2.1 %shard_map.78.refs_6_ = f32[128,1280]{1,0:T(8,128)S(1)} custom-call(s32[4,4]{1,0:T(4,128)S(1)} %copy-done.3, bf16[640,128]{1,0:T(8,128)(2,1)S(1)} %get-tuple-element.25.refs_0_, bf16[640,128]{1,0:T(8,128)(2,1)S(1)} %collective-permute-done.8.refs_8_.refs_1_, bf16[640,128]{1,0:T(8,128)(2,1)S(1)} %collective-permute-done.9.refs_9_.refs_2_, ...), custom_call_target="tpu_custom_call" | custom-call | flops 1000 | bytes 1000 | tf_op jit(solution)/shard_map/pallas_call | solution.py:231
  47.5 0.0 collective-permute-done.19.refs_7_
  47.5 2.2 %shard_map.79 = bf16[128,1280]{1,0:T(8,128)(2,1)S(1)} custom-call(s32[4,4]{1,0:T(4,128)S(1)} %copy-done.3, bf16[640,128]{1,0:T(8,128)(2,1)S(1)} %get-tuple-element.25.refs_0_, bf16[640,128]{1,0:T(8,128)(2,1)S(1)} %collective-permute-done.8.refs_8_.refs_1_, bf16[640,128]{1,0:T(8,128)(2,1)S(1)} %collective-permute-done.9.refs_9_.refs_2_, ...), custom_call_target="tpu_custom_call" | custom-call | flops 1000 | bytes 1000 | tf_op jit(solution)/shard_map/pallas_call | solution.py:231
  49.7 1.6 %collective-permute-start.20 = (bf16[128,1280]{1,0:T(8,128)(2,1)S(1)}, bf16[128,1280]{1,0:T(8,128)(2,1)S(1)}, u32[]{:S(2)}, u32[]{:S(2)}) collective-permute-start(bf16[128,1280]{1,0:T(8,128)(2,1)S(1)} %shard_map.79), channel_id=1, source_target_pairs={{0,16},{16,0},{1,17},{17,1},{2,18},{18,2},{3,19},{19,3},{4,20},{20... | collective-permute-start | bytes 983048 | tf_op jit(solution)/shard_map/ppermute | solution.py:351
  51.3 8.6 %collective-permute-done.20 = bf16[128,1280]{1,0:T(8,128)(2,1)S(1)} collective-permute-done((bf16[128,1280]{1,0:T(8,128)(2,1)S(1)}, bf16[128,1280]{1,0:T(8,128)(2,1)S(1)}, u32[]{:S(2)}, u32[]{:S(2)}) %collective-permute-start.20) | collective-permute-done | bytes 327712 | tf_op jit(solution)/shard_map/ppermute | solution.py:351
  59.9 0.7 %copy.9 = bf16[1,1,128,1280]{3,2,1,0:T(8,128)(2,1)} copy(bf16[1,1,128,1280]{3,2,1,0:T(8,128)(2,1)S(1)} %bitcast.25) | data formatting | bytes 655360
  (5 shorter events, 0.1 us)
Async XLA Ops:
  0.0 4.4 %collective-permute-start.1 = (bf16[160,1280]{1,0:T(8,128)(2,1)}, bf16[160,1280]{1,0:T(8,128)(2,1)S(1)}, u32[]{:S(2)}, u32[]{:S(2)}) collective-permute-start(bf16[160,1280]{1,0:T(8,128)(2,1)} %bitcast.19), channel_id=1, source_target_pairs={{0,1},{1,0},{2,3},{3,2},{4,5},{5,4},{6,7},{7,6},{8,9},{9,8},{10,11... | collective-permute-start | bytes 1228808 | tf_op jit(solution)/shard_map/ppermute | solution.py:264
  0.5 13.0 %collective-permute-start = (bf16[160,1280]{1,0:T(8,128)(2,1)}, bf16[160,1280]{1,0:T(8,128)(2,1)S(1)}, u32[]{:S(2)}, u32[]{:S(2)}) collective-permute-start(bf16[160,1280]{1,0:T(8,128)(2,1)} %bitcast.20), channel_id=1, source_target_pairs={{0,2},{1,3},{2,0},{3,1},{4,6},{5,7},{6,4},{7,5},{8,10},{9,11},{10,... | collective-permute-start | bytes 1228808 | tf_op jit(solution)/shard_map/ppermute | solution.py:264
  2.9 1.5 %copy-start = (bf16[1,1,128,1280]{3,2,1,0:T(8,128)(2,1)S(1)}, bf16[1,1,128,1280]{3,2,1,0:T(8,128)(2,1)}, u32[]{:S(2)}) copy-start(bf16[1,1,128,1280]{3,2,1,0:T(8,128)(2,1)} %param.7) | copy-start | bytes 983044
  4.4 9.9 %copy-start.1 = (bf16[1,1,128,1280]{3,2,1,0:T(8,128)(2,1)S(1)}, bf16[1,1,128,1280]{3,2,1,0:T(8,128)(2,1)}, u32[]{:S(2)}) copy-start(bf16[1,1,128,1280]{3,2,1,0:T(8,128)(2,1)} %param.8) | copy-start | bytes 983044
  4.4 9.9 %copy-start.2 = (bf16[1,160,1280]{2,1,0:T(8,128)(2,1)S(1)}, bf16[1,160,1280]{2,1,0:T(8,128)(2,1)}, u32[]{:S(2)}) copy-start(bf16[1,160,1280]{2,1,0:T(8,128)(2,1)} %param.13) | copy-start | bytes 1228804
  4.4 9.9 %collective-permute-start.2 = (bf16[128,1280]{1,0:T(8,128)(2,1)S(1)}, bf16[128,1280]{1,0:T(8,128)(2,1)S(1)}, u32[]{:S(2)}, u32[]{:S(2)}) collective-permute-start(bf16[128,1280]{1,0:T(8,128)(2,1)S(1)} %bitcast.13), channel_id=1, source_target_pairs={{0,4},{1,5},{2,6},{3,7},{4,0},{5,1},{6,2},{7,3},{8,12},{9,13},{10,... | collective-permute-start | bytes 983048 | tf_op jit(solution)/shard_map/ppermute | solution.py:252
  6.1 8.3 %collective-permute-start.3 = (bf16[128,1280]{1,0:T(8,128)(2,1)S(1)}, bf16[128,1280]{1,0:T(8,128)(2,1)S(1)}, u32[]{:S(2)}, u32[]{:S(2)}) collective-permute-start(bf16[128,1280]{1,0:T(8,128)(2,1)S(1)} %bitcast.14), channel_id=1, source_target_pairs={{0,1},{1,0},{2,3},{3,2},{4,8},{5,9},{6,10},{7,11},{8,4},{9,5},{10,... | collective-permute-start | bytes 983048 | tf_op jit(solution)/shard_map/ppermute | solution.py:252
  6.2 22.9 %collective-permute-start.14 = (bf16[240,1280]{1,0:T(8,128)(2,1)S(1)}, bf16[240,1280]{1,0:T(8,128)(2,1)S(1)}, u32[]{:S(2)}, u32[]{:S(2)}) collective-permute-start(bf16[240,1280]{1,0:T(8,128)(2,1)S(1)} %get-tuple-element.34), channel_id=1, source_target_pairs={{0,2},{1,3},{2,0},{3,1},{4,6},{5,7},{6,4},{7,5},{8,10},{9,11},{10,... | collective-permute-start | bytes 1843208 | tf_op jit(solution)/shard_map/ppermute | solution.py:264
  15.0 11.8 %collective-permute-start.4 = (bf16[1600,128]{1,0:T(8,128)(2,1)S(1)}, bf16[1600,128]{1,0:T(8,128)(2,1)S(1)}, u32[]{:S(2)}, u32[]{:S(2)}) collective-permute-start(bf16[1600,128]{1,0:T(8,128)(2,1)S(1)} %get-tuple-element.21.refs_2_.refs_5_), channel_id=1, source_target_pairs={{0,4},{1,5},{2,6},{3,7},{4,0},{5,1},{6,2},{7,3},{8,12},{9,13},{10,... | collective-permute-start | bytes 1228808 | tf_op jit(solution)/shard_map/ppermute | solution.py:252
  17.7 9.0 %collective-permute-start.5 = (bf16[1600,128]{1,0:T(8,128)(2,1)S(1)}, bf16[1600,128]{1,0:T(8,128)(2,1)S(1)}, u32[]{:S(2)}, u32[]{:S(2)}) collective-permute-start(bf16[1600,128]{1,0:T(8,128)(2,1)S(1)} %get-tuple-element.22.refs_1_), channel_id=1, source_target_pairs={{0,1},{1,0},{2,3},{3,2},{4,8},{5,9},{6,10},{7,11},{8,4},{9,5},{10,... | collective-permute-start | bytes 1228808 | tf_op jit(solution)/shard_map/ppermute | solution.py:252
  17.8 2.0 %collective-permute-start.6 = (bf16[80,1280]{1,0:T(8,128)(2,1)S(1)}, bf16[80,1280]{1,0:T(8,128)(2,1)S(1)}, u32[]{:S(2)}, u32[]{:S(2)}) collective-permute-start(bf16[80,1280]{1,0:T(8,128)(2,1)S(1)} %get-tuple-element.39), channel_id=1, source_target_pairs={{0,1},{1,0},{2,3},{3,2},{4,5},{5,4},{6,7},{7,6},{8,9},{9,8},{10,11... | collective-permute-start | bytes 614408 | tf_op jit(solution)/shard_map/ppermute | solution.py:264
  18.3 1.7 %collective-permute-start.7 = (bf16[80,1280]{1,0:T(8,128)(2,1)S(1)}, bf16[80,1280]{1,0:T(8,128)(2,1)S(1)}, u32[]{:S(2)}, u32[]{:S(2)}) collective-permute-start(bf16[80,1280]{1,0:T(8,128)(2,1)S(1)} %get-tuple-element.38), channel_id=1, source_target_pairs={{0,1},{1,0},{2,3},{3,2},{4,5},{5,4},{6,7},{7,6},{8,9},{9,8},{10,11... | collective-permute-start | bytes 614408 | tf_op jit(solution)/shard_map/ppermute | solution.py:264
  19.8 13.4 %collective-permute-start.12 = (bf16[320,1280]{1,0:T(8,128)(2,1)S(1)}, bf16[320,1280]{1,0:T(8,128)(2,1)S(1)}, u32[]{:S(2)}, u32[]{:S(2)}) collective-permute-start(bf16[320,1280]{1,0:T(8,128)(2,1)S(1)} %slice.37), channel_id=1, source_target_pairs={{0,1},{1,0},{2,3},{3,2},{4,5},{5,4},{6,7},{7,6},{8,9},{9,8},{10,11... | collective-permute-start | bytes 2457608 | tf_op jit(solution)/shard_map/ppermute | solution.py:264
  20.1 10.0 %collective-permute-start.13 = (bf16[160,1280]{1,0:T(8,128)(2,1)S(1)}, bf16[160,1280]{1,0:T(8,128)(2,1)S(1)}, u32[]{:S(2)}, u32[]{:S(2)}) collective-permute-start(bf16[160,1280]{1,0:T(8,128)(2,1)S(1)} %slice.38), channel_id=1, source_target_pairs={{0,1},{1,0},{2,3},{3,2},{4,5},{5,4},{6,7},{7,6},{8,9},{9,8},{10,11... | collective-permute-start | bytes 1228808 | tf_op jit(solution)/shard_map/ppermute | solution.py:264
  27.2 7.8 %copy-start.3 = (s32[4,4]{1,0:T(4,128)S(1)}, s32[4,4]{1,0:T(4,128)}, u32[]{:S(2)}) copy-start(s32[4,4]{1,0:T(4,128)} %ids_ref.7) | copy-start | bytes 196
  27.2 5.4 %collective-permute-start.8 = (bf16[640,128]{1,0:T(8,128)(2,1)S(1)}, bf16[640,128]{1,0:T(8,128)(2,1)S(1)}, u32[]{:S(2)}, u32[]{:S(2)}) collective-permute-start(bf16[640,128]{1,0:T(8,128)(2,1)S(1)} %get-tuple-element.25.refs_0_), channel_id=1, source_target_pairs={{0,4},{1,5},{2,6},{3,7},{4,0},{5,1},{6,2},{7,3},{8,12},{9,13},{10,... | collective-permute-start | bytes 491528 | tf_op jit(solution)/shard_map/ppermute | solution.py:252
  29.1 3.5 %collective-permute-start.9 = (bf16[640,128]{1,0:T(8,128)(2,1)S(1)}, bf16[640,128]{1,0:T(8,128)(2,1)S(1)}, u32[]{:S(2)}, u32[]{:S(2)}) collective-permute-start(bf16[640,128]{1,0:T(8,128)(2,1)S(1)} %get-tuple-element.26), channel_id=1, source_target_pairs={{0,1},{1,0},{2,3},{3,2},{4,8},{5,9},{6,10},{7,11},{8,4},{9,5},{10,... | collective-permute-start | bytes 491528 | tf_op jit(solution)/shard_map/ppermute | solution.py:252
  29.1 16.3 %collective-permute-start.18 = (bf16[240,1280]{1,0:T(8,128)(2,1)S(1)}, bf16[240,1280]{1,0:T(8,128)(2,1)S(1)}, u32[]{:S(2)}, u32[]{:S(2)}) collective-permute-start(bf16[240,1280]{1,0:T(8,128)(2,1)S(1)} %get-tuple-element.31), channel_id=1, source_target_pairs={{0,2},{1,3},{2,0},{3,1},{4,6},{5,7},{6,4},{7,5},{8,10},{9,11},{10,... | collective-permute-start | bytes 1843208 | tf_op jit(solution)/shard_map/ppermute | solution.py:264
  30.1 4.9 %collective-permute-start.15 = (bf16[80,1280]{1,0:T(8,128)(2,1)S(1)}, bf16[80,1280]{1,0:T(8,128)(2,1)S(1)}, u32[]{:S(2)}, u32[]{:S(2)}) collective-permute-start(bf16[80,1280]{1,0:T(8,128)(2,1)S(1)} %get-tuple-element.37), channel_id=1, source_target_pairs={{0,1},{1,0},{2,3},{3,2},{4,5},{5,4},{6,7},{7,6},{8,9},{9,8},{10,11... | collective-permute-start | bytes 614408 | tf_op jit(solution)/shard_map/ppermute | solution.py:264
  32.6 6.4 %collective-permute-start.16 = (bf16[80,1280]{1,0:T(8,128)(2,1)S(1)}, bf16[80,1280]{1,0:T(8,128)(2,1)S(1)}, u32[]{:S(2)}, u32[]{:S(2)}) collective-permute-start(bf16[80,1280]{1,0:T(8,128)(2,1)S(1)} %get-tuple-element.36), channel_id=1, source_target_pairs={{0,1},{1,0},{2,3},{3,2},{4,5},{5,4},{6,7},{7,6},{8,9},{9,8},{10,11... | collective-permute-start | bytes 614408 | tf_op jit(solution)/shard_map/ppermute | solution.py:264
  32.6 6.4 %collective-permute-start.17 = (bf16[80,1280]{1,0:T(8,128)(2,1)S(1)}, bf16[80,1280]{1,0:T(8,128)(2,1)S(1)}, u32[]{:S(2)}, u32[]{:S(2)}) collective-permute-start(bf16[80,1280]{1,0:T(8,128)(2,1)S(1)} %get-tuple-element.35), channel_id=1, source_target_pairs={{0,1},{1,0},{2,3},{3,2},{4,5},{5,4},{6,7},{7,6},{8,9},{9,8},{10,11... | collective-permute-start | bytes 614408 | tf_op jit(solution)/shard_map/ppermute | solution.py:264
  33.1 5.9 %collective-permute-start.10 = (bf16[320,128]{1,0:T(8,128)(2,1)S(1)}, bf16[320,128]{1,0:T(8,128)(2,1)S(1)}, u32[]{:S(2)}, u32[]{:S(2)}) collective-permute-start(bf16[320,128]{1,0:T(8,128)(2,1)S(1)} %slice.44), channel_id=1, source_target_pairs={{0,4},{1,5},{2,6},{3,7},{4,0},{5,1},{6,2},{7,3},{8,12},{9,13},{10,... | collective-permute-start | bytes 245768 | tf_op jit(solution)/shard_map/ppermute | solution.py:252
  35.0 4.0 %collective-permute-start.11 = (bf16[320,128]{1,0:T(8,128)(2,1)S(1)}, bf16[320,128]{1,0:T(8,128)(2,1)S(1)}, u32[]{:S(2)}, u32[]{:S(2)}) collective-permute-start(bf16[320,128]{1,0:T(8,128)(2,1)S(1)} %slice.45), channel_id=1, source_target_pairs={{0,1},{1,0},{2,3},{3,2},{4,8},{5,9},{6,10},{7,11},{8,4},{9,5},{10,... | collective-permute-start | bytes 245768 | tf_op jit(solution)/shard_map/ppermute | solution.py:252
  45.4 2.1 %collective-permute-start.19 = (bf16[240,1280]{1,0:T(8,128)(2,1)S(1)}, bf16[240,1280]{1,0:T(8,128)(2,1)S(1)}, u32[]{:S(2)}, u32[]{:S(2)}) collective-permute-start(bf16[240,1280]{1,0:T(8,128)(2,1)S(1)} %collective-permute-done.18.refs_7_), channel_id=1, source_target_pairs={{0,1},{1,0},{2,3},{3,2},{4,5},{5,4},{6,7},{7,6},{8,9},{9,8},{10,11... | collective-permute-start | bytes 1843208 | tf_op jit(solution)/shard_map/ppermute | solution.py:264
  49.7 10.2 %collective-permute-start.20 = (bf16[128,1280]{1,0:T(8,128)(2,1)S(1)}, bf16[128,1280]{1,0:T(8,128)(2,1)S(1)}, u32[]{:S(2)}, u32[]{:S(2)}) collective-permute-start(bf16[128,1280]{1,0:T(8,128)(2,1)S(1)} %shard_map.79), channel_id=1, source_target_pairs={{0,16},{16,0},{1,17},{17,1},{2,18},{18,2},{3,19},{19,3},{4,20},{20... | collective-permute-start | bytes 983048 | tf_op jit(solution)/shard_map/ppermute | solution.py:351

commit v4 on v3

--- a/solution.py
+++ b/solution.py
@@ -306,13 +306,13 @@
     skip = width if count == 3 else 0
     far_grad, to_odd = call(
         functools.partial(relay_kernel, skip),
-        [own_grad, *steps[1], far_out, *far_near_out],
+        [after(own_grad, near[1]), *steps[1], far_out, *far_near_out],
         (sized(steps[1][0].shape[0] - skip + some, BLOCK, BF16),) * 2,
         window,
         scalars=False,
     )
     steps.append(pair_steps(to_odd, far_grad))
-    far_first = dp_swap(after(local[:QKV], far_grad), 2)
+    far_first = dp_swap(after(local[:QKV], normed), 2)
     thirds = after(far_last, far_grad)
     far_near_last = [dp_swap(thirds[at : at + HEAD_DIM], 1) for at in range(0, QKV, HEAD_DIM)]
     while len(steps) < count + 1:

time: 60.8 us -> 59.3 us (0.975)
  waiting for transfers between devices: 30 us -> 26.1 us
  starting transfers between devices: 16.2 us -> 18.5 us
    ppermute x12, waiting for transfers between devices: 11.9 us -> 8.16 us  [dp_swap(): lax.ppermute(array, 'dp', [(i, i ^ by) for i in range(lax.axis_size('dp'))])]
    ppermute x8, starting transfers between devices: 8.18 us -> 11.1 us  [pair_swap(): return lax.ppermute(array, ('ctx', 'dp'), pairs)]
  transfers between devices with their start and end apart: 21 -> 21, of which waited for: 8 -> 7; matrix products, arithmetic and copies ran while one was open for 0% -> 0% of each run, Pallas kernels for 18% -> 19%
where the time goes in v4:
time: 59.3 us; the launch traced here: 59.2 us
  waiting for transfers between devices  26.1 us (44%)
  starting transfers between devices  18.5 us (31%)
  Pallas kernels  13.4 us (23%)
  local copies, waits for them, and re-layouts  0.99 us (2%)
    pallas_call x7, Pallas kernels, call(): pl.pallas_call(kernel, out_shape=out_shape, in_specs=specs + [pl.BlockSpe...  13.4 us
    ppermute x8, starting transfers between devices, pair_swap(): return lax.ppermute(array, ('ctx', 'dp'), pairs)  11.1 us
    ppermute x8, waiting for transfers between devices, pair_swap(): return lax.ppermute(array, ('ctx', 'dp'), pairs)  9.62 us
    ppermute x1, waiting for transfers between devices, body(): lax.ppermute(result, 'section', [(i, (i - 1) % sections) for i in range(s...  8.31 us
    ppermute x12, waiting for transfers between devices, dp_swap(): lax.ppermute(array, 'dp', [(i, i ^ by) for i in range(lax.axis_size('dp'))])  8.16 us
    ppermute x12, starting transfers between devices, dp_swap(): lax.ppermute(array, 'dp', [(i, i ^ by) for i in range(lax.axis_size('dp'))])  5.86 us
    ppermute x1, starting transfers between devices, body(): lax.ppermute(result, 'section', [(i, (i - 1) % sections) for i in range(s...  1.58 us
  transfers between devices with their start and end apart: 21, of which 7 were waited for; matrix products, arithmetic and copies ran while one was open for 0% of the time, Pallas kernels for 19%

profile of v4, /device:TPU:0, one launch (start us, length us, event | category | flops | bytes accessed | tf_op | source)
XLA Modules:
  0.0 59.2 jit_solution(6491488764336347899)
XLA Ops:
  0.0 0.5 collective-permute-start.2
  0.5 2.5 %collective-permute-start = (bf16[160,1280]{1,0:T(8,128)(2,1)}, bf16[160,1280]{1,0:T(8,128)(2,1)S(1)}, u32[]{:S(2)}, u32[]{:S(2)}) collective-permute-start(bf16[160,1280]{1,0:T(8,128)(2,1)} %bitcast.20), channel_id=1, source_target_pairs={{0,2},{1,3},{2,0},{3,1},{4,6},{5,7},{6,4},{7,5},{8,10},{9,11},{10,... | collective-permute-start | bytes 1228808 | tf_op jit(solution)/shard_map/ppermute | solution.py:264
  2.9 0.0 copy-start
  2.9 1.4 %shard_map.73.refs_10_ = bf16[480,1280]{1,0:T(8,128)(2,1)S(1)} custom-call(bf16[160,1280]{1,0:T(8,128)(2,1)} %bitcast.22, bf16[160,1280]{1,0:T(8,128)(2,1)} %bitcast.23, bf16[160,1280]{1,0:T(8,128)(2,1)} %bitcast.24), custom_call_target="tpu_custom_call" | custom-call | flops 1000 | bytes 1000 | tf_op jit(solution)/shard_map/pallas_call | solution.py:231
  4.4 0.0 collective-permute-done.2.refs_1_
  4.4 0.0 copy-done
  4.4 0.0 copy-start.1
  4.4 0.0 copy-start.2
  4.4 1.6 %collective-permute-start.3 = (bf16[128,1280]{1,0:T(8,128)(2,1)S(1)}, bf16[128,1280]{1,0:T(8,128)(2,1)S(1)}, u32[]{:S(2)}, u32[]{:S(2)}) collective-permute-start(bf16[128,1280]{1,0:T(8,128)(2,1)S(1)} %bitcast.13), channel_id=1, source_target_pairs={{0,4},{1,5},{2,6},{3,7},{4,0},{5,1},{6,2},{7,3},{8,12},{9,13},{10,... | collective-permute-start | bytes 983048 | tf_op jit(solution)/shard_map/ppermute | solution.py:252
  6.1 0.0 collective-permute-start.4
  6.1 0.1 fusion
  6.2 0.6 %collective-permute-start.14 = (bf16[240,1280]{1,0:T(8,128)(2,1)S(1)}, bf16[240,1280]{1,0:T(8,128)(2,1)S(1)}, u32[]{:S(2)}, u32[]{:S(2)}) collective-permute-start(bf16[240,1280]{1,0:T(8,128)(2,1)S(1)} %get-tuple-element.36), channel_id=1, source_target_pairs={{0,2},{1,3},{2,0},{3,1},{4,6},{5,7},{6,4},{7,5},{8,10},{9,11},{10,... | collective-permute-start | bytes 1843208 | tf_op jit(solution)/shard_map/ppermute | solution.py:264
  6.8 6.7 %collective-permute-done.refs_0_ = bf16[160,1280]{1,0:T(8,128)(2,1)S(1)} collective-permute-done((bf16[160,1280]{1,0:T(8,128)(2,1)}, bf16[160,1280]{1,0:T(8,128)(2,1)S(1)}, u32[]{:S(2)}, u32[]{:S(2)}) %collective-permute-start) | collective-permute-done | bytes 409632 | tf_op jit(solution)/shard_map/ppermute | solution.py:264
  13.5 0.1 collective-permute-start.1
  13.6 0.8 %collective-permute-done.3.even_ref = bf16[128,1280]{1,0:T(8,128)(2,1)S(1)} collective-permute-done((bf16[128,1280]{1,0:T(8,128)(2,1)S(1)}, bf16[128,1280]{1,0:T(8,128)(2,1)S(1)}, u32[]{:S(2)}, u32[]{:S(2)}) %collective-permute-start.3) | collective-permute-done | bytes 327712 | tf_op jit(solution)/shard_map/ppermute | solution.py:252
  14.4 0.0 collective-permute-done.4.odd_ref
  14.4 0.0 copy-done.1
  14.4 0.0 copy-done.2
  14.4 0.6 %shard_map.74 = (bf16[1280,128]{1,0:T(8,128)(2,1)S(1)}, bf16[1600,128]{1,0:T(8,128)(2,1)S(1)}, bf16[1600,128]{1,0:T(8,128)(2,1)S(1)}) custom-call(bf16[128,1280]{1,0:T(8,128)(2,1)S(1)} %bitcast.15, bf16[128,1280]{1,0:T(8,128)(2,1)S(1)} %bitcast.17, bf16[128,1280]{1,0:T(8,128)(2,1)S(1)} %collective-permute-done.3.even_ref, ...), custom_call_target="tpu_custom_call" | custom-call | flops 1000 | bytes 1000 | tf_op jit(solution)/shard_map/pallas_call | solution.py:231
  15.0 2.8 %collective-permute-start.5 = (bf16[1600,128]{1,0:T(8,128)(2,1)S(1)}, bf16[1600,128]{1,0:T(8,128)(2,1)S(1)}, u32[]{:S(2)}, u32[]{:S(2)}) collective-permute-start(bf16[1600,128]{1,0:T(8,128)(2,1)S(1)} %get-tuple-element.24.refs_2_.refs_5_), channel_id=1, source_target_pairs={{0,4},{1,5},{2,6},{3,7},{4,0},{5,1},{6,2},{7,3},{8,12},{9,13},{10,... | collective-permute-start | bytes 1228808 | tf_op jit(solution)/shard_map/ppermute | solution.py:252
  17.7 0.0 collective-permute-start.6
  17.8 0.6 collective-permute-start.7
  18.3 0.0 collective-permute-done.1.refs_12_
  18.3 0.1 collective-permute-start.8
  18.4 0.1 slice.38
  18.5 1.3 %collective-permute-done.7.refs_1_ = bf16[80,1280]{1,0:T(8,128)(2,1)S(1)} collective-permute-done((bf16[80,1280]{1,0:T(8,128)(2,1)S(1)}, bf16[80,1280]{1,0:T(8,128)(2,1)S(1)}, u32[]{:S(2)}, u32[]{:S(2)}) %collective-permute-start.7) | collective-permute-done | bytes 204832 | tf_op jit(solution)/shard_map/ppermute | solution.py:264
  19.8 0.1 collective-permute-start.13
  19.9 0.2 collective-permute-done.8.refs_2_
  20.1 0.5 collective-permute-start.18
  20.6 6.2 %collective-permute-done.5.even_ref.refs_3_.refs_6_ = bf16[1600,128]{1,0:T(8,128)(2,1)S(1)} collective-permute-done((bf16[1600,128]{1,0:T(8,128)(2,1)S(1)}, bf16[1600,128]{1,0:T(8,128)(2,1)S(1)}, u32[]{:S(2)}, u32[]{:S(2)}) %collective-permute-start.5) | collective-permute-done | bytes 409632 | tf_op jit(solution)/shard_map/ppermute | solution.py:252
  26.8 0.0 collective-permute-done.6.odd_ref.refs_4_.refs_7_
  26.8 0.4 shard_map.75
  27.2 0.0 copy-start.3
  27.2 0.1 collective-permute-start.10
  27.3 4.3 %collective-permute-start.9 = (bf16[640,128]{1,0:T(8,128)(2,1)S(1)}, bf16[640,128]{1,0:T(8,128)(2,1)S(1)}, u32[]{:S(2)}, u32[]{:S(2)}) collective-permute-start(bf16[640,128]{1,0:T(8,128)(2,1)S(1)} %get-tuple-element.28.refs_0_), channel_id=1, source_target_pairs={{0,4},{1,5},{2,6},{3,7},{4,0},{5,1},{6,2},{7,3},{8,12},{9,13},{10,... | collective-permute-start | bytes 491528 | tf_op jit(solution)/shard_map/ppermute | solution.py:252
  31.6 0.0 collective-permute-done.14.refs_7_
  31.6 0.1 collective-permute-start.15
  31.7 0.0 collective-permute-done.10.refs_9_.refs_2_
  31.7 0.5 collective-permute-start.16
  32.2 2.7 %collective-permute-done.9.refs_8_.refs_1_ = bf16[640,128]{1,0:T(8,128)(2,1)S(1)} collective-permute-done((bf16[640,128]{1,0:T(8,128)(2,1)S(1)}, bf16[640,128]{1,0:T(8,128)(2,1)S(1)}, u32[]{:S(2)}, u32[]{:S(2)}) %collective-permute-start.9) | collective-permute-done | bytes 163872 | tf_op jit(solution)/shard_map/ppermute | solution.py:252
  34.9 0.0 collective-permute-start.17
  34.9 0.0 collective-permute-done.13.refs_11_
  34.9 2.1 %collective-permute-start.11 = (bf16[320,128]{1,0:T(8,128)(2,1)S(1)}, bf16[320,128]{1,0:T(8,128)(2,1)S(1)}, u32[]{:S(2)}, u32[]{:S(2)}) collective-permute-start(bf16[320,128]{1,0:T(8,128)(2,1)S(1)} %slice.44), channel_id=1, source_target_pairs={{0,4},{1,5},{2,6},{3,7},{4,0},{5,1},{6,2},{7,3},{8,12},{9,13},{10,... | collective-permute-start | bytes 245768 | tf_op jit(solution)/shard_map/ppermute | solution.py:252
  37.0 0.0 collective-permute-done.15.refs_8_
  37.0 0.2 collective-permute-start.12
  37.2 0.0 copy-done.3
  37.2 4.0 %shard_map.76 = (bf16[1280,384]{1,0:T(8,128)(2,1)S(1)}, f32[128,1280]{1,0:T(8,128)S(1)}) custom-call(s32[4,4]{1,0:T(4,128)S(1)} %copy-done.3, bf16[1280,128]{1,0:T(8,128)(2,1)S(1)} %get-tuple-element.26.refs_0_, bf16[1600,128]{1,0:T(8,128)(2,1)S(1)} %get-tuple-element.25.refs_1_, bf16[1600,128]{1,0:T(8,128)(2,1)S(1)} %get-tuple-element.24.refs_2_.refs_5_, ...), custom_call_target="tpu_custom_call" | custom-call | flops 1000 | bytes 1000 | tf_op jit(solution)/shard_map/pallas_call | solution.py:231
  41.2 0.0 collective-permute-done.16.refs_9_
  41.2 0.0 collective-permute-done.17.refs_10_
  41.2 0.0 collective-permute-done.11.refs_3_
  41.2 0.0 collective-permute-done.12.refs_4_
  41.2 2.6 %shard_map.77.refs_6_ = f32[128,1280]{1,0:T(8,128)S(1)} custom-call(s32[4,4]{1,0:T(4,128)S(1)} %copy-done.3, bf16[640,128]{1,0:T(8,128)(2,1)S(1)} %get-tuple-element.28.refs_0_, bf16[640,128]{1,0:T(8,128)(2,1)S(1)} %collective-permute-done.9.refs_8_.refs_1_, bf16[640,128]{1,0:T(8,128)(2,1)S(1)} %collective-permute-done.10.refs_9_.refs_2_, ...), custom_call_target="tpu_custom_call" | custom-call | flops 1000 | bytes 1000 | tf_op jit(solution)/shard_map/pallas_call | solution.py:231
  43.8 0.0 collective-permute-done.18.refs_7_
  43.8 0.4 collective-permute-start.19
  44.2 2.1 %shard_map.78.refs_6_ = f32[128,1280]{1,0:T(8,128)S(1)} custom-call(s32[4,4]{1,0:T(4,128)S(1)} %copy-done.3, bf16[640,128]{1,0:T(8,128)(2,1)S(1)} %get-tuple-element.28.refs_0_, bf16[640,128]{1,0:T(8,128)(2,1)S(1)} %collective-permute-done.9.refs_8_.refs_1_, bf16[640,128]{1,0:T(8,128)(2,1)S(1)} %collective-permute-done.10.refs_9_.refs_2_, ...), custom_call_target="tpu_custom_call" | custom-call | flops 1000 | bytes 1000 | tf_op jit(solution)/shard_map/pallas_call | solution.py:231
  46.3 0.0 collective-permute-done.19.refs_7_
  46.3 2.3 %shard_map.79 = bf16[128,1280]{1,0:T(8,128)(2,1)S(1)} custom-call(s32[4,4]{1,0:T(4,128)S(1)} %copy-done.3, bf16[640,128]{1,0:T(8,128)(2,1)S(1)} %get-tuple-element.28.refs_0_, bf16[640,128]{1,0:T(8,128)(2,1)S(1)} %collective-permute-done.9.refs_8_.refs_1_, bf16[640,128]{1,0:T(8,128)(2,1)S(1)} %collective-permute-done.10.refs_9_.refs_2_, ...), custom_call_target="tpu_custom_call" | custom-call | flops 1000 | bytes 1000 | tf_op jit(solution)/shard_map/pallas_call | solution.py:231
  48.6 1.6 %collective-permute-start.20 = (bf16[128,1280]{1,0:T(8,128)(2,1)S(1)}, bf16[128,1280]{1,0:T(8,128)(2,1)S(1)}, u32[]{:S(2)}, u32[]{:S(2)}) collective-permute-start(bf16[128,1280]{1,0:T(8,128)(2,1)S(1)} %shard_map.79), channel_id=1, source_target_pairs={{0,16},{16,0},{1,17},{17,1},{2,18},{18,2},{3,19},{19,3},{4,20},{20... | collective-permute-start | bytes 983048 | tf_op jit(solution)/shard_map/ppermute | solution.py:351
  50.1 8.3 %collective-permute-done.20 = bf16[128,1280]{1,0:T(8,128)(2,1)S(1)} collective-permute-done((bf16[128,1280]{1,0:T(8,128)(2,1)S(1)}, bf16[128,1280]{1,0:T(8,128)(2,1)S(1)}, u32[]{:S(2)}, u32[]{:S(2)}) %collective-permute-start.20) | collective-permute-done | bytes 327712 | tf_op jit(solution)/shard_map/ppermute | solution.py:351
  58.5 0.7 %copy.9 = bf16[1,1,128,1280]{3,2,1,0:T(8,128)(2,1)} copy(bf16[1,1,128,1280]{3,2,1,0:T(8,128)(2,1)S(1)} %bitcast.25) | data formatting | bytes 655360
  (5 shorter events, 0.1 us)
Async XLA Ops:
  0.0 4.4 %collective-permute-start.2 = (bf16[160,1280]{1,0:T(8,128)(2,1)}, bf16[160,1280]{1,0:T(8,128)(2,1)S(1)}, u32[]{:S(2)}, u32[]{:S(2)}) collective-permute-start(bf16[160,1280]{1,0:T(8,128)(2,1)} %bitcast.19), channel_id=1, source_target_pairs={{0,1},{1,0},{2,3},{3,2},{4,5},{5,4},{6,7},{7,6},{8,9},{9,8},{10,11... | collective-permute-start | bytes 1228808 | tf_op jit(solution)/shard_map/ppermute | solution.py:264
  0.5 13.0 %collective-permute-start = (bf16[160,1280]{1,0:T(8,128)(2,1)}, bf16[160,1280]{1,0:T(8,128)(2,1)S(1)}, u32[]{:S(2)}, u32[]{:S(2)}) collective-permute-start(bf16[160,1280]{1,0:T(8,128)(2,1)} %bitcast.20), channel_id=1, source_target_pairs={{0,2},{1,3},{2,0},{3,1},{4,6},{5,7},{6,4},{7,5},{8,10},{9,11},{10,... | collective-permute-start | bytes 1228808 | tf_op jit(solution)/shard_map/ppermute | solution.py:264
  2.9 1.5 %copy-start = (bf16[1,1,128,1280]{3,2,1,0:T(8,128)(2,1)S(1)}, bf16[1,1,128,1280]{3,2,1,0:T(8,128)(2,1)}, u32[]{:S(2)}) copy-start(bf16[1,1,128,1280]{3,2,1,0:T(8,128)(2,1)} %param.7) | copy-start | bytes 983044
  4.4 9.9 %copy-start.1 = (bf16[1,1,128,1280]{3,2,1,0:T(8,128)(2,1)S(1)}, bf16[1,1,128,1280]{3,2,1,0:T(8,128)(2,1)}, u32[]{:S(2)}) copy-start(bf16[1,1,128,1280]{3,2,1,0:T(8,128)(2,1)} %param.8) | copy-start | bytes 983044
  4.4 9.9 %copy-start.2 = (bf16[1,160,1280]{2,1,0:T(8,128)(2,1)S(1)}, bf16[1,160,1280]{2,1,0:T(8,128)(2,1)}, u32[]{:S(2)}) copy-start(bf16[1,160,1280]{2,1,0:T(8,128)(2,1)} %param.13) | copy-start | bytes 1228804
  4.4 9.9 %collective-permute-start.3 = (bf16[128,1280]{1,0:T(8,128)(2,1)S(1)}, bf16[128,1280]{1,0:T(8,128)(2,1)S(1)}, u32[]{:S(2)}, u32[]{:S(2)}) collective-permute-start(bf16[128,1280]{1,0:T(8,128)(2,1)S(1)} %bitcast.13), channel_id=1, source_target_pairs={{0,4},{1,5},{2,6},{3,7},{4,0},{5,1},{6,2},{7,3},{8,12},{9,13},{10,... | collective-permute-start | bytes 983048 | tf_op jit(solution)/shard_map/ppermute | solution.py:252
  6.1 8.3 %collective-permute-start.4 = (bf16[128,1280]{1,0:T(8,128)(2,1)S(1)}, bf16[128,1280]{1,0:T(8,128)(2,1)S(1)}, u32[]{:S(2)}, u32[]{:S(2)}) collective-permute-start(bf16[128,1280]{1,0:T(8,128)(2,1)S(1)} %bitcast.14), channel_id=1, source_target_pairs={{0,1},{1,0},{2,3},{3,2},{4,8},{5,9},{6,10},{7,11},{8,4},{9,5},{10,... | collective-permute-start | bytes 983048 | tf_op jit(solution)/shard_map/ppermute | solution.py:252
  6.2 25.4 %collective-permute-start.14 = (bf16[240,1280]{1,0:T(8,128)(2,1)S(1)}, bf16[240,1280]{1,0:T(8,128)(2,1)S(1)}, u32[]{:S(2)}, u32[]{:S(2)}) collective-permute-start(bf16[240,1280]{1,0:T(8,128)(2,1)S(1)} %get-tuple-element.36), channel_id=1, source_target_pairs={{0,2},{1,3},{2,0},{3,1},{4,6},{5,7},{6,4},{7,5},{8,10},{9,11},{10,... | collective-permute-start | bytes 1843208 | tf_op jit(solution)/shard_map/ppermute | solution.py:264
  13.5 4.8 %collective-permute-start.1 = (bf16[160,1280]{1,0:T(8,128)(2,1)S(1)}, bf16[160,1280]{1,0:T(8,128)(2,1)S(1)}, u32[]{:S(2)}, u32[]{:S(2)}) collective-permute-start(bf16[160,1280]{1,0:T(8,128)(2,1)S(1)} %slice.33), channel_id=1, source_target_pairs={{0,1},{1,0},{2,3},{3,2},{4,5},{5,4},{6,7},{7,6},{8,9},{9,8},{10,11... | collective-permute-start | bytes 1228808 | tf_op jit(solution)/shard_map/ppermute | solution.py:264
  15.0 11.8 %collective-permute-start.5 = (bf16[1600,128]{1,0:T(8,128)(2,1)S(1)}, bf16[1600,128]{1,0:T(8,128)(2,1)S(1)}, u32[]{:S(2)}, u32[]{:S(2)}) collective-permute-start(bf16[1600,128]{1,0:T(8,128)(2,1)S(1)} %get-tuple-element.24.refs_2_.refs_5_), channel_id=1, source_target_pairs={{0,4},{1,5},{2,6},{3,7},{4,0},{5,1},{6,2},{7,3},{8,12},{9,13},{10,... | collective-permute-start | bytes 1228808 | tf_op jit(solution)/shard_map/ppermute | solution.py:252
  17.7 9.0 %collective-permute-start.6 = (bf16[1600,128]{1,0:T(8,128)(2,1)S(1)}, bf16[1600,128]{1,0:T(8,128)(2,1)S(1)}, u32[]{:S(2)}, u32[]{:S(2)}) collective-permute-start(bf16[1600,128]{1,0:T(8,128)(2,1)S(1)} %get-tuple-element.25.refs_1_), channel_id=1, source_target_pairs={{0,1},{1,0},{2,3},{3,2},{4,8},{5,9},{6,10},{7,11},{8,4},{9,5},{10,... | collective-permute-start | bytes 1228808 | tf_op jit(solution)/shard_map/ppermute | solution.py:252
  17.8 2.0 %collective-permute-start.7 = (bf16[80,1280]{1,0:T(8,128)(2,1)S(1)}, bf16[80,1280]{1,0:T(8,128)(2,1)S(1)}, u32[]{:S(2)}, u32[]{:S(2)}) collective-permute-start(bf16[80,1280]{1,0:T(8,128)(2,1)S(1)} %get-tuple-element.41), channel_id=1, source_target_pairs={{0,1},{1,0},{2,3},{3,2},{4,5},{5,4},{6,7},{7,6},{8,9},{9,8},{10,11... | collective-permute-start | bytes 614408 | tf_op jit(solution)/shard_map/ppermute | solution.py:264
  18.3 1.7 %collective-permute-start.8 = (bf16[80,1280]{1,0:T(8,128)(2,1)S(1)}, bf16[80,1280]{1,0:T(8,128)(2,1)S(1)}, u32[]{:S(2)}, u32[]{:S(2)}) collective-permute-start(bf16[80,1280]{1,0:T(8,128)(2,1)S(1)} %get-tuple-element.40), channel_id=1, source_target_pairs={{0,1},{1,0},{2,3},{3,2},{4,5},{5,4},{6,7},{7,6},{8,9},{9,8},{10,11... | collective-permute-start | bytes 614408 | tf_op jit(solution)/shard_map/ppermute | solution.py:264
  19.8 15.1 %collective-permute-start.13 = (bf16[320,1280]{1,0:T(8,128)(2,1)S(1)}, bf16[320,1280]{1,0:T(8,128)(2,1)S(1)}, u32[]{:S(2)}, u32[]{:S(2)}) collective-permute-start(bf16[320,1280]{1,0:T(8,128)(2,1)S(1)} %slice.38), channel_id=1, source_target_pairs={{0,1},{1,0},{2,3},{3,2},{4,5},{5,4},{6,7},{7,6},{8,9},{9,8},{10,11... | collective-permute-start | bytes 2457608 | tf_op jit(solution)/shard_map/ppermute | solution.py:264
  20.1 23.7 %collective-permute-start.18 = (bf16[240,1280]{1,0:T(8,128)(2,1)S(1)}, bf16[240,1280]{1,0:T(8,128)(2,1)S(1)}, u32[]{:S(2)}, u32[]{:S(2)}) collective-permute-start(bf16[240,1280]{1,0:T(8,128)(2,1)S(1)} %get-tuple-element.33), channel_id=1, source_target_pairs={{0,2},{1,3},{2,0},{3,1},{4,6},{5,7},{6,4},{7,5},{8,10},{9,11},{10,... | collective-permute-start | bytes 1843208 | tf_op jit(solution)/shard_map/ppermute | solution.py:264
  27.2 10.0 %copy-start.3 = (s32[4,4]{1,0:T(4,128)S(1)}, s32[4,4]{1,0:T(4,128)}, u32[]{:S(2)}) copy-start(s32[4,4]{1,0:T(4,128)} %ids_ref.7) | copy-start | bytes 196
  27.2 4.5 %collective-permute-start.10 = (bf16[640,128]{1,0:T(8,128)(2,1)S(1)}, bf16[640,128]{1,0:T(8,128)(2,1)S(1)}, u32[]{:S(2)}, u32[]{:S(2)}) collective-permute-start(bf16[640,128]{1,0:T(8,128)(2,1)S(1)} %get-tuple-element.29), channel_id=1, source_target_pairs={{0,1},{1,0},{2,3},{3,2},{4,8},{5,9},{6,10},{7,11},{8,4},{9,5},{10,... | collective-permute-start | bytes 491528 | tf_op jit(solution)/shard_map/ppermute | solution.py:252
  27.3 7.6 %collective-permute-start.9 = (bf16[640,128]{1,0:T(8,128)(2,1)S(1)}, bf16[640,128]{1,0:T(8,128)(2,1)S(1)}, u32[]{:S(2)}, u32[]{:S(2)}) collective-permute-start(bf16[640,128]{1,0:T(8,128)(2,1)S(1)} %get-tuple-element.28.refs_0_), channel_id=1, source_target_pairs={{0,4},{1,5},{2,6},{3,7},{4,0},{5,1},{6,2},{7,3},{8,12},{9,13},{10,... | collective-permute-start | bytes 491528 | tf_op jit(solution)/shard_map/ppermute | solution.py:252
  31.6 5.4 %collective-permute-start.15 = (bf16[80,1280]{1,0:T(8,128)(2,1)S(1)}, bf16[80,1280]{1,0:T(8,128)(2,1)S(1)}, u32[]{:S(2)}, u32[]{:S(2)}) collective-permute-start(bf16[80,1280]{1,0:T(8,128)(2,1)S(1)} %get-tuple-element.39), channel_id=1, source_target_pairs={{0,1},{1,0},{2,3},{3,2},{4,5},{5,4},{6,7},{7,6},{8,9},{9,8},{10,11... | collective-permute-start | bytes 614408 | tf_op jit(solution)/shard_map/ppermute | solution.py:264
  31.7 9.5 %collective-permute-start.16 = (bf16[80,1280]{1,0:T(8,128)(2,1)S(1)}, bf16[80,1280]{1,0:T(8,128)(2,1)S(1)}, u32[]{:S(2)}, u32[]{:S(2)}) collective-permute-start(bf16[80,1280]{1,0:T(8,128)(2,1)S(1)} %get-tuple-element.38), channel_id=1, source_target_pairs={{0,1},{1,0},{2,3},{3,2},{4,5},{5,4},{6,7},{7,6},{8,9},{9,8},{10,11... | collective-permute-start | bytes 614408 | tf_op jit(solution)/shard_map/ppermute | solution.py:264
  34.9 6.3 %collective-permute-start.17 = (bf16[80,1280]{1,0:T(8,128)(2,1)S(1)}, bf16[80,1280]{1,0:T(8,128)(2,1)S(1)}, u32[]{:S(2)}, u32[]{:S(2)}) collective-permute-start(bf16[80,1280]{1,0:T(8,128)(2,1)S(1)} %get-tuple-element.37), channel_id=1, source_target_pairs={{0,1},{1,0},{2,3},{3,2},{4,5},{5,4},{6,7},{7,6},{8,9},{9,8},{10,11... | collective-permute-start | bytes 614408 | tf_op jit(solution)/shard_map/ppermute | solution.py:264
  34.9 6.3 %collective-permute-start.11 = (bf16[320,128]{1,0:T(8,128)(2,1)S(1)}, bf16[320,128]{1,0:T(8,128)(2,1)S(1)}, u32[]{:S(2)}, u32[]{:S(2)}) collective-permute-start(bf16[320,128]{1,0:T(8,128)(2,1)S(1)} %slice.44), channel_id=1, source_target_pairs={{0,4},{1,5},{2,6},{3,7},{4,0},{5,1},{6,2},{7,3},{8,12},{9,13},{10,... | collective-permute-start | bytes 245768 | tf_op jit(solution)/shard_map/ppermute | solution.py:252
  37.0 4.2 %collective-permute-start.12 = (bf16[320,128]{1,0:T(8,128)(2,1)S(1)}, bf16[320,128]{1,0:T(8,128)(2,1)S(1)}, u32[]{:S(2)}, u32[]{:S(2)}) collective-permute-start(bf16[320,128]{1,0:T(8,128)(2,1)S(1)} %slice.45), channel_id=1, source_target_pairs={{0,1},{1,0},{2,3},{3,2},{4,8},{5,9},{6,10},{7,11},{8,4},{9,5},{10,... | collective-permute-start | bytes 245768 | tf_op jit(solution)/shard_map/ppermute | solution.py:252
  43.8 2.5 %collective-permute-start.19 = (bf16[240,1280]{1,0:T(8,128)(2,1)S(1)}, bf16[240,1280]{1,0:T(8,128)(2,1)S(1)}, u32[]{:S(2)}, u32[]{:S(2)}) collective-permute-start(bf16[240,1280]{1,0:T(8,128)(2,1)S(1)} %collective-permute-done.18.refs_7_), channel_id=1, source_target_pairs={{0,1},{1,0},{2,3},{3,2},{4,5},{5,4},{6,7},{7,6},{8,9},{9,8},{10,11... | collective-permute-start | bytes 1843208 | tf_op jit(solution)/shard_map/ppermute | solution.py:264
  48.6 9.9 %collective-permute-start.20 = (bf16[128,1280]{1,0:T(8,128)(2,1)S(1)}, bf16[128,1280]{1,0:T(8,128)(2,1)S(1)}, u32[]{:S(2)}, u32[]{:S(2)}) collective-permute-start(bf16[128,1280]{1,0:T(8,128)(2,1)S(1)} %shard_map.79), channel_id=1, source_target_pairs={{0,16},{16,0},{1,17},{17,1},{2,18},{18,2},{3,19},{19,3},{4,20},{20... | collective-permute-start | bytes 983048 | tf_op jit(solution)/shard_map/ppermute | solution.py:351

commit v5 on v4

--- a/solution.py
+++ b/solution.py
@@ -343,10 +343,9 @@
             scratch=[pltpu.VMEM((len(places) * HEAD_DIM, window), BF16)],
         )
 
+    far_near_first = dp_swap(after(far_first, total, steps[-1], far_near_last), 1)
     total = add(total, (1, heads + 1), [far_last, *far_near_last])
-    far_near_first = dp_swap(after(far_first, total), 1)
-    total = add(total, (0,), [far_first])
-    result = add(total, (heads,), [far_near_first], [own_input])
+    result = add(total, (0, heads), [far_first, far_near_first], [own_input])
     sections = lax.axis_size("section")
     result = lax.ppermute(result, "section", [(i, (i - 1) % sections) for i in range(sections)])
     return result[None, None]

time: 59.3 us -> 57.7 us (0.973)
  Pallas kernels: 13.4 us -> 11.8 us
    pallas_call x7 -> x6, Pallas kernels: 13.4 us -> 11.8 us  [call(): pl.pallas_call(kernel, out_shape=out_shape, in_specs=specs + [pl.BlockSpe...]
  transfers between devices with their start and end apart: 21 -> 21, of which waited for: 7 -> 7; matrix products, arithmetic and copies ran while one was open for 0% -> 0% of each run, Pallas kernels for 19% -> 16%
where the time goes in v5:
time: 57.7 us; the launch traced here: 57.6 us
  waiting for transfers between devices  26.1 us (45%)
  starting transfers between devices  18.5 us (32%)
  Pallas kernels  11.8 us (20%)
  local copies, waits for them, and re-layouts  0.99 us (2%)
    pallas_call x6, Pallas kernels, call(): pl.pallas_call(kernel, out_shape=out_shape, in_specs=specs + [pl.BlockSpe...  11.8 us
    ppermute x8, starting transfers between devices, pair_swap(): return lax.ppermute(array, ('ctx', 'dp'), pairs)  11 us
    ppermute x8, waiting for transfers between devices, pair_swap(): return lax.ppermute(array, ('ctx', 'dp'), pairs)  9.62 us
    ppermute x1, waiting for transfers between devices, body(): lax.ppermute(result, 'section', [(i, (i - 1) % sections) for i in range(s...  8.32 us
    ppermute x12, waiting for transfers between devices, dp_swap(): lax.ppermute(array, 'dp', [(i, i ^ by) for i in range(lax.axis_size('dp'))])  8.16 us
    ppermute x12, starting transfers between devices, dp_swap(): lax.ppermute(array, 'dp', [(i, i ^ by) for i in range(lax.axis_size('dp'))])  5.87 us
    ppermute x1, starting transfers between devices, body(): lax.ppermute(result, 'section', [(i, (i - 1) % sections) for i in range(s...  1.58 us
  transfers between devices with their start and end apart: 21, of which 7 were waited for; matrix products, arithmetic and copies ran while one was open for 0% of the time, Pallas kernels for 16%

profile of v5, /device:TPU:0, one launch (start us, length us, event | category | flops | bytes accessed | tf_op | source)
XLA Modules:
  0.0 57.6 jit_solution(1853712739366334000)
XLA Ops:
  0.0 0.5 collective-permute-start.2
  0.5 2.5 %collective-permute-start = (bf16[160,1280]{1,0:T(8,128)(2,1)}, bf16[160,1280]{1,0:T(8,128)(2,1)S(1)}, u32[]{:S(2)}, u32[]{:S(2)}) collective-permute-start(bf16[160,1280]{1,0:T(8,128)(2,1)} %bitcast.20), channel_id=1, source_target_pairs={{0,2},{1,3},{2,0},{3,1},{4,6},{5,7},{6,4},{7,5},{8,10},{9,11},{10,... | collective-permute-start | bytes 1228808 | tf_op jit(solution)/shard_map/ppermute | solution.py:264
  2.9 0.0 copy-start.1
  2.9 1.4 %shard_map.73.refs_10_ = bf16[480,1280]{1,0:T(8,128)(2,1)S(1)} custom-call(bf16[160,1280]{1,0:T(8,128)(2,1)} %bitcast.22, bf16[160,1280]{1,0:T(8,128)(2,1)} %bitcast.23, bf16[160,1280]{1,0:T(8,128)(2,1)} %bitcast.24), custom_call_target="tpu_custom_call" | custom-call | flops 1000 | bytes 1000 | tf_op jit(solution)/shard_map/pallas_call | solution.py:231
  4.4 0.0 collective-permute-done.2.refs_1_
  4.4 0.0 copy-done.1
  4.4 0.0 copy-start
  4.4 0.0 copy-start.2
  4.4 1.6 %collective-permute-start.3 = (bf16[128,1280]{1,0:T(8,128)(2,1)S(1)}, bf16[128,1280]{1,0:T(8,128)(2,1)S(1)}, u32[]{:S(2)}, u32[]{:S(2)}) collective-permute-start(bf16[128,1280]{1,0:T(8,128)(2,1)S(1)} %bitcast.15), channel_id=1, source_target_pairs={{0,4},{1,5},{2,6},{3,7},{4,0},{5,1},{6,2},{7,3},{8,12},{9,13},{10,... | collective-permute-start | bytes 983048 | tf_op jit(solution)/shard_map/ppermute | solution.py:252
  6.1 0.0 collective-permute-start.4
  6.1 0.1 fusion
  6.2 0.6 %collective-permute-start.14 = (bf16[240,1280]{1,0:T(8,128)(2,1)S(1)}, bf16[240,1280]{1,0:T(8,128)(2,1)S(1)}, u32[]{:S(2)}, u32[]{:S(2)}) collective-permute-start(bf16[240,1280]{1,0:T(8,128)(2,1)S(1)} %get-tuple-element.36), channel_id=1, source_target_pairs={{0,2},{1,3},{2,0},{3,1},{4,6},{5,7},{6,4},{7,5},{8,10},{9,11},{10,... | collective-permute-start | bytes 1843208 | tf_op jit(solution)/shard_map/ppermute | solution.py:264
  6.8 6.7 %collective-permute-done.refs_0_ = bf16[160,1280]{1,0:T(8,128)(2,1)S(1)} collective-permute-done((bf16[160,1280]{1,0:T(8,128)(2,1)}, bf16[160,1280]{1,0:T(8,128)(2,1)S(1)}, u32[]{:S(2)}, u32[]{:S(2)}) %collective-permute-start) | collective-permute-done | bytes 409632 | tf_op jit(solution)/shard_map/ppermute | solution.py:264
  13.5 0.1 collective-permute-start.1
  13.6 0.8 %collective-permute-done.3.even_ref = bf16[128,1280]{1,0:T(8,128)(2,1)S(1)} collective-permute-done((bf16[128,1280]{1,0:T(8,128)(2,1)S(1)}, bf16[128,1280]{1,0:T(8,128)(2,1)S(1)}, u32[]{:S(2)}, u32[]{:S(2)}) %collective-permute-start.3) | collective-permute-done | bytes 327712 | tf_op jit(solution)/shard_map/ppermute | solution.py:252
  14.4 0.0 collective-permute-done.4.odd_ref
  14.4 0.0 copy-done
  14.4 0.0 copy-done.2
  14.4 0.6 %shard_map.74 = (bf16[1280,128]{1,0:T(8,128)(2,1)S(1)}, bf16[1600,128]{1,0:T(8,128)(2,1)S(1)}, bf16[1600,128]{1,0:T(8,128)(2,1)S(1)}) custom-call(bf16[128,1280]{1,0:T(8,128)(2,1)S(1)} %bitcast.17, bf16[128,1280]{1,0:T(8,128)(2,1)S(1)} %bitcast.13, bf16[128,1280]{1,0:T(8,128)(2,1)S(1)} %collective-permute-done.3.even_ref, ...), custom_call_target="tpu_custom_call" | custom-call | flops 1000 | bytes 1000 | tf_op jit(solution)/shard_map/pallas_call | solution.py:231
  15.0 2.8 %collective-permute-start.5 = (bf16[1600,128]{1,0:T(8,128)(2,1)S(1)}, bf16[1600,128]{1,0:T(8,128)(2,1)S(1)}, u32[]{:S(2)}, u32[]{:S(2)}) collective-permute-start(bf16[1600,128]{1,0:T(8,128)(2,1)S(1)} %get-tuple-element.24.refs_2_.refs_5_), channel_id=1, source_target_pairs={{0,4},{1,5},{2,6},{3,7},{4,0},{5,1},{6,2},{7,3},{8,12},{9,13},{10,... | collective-permute-start | bytes 1228808 | tf_op jit(solution)/shard_map/ppermute | solution.py:252
  17.7 0.0 collective-permute-start.6
  17.8 0.6 collective-permute-start.7
  18.3 0.0 collective-permute-done.1.refs_12_
  18.3 0.1 collective-permute-start.8
  18.4 0.1 slice.38
  18.5 1.3 %collective-permute-done.7.refs_1_ = bf16[80,1280]{1,0:T(8,128)(2,1)S(1)} collective-permute-done((bf16[80,1280]{1,0:T(8,128)(2,1)S(1)}, bf16[80,1280]{1,0:T(8,128)(2,1)S(1)}, u32[]{:S(2)}, u32[]{:S(2)}) %collective-permute-start.7) | collective-permute-done | bytes 204832 | tf_op jit(solution)/shard_map/ppermute | solution.py:264
  19.8 0.1 collective-permute-start.13
  19.9 0.2 collective-permute-done.8.refs_2_
  20.1 0.5 collective-permute-start.18
  20.6 6.2 %collective-permute-done.5.even_ref.refs_3_.refs_6_ = bf16[1600,128]{1,0:T(8,128)(2,1)S(1)} collective-permute-done((bf16[1600,128]{1,0:T(8,128)(2,1)S(1)}, bf16[1600,128]{1,0:T(8,128)(2,1)S(1)}, u32[]{:S(2)}, u32[]{:S(2)}) %collective-permute-start.5) | collective-permute-done | bytes 409632 | tf_op jit(solution)/shard_map/ppermute | solution.py:252
  26.8 0.0 collective-permute-done.6.odd_ref.refs_4_.refs_7_
  26.8 0.4 shard_map.75
  27.2 0.0 copy-start.3
  27.2 0.1 collective-permute-start.10
  27.3 4.3 %collective-permute-start.9 = (bf16[640,128]{1,0:T(8,128)(2,1)S(1)}, bf16[640,128]{1,0:T(8,128)(2,1)S(1)}, u32[]{:S(2)}, u32[]{:S(2)}) collective-permute-start(bf16[640,128]{1,0:T(8,128)(2,1)S(1)} %get-tuple-element.28.refs_0_), channel_id=1, source_target_pairs={{0,4},{1,5},{2,6},{3,7},{4,0},{5,1},{6,2},{7,3},{8,12},{9,13},{10,... | collective-permute-start | bytes 491528 | tf_op jit(solution)/shard_map/ppermute | solution.py:252
  31.6 0.0 collective-permute-done.14.refs_7_
  31.6 0.1 collective-permute-start.15
  31.7 0.0 collective-permute-done.10.refs_9_.refs_2_
  31.7 0.5 collective-permute-start.16
  32.2 2.7 %collective-permute-done.9.refs_8_.refs_1_ = bf16[640,128]{1,0:T(8,128)(2,1)S(1)} collective-permute-done((bf16[640,128]{1,0:T(8,128)(2,1)S(1)}, bf16[640,128]{1,0:T(8,128)(2,1)S(1)}, u32[]{:S(2)}, u32[]{:S(2)}) %collective-permute-start.9) | collective-permute-done | bytes 163872 | tf_op jit(solution)/shard_map/ppermute | solution.py:252
  34.9 0.0 collective-permute-start.17
  34.9 0.0 collective-permute-done.13.refs_11_
  34.9 2.1 %collective-permute-start.11 = (bf16[320,128]{1,0:T(8,128)(2,1)S(1)}, bf16[320,128]{1,0:T(8,128)(2,1)S(1)}, u32[]{:S(2)}, u32[]{:S(2)}) collective-permute-start(bf16[320,128]{1,0:T(8,128)(2,1)S(1)} %slice.44), channel_id=1, source_target_pairs={{0,4},{1,5},{2,6},{3,7},{4,0},{5,1},{6,2},{7,3},{8,12},{9,13},{10,... | collective-permute-start | bytes 245768 | tf_op jit(solution)/shard_map/ppermute | solution.py:252
  37.0 0.0 collective-permute-done.15.refs_8_
  37.0 0.2 collective-permute-start.12
  37.2 0.0 copy-done.3
  37.2 4.0 %shard_map.76 = (bf16[1280,384]{1,0:T(8,128)(2,1)S(1)}, f32[128,1280]{1,0:T(8,128)S(1)}) custom-call(s32[4,4]{1,0:T(4,128)S(1)} %copy-done.3, bf16[1280,128]{1,0:T(8,128)(2,1)S(1)} %get-tuple-element.26.refs_0_, bf16[1600,128]{1,0:T(8,128)(2,1)S(1)} %get-tuple-element.25.refs_1_, bf16[1600,128]{1,0:T(8,128)(2,1)S(1)} %get-tuple-element.24.refs_2_.refs_5_, ...), custom_call_target="tpu_custom_call" | custom-call | flops 1000 | bytes 1000 | tf_op jit(solution)/shard_map/pallas_call | solution.py:231
  41.2 0.0 collective-permute-done.16.refs_9_
  41.2 0.0 collective-permute-done.17.refs_10_
  41.2 0.0 collective-permute-done.18.refs_7_
  41.2 0.0 collective-permute-done.11.refs_3_
  41.2 0.0 collective-permute-done.12.refs_4_
  41.2 0.4 collective-permute-start.19
  41.6 2.6 %shard_map.77.refs_6_ = f32[128,1280]{1,0:T(8,128)S(1)} custom-call(s32[4,4]{1,0:T(4,128)S(1)} %copy-done.3, bf16[640,128]{1,0:T(8,128)(2,1)S(1)} %get-tuple-element.28.refs_0_, bf16[640,128]{1,0:T(8,128)(2,1)S(1)} %collective-permute-done.9.refs_8_.refs_1_, bf16[640,128]{1,0:T(8,128)(2,1)S(1)} %collective-permute-done.10.refs_9_.refs_2_, ...), custom_call_target="tpu_custom_call" | custom-call | flops 1000 | bytes 1000 | tf_op jit(solution)/shard_map/pallas_call | solution.py:231
  44.2 0.0 collective-permute-done.19.refs_8_
  44.2 2.7 %shard_map.78 = bf16[128,1280]{1,0:T(8,128)(2,1)S(1)} custom-call(s32[4,4]{1,0:T(4,128)S(1)} %copy-done.3, bf16[640,128]{1,0:T(8,128)(2,1)S(1)} %get-tuple-element.28.refs_0_, bf16[640,128]{1,0:T(8,128)(2,1)S(1)} %collective-permute-done.9.refs_8_.refs_1_, bf16[640,128]{1,0:T(8,128)(2,1)S(1)} %collective-permute-done.10.refs_9_.refs_2_, ...), custom_call_target="tpu_custom_call" | custom-call | flops 1000 | bytes 1000 | tf_op jit(solution)/shard_map/pallas_call | solution.py:231
  46.9 1.6 %collective-permute-start.20 = (bf16[128,1280]{1,0:T(8,128)(2,1)S(1)}, bf16[128,1280]{1,0:T(8,128)(2,1)S(1)}, u32[]{:S(2)}, u32[]{:S(2)}) collective-permute-start(bf16[128,1280]{1,0:T(8,128)(2,1)S(1)} %shard_map.78), channel_id=1, source_target_pairs={{0,16},{16,0},{1,17},{17,1},{2,18},{18,2},{3,19},{19,3},{4,20},{20... | collective-permute-start | bytes 983048 | tf_op jit(solution)/shard_map/ppermute | solution.py:350
  48.5 8.3 %collective-permute-done.20 = bf16[128,1280]{1,0:T(8,128)(2,1)S(1)} collective-permute-done((bf16[128,1280]{1,0:T(8,128)(2,1)S(1)}, bf16[128,1280]{1,0:T(8,128)(2,1)S(1)}, u32[]{:S(2)}, u32[]{:S(2)}) %collective-permute-start.20) | collective-permute-done | bytes 327712 | tf_op jit(solution)/shard_map/ppermute | solution.py:350
  56.8 0.7 %copy.9 = bf16[1,1,128,1280]{3,2,1,0:T(8,128)(2,1)} copy(bf16[1,1,128,1280]{3,2,1,0:T(8,128)(2,1)S(1)} %bitcast.25) | data formatting | bytes 655360
  (5 shorter events, 0.1 us)
Async XLA Ops:
  0.0 4.4 %collective-permute-start.2 = (bf16[160,1280]{1,0:T(8,128)(2,1)}, bf16[160,1280]{1,0:T(8,128)(2,1)S(1)}, u32[]{:S(2)}, u32[]{:S(2)}) collective-permute-start(bf16[160,1280]{1,0:T(8,128)(2,1)} %bitcast.19), channel_id=1, source_target_pairs={{0,1},{1,0},{2,3},{3,2},{4,5},{5,4},{6,7},{7,6},{8,9},{9,8},{10,11... | collective-permute-start | bytes 1228808 | tf_op jit(solution)/shard_map/ppermute | solution.py:264
  0.5 13.0 %collective-permute-start = (bf16[160,1280]{1,0:T(8,128)(2,1)}, bf16[160,1280]{1,0:T(8,128)(2,1)S(1)}, u32[]{:S(2)}, u32[]{:S(2)}) collective-permute-start(bf16[160,1280]{1,0:T(8,128)(2,1)} %bitcast.20), channel_id=1, source_target_pairs={{0,2},{1,3},{2,0},{3,1},{4,6},{5,7},{6,4},{7,5},{8,10},{9,11},{10,... | collective-permute-start | bytes 1228808 | tf_op jit(solution)/shard_map/ppermute | solution.py:264
  2.9 1.5 %copy-start.1 = (bf16[1,1,128,1280]{3,2,1,0:T(8,128)(2,1)S(1)}, bf16[1,1,128,1280]{3,2,1,0:T(8,128)(2,1)}, u32[]{:S(2)}) copy-start(bf16[1,1,128,1280]{3,2,1,0:T(8,128)(2,1)} %param.7) | copy-start | bytes 983044
  4.4 9.9 %copy-start = (bf16[1,1,128,1280]{3,2,1,0:T(8,128)(2,1)S(1)}, bf16[1,1,128,1280]{3,2,1,0:T(8,128)(2,1)}, u32[]{:S(2)}) copy-start(bf16[1,1,128,1280]{3,2,1,0:T(8,128)(2,1)} %param.8) | copy-start | bytes 983044
  4.4 9.9 %copy-start.2 = (bf16[1,160,1280]{2,1,0:T(8,128)(2,1)S(1)}, bf16[1,160,1280]{2,1,0:T(8,128)(2,1)}, u32[]{:S(2)}) copy-start(bf16[1,160,1280]{2,1,0:T(8,128)(2,1)} %param.13) | copy-start | bytes 1228804
  4.4 9.9 %collective-permute-start.3 = (bf16[128,1280]{1,0:T(8,128)(2,1)S(1)}, bf16[128,1280]{1,0:T(8,128)(2,1)S(1)}, u32[]{:S(2)}, u32[]{:S(2)}) collective-permute-start(bf16[128,1280]{1,0:T(8,128)(2,1)S(1)} %bitcast.15), channel_id=1, source_target_pairs={{0,4},{1,5},{2,6},{3,7},{4,0},{5,1},{6,2},{7,3},{8,12},{9,13},{10,... | collective-permute-start | bytes 983048 | tf_op jit(solution)/shard_map/ppermute | solution.py:252
  6.1 8.3 %collective-permute-start.4 = (bf16[128,1280]{1,0:T(8,128)(2,1)S(1)}, bf16[128,1280]{1,0:T(8,128)(2,1)S(1)}, u32[]{:S(2)}, u32[]{:S(2)}) collective-permute-start(bf16[128,1280]{1,0:T(8,128)(2,1)S(1)} %bitcast.16), channel_id=1, source_target_pairs={{0,1},{1,0},{2,3},{3,2},{4,8},{5,9},{6,10},{7,11},{8,4},{9,5},{10,... | collective-permute-start | bytes 983048 | tf_op jit(solution)/shard_map/ppermute | solution.py:252
  6.2 25.4 %collective-permute-start.14 = (bf16[240,1280]{1,0:T(8,128)(2,1)S(1)}, bf16[240,1280]{1,0:T(8,128)(2,1)S(1)}, u32[]{:S(2)}, u32[]{:S(2)}) collective-permute-start(bf16[240,1280]{1,0:T(8,128)(2,1)S(1)} %get-tuple-element.36), channel_id=1, source_target_pairs={{0,2},{1,3},{2,0},{3,1},{4,6},{5,7},{6,4},{7,5},{8,10},{9,11},{10,... | collective-permute-start | bytes 1843208 | tf_op jit(solution)/shard_map/ppermute | solution.py:264
  13.5 4.8 %collective-permute-start.1 = (bf16[160,1280]{1,0:T(8,128)(2,1)S(1)}, bf16[160,1280]{1,0:T(8,128)(2,1)S(1)}, u32[]{:S(2)}, u32[]{:S(2)}) collective-permute-start(bf16[160,1280]{1,0:T(8,128)(2,1)S(1)} %slice.33), channel_id=1, source_target_pairs={{0,1},{1,0},{2,3},{3,2},{4,5},{5,4},{6,7},{7,6},{8,9},{9,8},{10,11... | collective-permute-start | bytes 1228808 | tf_op jit(solution)/shard_map/ppermute | solution.py:264
  15.0 11.8 %collective-permute-start.5 = (bf16[1600,128]{1,0:T(8,128)(2,1)S(1)}, bf16[1600,128]{1,0:T(8,128)(2,1)S(1)}, u32[]{:S(2)}, u32[]{:S(2)}) collective-permute-start(bf16[1600,128]{1,0:T(8,128)(2,1)S(1)} %get-tuple-element.24.refs_2_.refs_5_), channel_id=1, source_target_pairs={{0,4},{1,5},{2,6},{3,7},{4,0},{5,1},{6,2},{7,3},{8,12},{9,13},{10,... | collective-permute-start | bytes 1228808 | tf_op jit(solution)/shard_map/ppermute | solution.py:252
  17.7 9.0 %collective-permute-start.6 = (bf16[1600,128]{1,0:T(8,128)(2,1)S(1)}, bf16[1600,128]{1,0:T(8,128)(2,1)S(1)}, u32[]{:S(2)}, u32[]{:S(2)}) collective-permute-start(bf16[1600,128]{1,0:T(8,128)(2,1)S(1)} %get-tuple-element.25.refs_1_), channel_id=1, source_target_pairs={{0,1},{1,0},{2,3},{3,2},{4,8},{5,9},{6,10},{7,11},{8,4},{9,5},{10,... | collective-permute-start | bytes 1228808 | tf_op jit(solution)/shard_map/ppermute | solution.py:252
  17.8 2.0 %collective-permute-start.7 = (bf16[80,1280]{1,0:T(8,128)(2,1)S(1)}, bf16[80,1280]{1,0:T(8,128)(2,1)S(1)}, u32[]{:S(2)}, u32[]{:S(2)}) collective-permute-start(bf16[80,1280]{1,0:T(8,128)(2,1)S(1)} %get-tuple-element.41), channel_id=1, source_target_pairs={{0,1},{1,0},{2,3},{3,2},{4,5},{5,4},{6,7},{7,6},{8,9},{9,8},{10,11... | collective-permute-start | bytes 614408 | tf_op jit(solution)/shard_map/ppermute | solution.py:264
  18.3 1.7 %collective-permute-start.8 = (bf16[80,1280]{1,0:T(8,128)(2,1)S(1)}, bf16[80,1280]{1,0:T(8,128)(2,1)S(1)}, u32[]{:S(2)}, u32[]{:S(2)}) collective-permute-start(bf16[80,1280]{1,0:T(8,128)(2,1)S(1)} %get-tuple-element.40), channel_id=1, source_target_pairs={{0,1},{1,0},{2,3},{3,2},{4,5},{5,4},{6,7},{7,6},{8,9},{9,8},{10,11... | collective-permute-start | bytes 614408 | tf_op jit(solution)/shard_map/ppermute | solution.py:264
  19.8 15.1 %collective-permute-start.13 = (bf16[320,1280]{1,0:T(8,128)(2,1)S(1)}, bf16[320,1280]{1,0:T(8,128)(2,1)S(1)}, u32[]{:S(2)}, u32[]{:S(2)}) collective-permute-start(bf16[320,1280]{1,0:T(8,128)(2,1)S(1)} %slice.38), channel_id=1, source_target_pairs={{0,1},{1,0},{2,3},{3,2},{4,5},{5,4},{6,7},{7,6},{8,9},{9,8},{10,11... | collective-permute-start | bytes 2457608 | tf_op jit(solution)/shard_map/ppermute | solution.py:264
  20.1 21.1 %collective-permute-start.18 = (bf16[240,1280]{1,0:T(8,128)(2,1)S(1)}, bf16[240,1280]{1,0:T(8,128)(2,1)S(1)}, u32[]{:S(2)}, u32[]{:S(2)}) collective-permute-start(bf16[240,1280]{1,0:T(8,128)(2,1)S(1)} %get-tuple-element.33), channel_id=1, source_target_pairs={{0,2},{1,3},{2,0},{3,1},{4,6},{5,7},{6,4},{7,5},{8,10},{9,11},{10,... | collective-permute-start | bytes 1843208 | tf_op jit(solution)/shard_map/ppermute | solution.py:264
  27.2 10.0 %copy-start.3 = (s32[4,4]{1,0:T(4,128)S(1)}, s32[4,4]{1,0:T(4,128)}, u32[]{:S(2)}) copy-start(s32[4,4]{1,0:T(4,128)} %ids_ref.5) | copy-start | bytes 196
  27.2 4.5 %collective-permute-start.10 = (bf16[640,128]{1,0:T(8,128)(2,1)S(1)}, bf16[640,128]{1,0:T(8,128)(2,1)S(1)}, u32[]{:S(2)}, u32[]{:S(2)}) collective-permute-start(bf16[640,128]{1,0:T(8,128)(2,1)S(1)} %get-tuple-element.29), channel_id=1, source_target_pairs={{0,1},{1,0},{2,3},{3,2},{4,8},{5,9},{6,10},{7,11},{8,4},{9,5},{10,... | collective-permute-start | bytes 491528 | tf_op jit(solution)/shard_map/ppermute | solution.py:252
  27.3 7.6 %collective-permute-start.9 = (bf16[640,128]{1,0:T(8,128)(2,1)S(1)}, bf16[640,128]{1,0:T(8,128)(2,1)S(1)}, u32[]{:S(2)}, u32[]{:S(2)}) collective-permute-start(bf16[640,128]{1,0:T(8,128)(2,1)S(1)} %get-tuple-element.28.refs_0_), channel_id=1, source_target_pairs={{0,4},{1,5},{2,6},{3,7},{4,0},{5,1},{6,2},{7,3},{8,12},{9,13},{10,... | collective-permute-start | bytes 491528 | tf_op jit(solution)/shard_map/ppermute | solution.py:252
  31.6 5.4 %collective-permute-start.15 = (bf16[80,1280]{1,0:T(8,128)(2,1)S(1)}, bf16[80,1280]{1,0:T(8,128)(2,1)S(1)}, u32[]{:S(2)}, u32[]{:S(2)}) collective-permute-start(bf16[80,1280]{1,0:T(8,128)(2,1)S(1)} %get-tuple-element.39), channel_id=1, source_target_pairs={{0,1},{1,0},{2,3},{3,2},{4,5},{5,4},{6,7},{7,6},{8,9},{9,8},{10,11... | collective-permute-start | bytes 614408 | tf_op jit(solution)/shard_map/ppermute | solution.py:264
  31.7 9.5 %collective-permute-start.16 = (bf16[80,1280]{1,0:T(8,128)(2,1)S(1)}, bf16[80,1280]{1,0:T(8,128)(2,1)S(1)}, u32[]{:S(2)}, u32[]{:S(2)}) collective-permute-start(bf16[80,1280]{1,0:T(8,128)(2,1)S(1)} %get-tuple-element.38), channel_id=1, source_target_pairs={{0,1},{1,0},{2,3},{3,2},{4,5},{5,4},{6,7},{7,6},{8,9},{9,8},{10,11... | collective-permute-start | bytes 614408 | tf_op jit(solution)/shard_map/ppermute | solution.py:264
  34.9 6.3 %collective-permute-start.17 = (bf16[80,1280]{1,0:T(8,128)(2,1)S(1)}, bf16[80,1280]{1,0:T(8,128)(2,1)S(1)}, u32[]{:S(2)}, u32[]{:S(2)}) collective-permute-start(bf16[80,1280]{1,0:T(8,128)(2,1)S(1)} %get-tuple-element.37), channel_id=1, source_target_pairs={{0,1},{1,0},{2,3},{3,2},{4,5},{5,4},{6,7},{7,6},{8,9},{9,8},{10,11... | collective-permute-start | bytes 614408 | tf_op jit(solution)/shard_map/ppermute | solution.py:264
  34.9 6.3 %collective-permute-start.11 = (bf16[320,128]{1,0:T(8,128)(2,1)S(1)}, bf16[320,128]{1,0:T(8,128)(2,1)S(1)}, u32[]{:S(2)}, u32[]{:S(2)}) collective-permute-start(bf16[320,128]{1,0:T(8,128)(2,1)S(1)} %slice.44), channel_id=1, source_target_pairs={{0,4},{1,5},{2,6},{3,7},{4,0},{5,1},{6,2},{7,3},{8,12},{9,13},{10,... | collective-permute-start | bytes 245768 | tf_op jit(solution)/shard_map/ppermute | solution.py:252
  37.0 4.2 %collective-permute-start.12 = (bf16[320,128]{1,0:T(8,128)(2,1)S(1)}, bf16[320,128]{1,0:T(8,128)(2,1)S(1)}, u32[]{:S(2)}, u32[]{:S(2)}) collective-permute-start(bf16[320,128]{1,0:T(8,128)(2,1)S(1)} %slice.45), channel_id=1, source_target_pairs={{0,1},{1,0},{2,3},{3,2},{4,8},{5,9},{6,10},{7,11},{8,4},{9,5},{10,... | collective-permute-start | bytes 245768 | tf_op jit(solution)/shard_map/ppermute | solution.py:252
  41.2 2.9 %collective-permute-start.19 = (bf16[240,1280]{1,0:T(8,128)(2,1)S(1)}, bf16[240,1280]{1,0:T(8,128)(2,1)S(1)}, u32[]{:S(2)}, u32[]{:S(2)}) collective-permute-start(bf16[240,1280]{1,0:T(8,128)(2,1)S(1)} %collective-permute-done.18.refs_7_), channel_id=1, source_target_pairs={{0,1},{1,0},{2,3},{3,2},{4,5},{5,4},{6,7},{7,6},{8,9},{9,8},{10,11... | collective-permute-start | bytes 1843208 | tf_op jit(solution)/shard_map/ppermute | solution.py:264
  46.9 9.9 %collective-permute-start.20 = (bf16[128,1280]{1,0:T(8,128)(2,1)S(1)}, bf16[128,1280]{1,0:T(8,128)(2,1)S(1)}, u32[]{:S(2)}, u32[]{:S(2)}) collective-permute-start(bf16[128,1280]{1,0:T(8,128)(2,1)S(1)} %shard_map.78), channel_id=1, source_target_pairs={{0,16},{16,0},{1,17},{17,1},{2,18},{18,2},{3,19},{19,3},{4,20},{20... | collective-permute-start | bytes 983048 | tf_op jit(solution)/shard_map/ppermute | solution.py:350
